TPU v7x, 256 devices: a whole 4x4x8 slice. The times are simulated.
256 devices in a mesh: row: 32 (over x, z_hi, core), col: 8 (over z_lo, y).
Axes of the slice: x: 4, y: 4, z: 8 (z_hi: 4, z_lo: 2; z = z_hi * 2 + z_lo), core: 2. Of those that a mesh axis runs over, the one named last changes fastest.
Arguments:
- group: bfloat16 [160, 1024, 128], P('row', 'col'), may hold values from -6 to 6
- pair: bfloat16 [1024, 1024, 128], P('col', 'row'), may hold values from -6 to 6
- mask: int32 [1024], replicated, may hold values from 0 to 1, as said below
- ln_gain: float32 [128], replicated, may hold values from 0.25 to 1.75
- ln_shift: float32 [128], replicated, may hold values from -3 to 3
- w_query: bfloat16 [128, 128], replicated, may hold values from -0.5 to 0.5
- w_key: bfloat16 [128, 128], replicated, may hold values from -0.25 to 0.25
- w_value: bfloat16 [128, 128], replicated, may hold values from -0.5 to 0.5
- w_gate: bfloat16 [128, 128], replicated, may hold values from -0.5 to 0.5
- gate_bias: float32 [128], replicated, may hold values from -4 to 4
- w_bias: bfloat16 [128, 4], replicated, may hold values from -0.1875 to 0.1875
- w_out: bfloat16 [128, 128], replicated, may hold values from -0.5 to 0.5
- cotangent: bfloat16 [160, 1024, 128], P('row', 'col'), may hold values from -6 to 6
Outputs:
- grad_group: bfloat16 [160, 1024, 128], P('row', 'col')
- grad_pair: bfloat16 [1024, 1024, 128], P('col', 'row')
Inputs may be any that keep to these rules, and one draw needn't show every extreme that they name: `mask`: the residues form aligned blocks of 8 positions, one padded chain segment each; in every block the real residues (1) come first and the padding (0) after them, and every block has 4 or more real residues.
All inputs are finite; a program needn't handle non-finite values.
Results may differ from a plain program's by a relative error of at most 0.03.
Values may be sent and summed in bfloat16 or wider, within the bound.
No kernel may reach another device: no remote copies, remote signals or barrier semaphores. Data moves between devices by JAX's collectives and lax.ppermute only.
A program may use at most 64 MiB of HBM per device.

v0:
```python
import jax
import jax.numpy as jnp
from jax import lax
from jax.sharding import PartitionSpec as P

HEADS = 4
HEAD_DIM = 32


epsilon = 1e-05
highest = lax.Precision.HIGHEST


def normalize(values_in):
    widened = values_in.astype(jnp.float32)
    average = jnp.mean(widened, axis=-1, keepdims=True)
    centered = widened - average
    variance = jnp.mean(centered * centered, axis=-1, keepdims=True)
    reciprocal = lax.rsqrt(variance + epsilon)
    return (centered * reciprocal, reciprocal)


def norm_backward(upstream, normalized, reciprocal, ln_gain):
    scaled = upstream * ln_gain
    first = jnp.mean(scaled, axis=-1, keepdims=True)
    second = jnp.mean(scaled * normalized, axis=-1, keepdims=True)
    return reciprocal * (scaled - first - normalized * second)


def wide_dot(left, right):
    return jnp.dot(left, right, precision=highest, preferred_element_type=jnp.float32)


def attention_row(
    query_row, key_row, value_row, gating_row, upstream_row, bias, live_keys, score_scale
):
    scores = (
        jnp.einsum("jhc,khc->hjk", query_row, key_row, preferred_element_type=jnp.float32) + bias
    )
    raised = jnp.where(live_keys, jnp.exp(scores), 0.0)
    weights = raised / jnp.sum(raised, axis=-1, keepdims=True)
    weights_low = weights.astype(jnp.bfloat16)
    attended = jnp.einsum(
        "hjk,khc->jhc", weights_low, value_row, preferred_element_type=jnp.float32
    )
    grad_attended = (upstream_row * gating_row).astype(jnp.bfloat16)
    grad_gate_in = upstream_row * attended * gating_row * (1.0 - gating_row)
    row_delta = jnp.sum(grad_attended * attended, axis=-1)
    grad_weights = jnp.einsum(
        "jhc,khc->hjk", grad_attended, value_row, preferred_element_type=jnp.float32
    )
    grad_scores = weights * (grad_weights - row_delta.T[:, :, None])
    scores_low = grad_scores.astype(jnp.bfloat16)
    grad_queries = (
        jnp.einsum("hjk,khc->jhc", scores_low, key_row, preferred_element_type=jnp.float32)
        * score_scale
    )
    grad_keys = jnp.einsum(
        "hjk,jhc->khc", scores_low, query_row, preferred_element_type=jnp.float32
    )
    grad_values = jnp.einsum(
        "hjk,jhc->khc", weights_low, grad_attended, preferred_element_type=jnp.float32
    )
    return (grad_queries, grad_keys, grad_values, grad_gate_in, grad_scores)


def per_device(
    group,
    pair,
    mask,
    ln_gain,
    ln_shift,
    w_query,
    w_key,
    w_value,
    w_gate,
    gate_bias,
    w_bias,
    w_out,
    cotangent,
):
    row_count, col_count, channels = group.shape
    key_count = mask.shape[0]
    head_width = HEADS * HEAD_DIM
    score_scale = HEAD_DIM ** (-0.5)
    shaped = (row_count, col_count, HEADS, HEAD_DIM)
    normalized, reciprocal = normalize(group)
    normed = (normalized * ln_gain + ln_shift).astype(jnp.bfloat16)
    flattened = normed.reshape(row_count * col_count, channels)
    queries = (
        (jnp.dot(flattened, w_query, preferred_element_type=jnp.float32) * score_scale)
        .astype(jnp.bfloat16)
        .reshape(shaped)
    )
    gating = jax.nn.sigmoid(
        jnp.dot(flattened, w_gate, preferred_element_type=jnp.float32) + gate_bias
    ).reshape(shaped)
    grad_gated = jnp.dot(
        cotangent.reshape(row_count * col_count, channels),
        w_out.T,
        preferred_element_type=jnp.float32,
    ).reshape(shaped)
    pair_normalized, pair_reciprocal = normalize(pair)
    pair_normed = (pair_normalized * ln_gain + ln_shift).astype(jnp.bfloat16)
    local_bias = jnp.dot(
        pair_normed.reshape(-1, channels), w_bias, preferred_element_type=jnp.float32
    ).astype(jnp.bfloat16)
    local_bias = jnp.transpose(local_bias.reshape(pair.shape[0], pair.shape[1], HEADS), (2, 0, 1))
    bias = lax.all_gather(local_bias, "row", axis=2, tiled=True)
    key_local = (
        jnp.dot(flattened, w_key, preferred_element_type=jnp.float32)
        .astype(jnp.bfloat16)
        .reshape(row_count, col_count, head_width)
    )
    value_local = (
        jnp.dot(flattened, w_value, preferred_element_type=jnp.float32)
        .astype(jnp.bfloat16)
        .reshape(row_count, col_count, head_width)
    )
    keys, values = (
        lax.all_gather(key_local, "col", axis=1, tiled=True),
        lax.all_gather(value_local, "col", axis=1, tiled=True),
    )
    keys = keys.reshape(row_count, key_count, HEADS, HEAD_DIM)
    values = values.reshape(row_count, key_count, HEADS, HEAD_DIM)
    live_keys = mask > 0

    def scan_row(partial_value, inputs):
        grad_q, grad_k, grad_v, grad_g, grad_s = attention_row(
            *inputs, bias, live_keys, score_scale
        )
        return (partial_value + grad_s, (grad_q, grad_k, grad_v, grad_g))

    partial_value, gradients = lax.scan(
        scan_row,
        jnp.zeros((HEADS, col_count, key_count), jnp.float32),
        (queries, keys, values, gating, grad_gated),
    )
    grad_queries = gradients[0].reshape(-1, head_width)
    grad_keys = gradients[1].reshape(row_count, key_count, head_width)
    grad_values = gradients[2].reshape(row_count, key_count, head_width)
    grad_gate_in = gradients[3].reshape(-1, head_width)
    key_weight = w_key.astype(jnp.float32).T
    value_weight = w_value.astype(jnp.float32).T
    summed_keys, summed_values = (
        lax.psum_scatter(
            grad_keys.astype(jnp.bfloat16), "col", scatter_dimension=1, tiled=True
        ).astype(jnp.float32),
        lax.psum_scatter(
            grad_values.astype(jnp.bfloat16), "col", scatter_dimension=1, tiled=True
        ).astype(jnp.float32),
    )
    key_term = wide_dot(summed_keys.reshape(-1, head_width), key_weight) + wide_dot(
        summed_values.reshape(-1, head_width), value_weight
    )
    grad_normed = (
        wide_dot(grad_queries, w_query.astype(jnp.float32).T)
        + wide_dot(grad_gate_in, w_gate.astype(jnp.float32).T)
        + key_term
    )
    grad_group = norm_backward(
        grad_normed.reshape(row_count, col_count, channels), normalized, reciprocal, ln_gain
    ).astype(jnp.bfloat16)
    grad_bias = lax.psum_scatter(
        partial_value.astype(jnp.bfloat16), "row", scatter_dimension=2, tiled=True
    ).astype(jnp.float32)
    upstream = jnp.einsum("hjk,ch->jkc", grad_bias, w_bias.astype(jnp.float32), precision=highest)
    grad_pair = norm_backward(upstream, pair_normalized, pair_reciprocal, ln_gain).astype(
        jnp.bfloat16
    )
    return (grad_group, grad_pair)


def solution(mesh):
    placed = (
        P("row", "col", None),
        P("col", "row", None),
        P(),
        P(),
        P(),
        P(),
        P(),
        P(),
        P(),
        P(),
        P(),
        P(),
        P("row", "col", None),
    )
    return jax.shard_map(
        per_device,
        mesh=mesh,
        in_specs=placed,
        out_specs=(P("row", "col", None), P("col", "row", None)),
        check_vma=False,
    )
```

profile of v0, /device:TPU:32, one launch (start us, length us, event | category | flops | bytes accessed | tf_op | source)
XLA Modules:
  0.0 628.6 jit_solution(1694618224337512096)
XLA Ops:
  19.0 47.1 %all-gather.6.cloned.1.call-done = bf16[4,128,1024]{1,0,2:T(4,128)(2,1)} async-done(((bf16[4,128,32]{1,0,2:T(4,128)(2,1)}), bf16[4,128,1024]{1,0,2:T(4,128)(2,1)}) %all-gather.6.cloned.1.call-update) | async-done | bytes 1048592 | tf_op jit(solution)/shard_map/all_gather | solution.py:109
  68.5 39.6 %all-gather.8.cloned.1.call-done = bf16[5,1024,128]{2,1,0:T(8,128)(2,1)} async-done(((bf16[5,128,128]{2,1,0:T(8,128)(2,1)}), bf16[5,1024,128]{2,1,0:T(8,128)(2,1)}) %all-gather.8.cloned.1.call-update) | async-done | bytes 1310736 | tf_op jit(solution)/shard_map/all_gather | solution.py:122
  110.6 40.9 %all-gather.4.cloned.1.call-done = bf16[5,1024,128]{2,1,0:T(8,128)(2,1)} async-done(((bf16[5,128,128]{2,1,0:T(8,128)(2,1)}), bf16[5,1024,128]{2,1,0:T(8,128)(2,1)}) %all-gather.4.cloned.1.call-update) | async-done | bytes 1310736 | tf_op jit(solution)/shard_map/all_gather | solution.py:121
  154.0 89.0 %while.19 = (s32[]{:T(128)}, f32[4,128,1024]{2,1,0:T(8,128)}, f32[5,128,4,32]{1,0,3,2:T(8,128)}, bf16[5,1024,4,32]{1,3,2,0:T(8,128)(2,1)}, bf16[5,1024,4,32]{1,3...) while((s32[]{:T(128)}, f32[4,128,1024]{2,1,0:T(8,128)}, ...), condition=%wide.region_7.8_spmd.clone, body=%wide.region_4.7_spmd.clone.sunk | while | flops 207258624 | bytes 19703460 | solution.py:134
  158.7 2.8 select_add_fusion.2
  164.7 2.8 dynamic_update_slice.26
  168.4 2.8 dynamic_update_slice.27
  175.9 3.6 select_add_fusion.2
  182.6 2.8 dynamic_update_slice.26
  186.4 2.8 dynamic_update_slice.27
  193.9 3.6 select_add_fusion.2
  200.6 2.8 dynamic_update_slice.26
  204.4 2.8 dynamic_update_slice.27
  211.8 3.6 select_add_fusion.2
  218.5 2.8 dynamic_update_slice.26
  222.3 2.8 dynamic_update_slice.27
  229.8 3.6 select_add_fusion.2
  236.5 2.8 dynamic_update_slice.26
  240.2 2.8 dynamic_update_slice.27
  245.9 3.2 copy.67
  250.7 3.2 copy.69
  258.5 272.8 %all-reduce.3.cloned.1.call-done = bf16[4,128,1024]{1,0,2:T(4,128)(2,1)} async-done(((bf16[4,128,1024]{1,0,2:T(4,128)(2,1)}), bf16[4,128,1024]{1,0,2:T(4,128)(2,1)}) %all-reduce.3.cloned.1.call-update) | async-done | bytes 1048592
  535.2 39.8 %reduce-scatter.7.cloned.1.call-done = bf16[128,640]{1,0:T(8,128)(2,1)} async-done(((bf16[1024,640]{1,0:T(8,128)(2,1)}), bf16[128,640]{1,0:T(8,128)(2,1)}) %reduce-scatter.7.cloned.1.call-update) | async-done | bytes 163856
  576.4 42.4 %reduce-scatter.9.cloned.1.call-done = bf16[128,640]{1,0:T(8,128)(2,1)} async-done(((bf16[1024,640]{1,0:T(8,128)(2,1)}), bf16[128,640]{1,0:T(8,128)(2,1)}) %reduce-scatter.9.cloned.1.call-update) | async-done | bytes 163856
  (134 shorter events, 79.3 us)
Async XLA Ops:
  7.2 10.9 %copy-start = (bf16[5,128,128]{2,1,0:T(8,128)(2,1)S(1)}, bf16[5,128,128]{2,1,0:T(8,128)(2,1)}, u32[]{:S(2)}) copy-start(bf16[5,128,128]{2,1,0:T(8,128)(2,1)} %param.27) | copy-start | bytes 491524
  7.2 2.6 copy-start.12
  7.2 2.6 copy-start.14
  7.2 58.9 %all-gather.6.cloned.1.call-start = ((), (), s32[]{:S(2)}) async-start(), calls=%async_computation.3 | async-start | bytes 1081344 | tf_op jit(solution)/shard_map/all_gather | solution.py:109
  9.8 1.7 copy-start.15
  10.4 2.4 copy-start.1
  10.4 4.0 copy-start.4
  11.4 2.1 copy-start.5
  11.5 4.0 copy-start.10
  11.5 4.0 copy-start.17
  12.8 95.4 %all-gather.8.cloned.1.call-start = ((), (), s32[]{:S(2)}) async-start(), calls=%async_computation.4 | async-start | bytes 1474560 | tf_op jit(solution)/shard_map/all_gather | solution.py:122
  13.5 3.3 copy-start.7
  14.4 137.1 %all-gather.4.cloned.1.call-start = ((), (), s32[]{:S(2)}) async-start(), calls=%async_computation.2 | async-start | bytes 1474560 | tf_op jit(solution)/shard_map/all_gather | solution.py:121
  15.4 515.9 %all-reduce.3.cloned.1.call-start = ((), (), s32[]{:S(2)}) async-start(), calls=%async_computation.7 | async-start | bytes 2097152
  15.5 2.6 copy-start.13
  15.5 2.6 copy-start.9
  245.8 329.2 %reduce-scatter.7.cloned.1.call-start = ((), (), s32[]{:S(2)}) async-start(), calls=%async_computation.5 | async-start | bytes 1474560
  250.4 368.3 %reduce-scatter.9.cloned.1.call-start = ((), (), s32[]{:S(2)}) async-start(), calls=%async_computation.6 | async-start | bytes 1474560
  253.9 2.6 copy-start.8
  253.9 4.1 copy-start.11
  255.2 2.8 copy-start.3
  255.2 276.0 %copy-start.16 = (bf16[128,4]{0,1:T(4,128)(2,1)S(1)}, bf16[128,4]{0,1:T(4,128)(2,1)}, u32[]{:S(2)}) copy-start(bf16[128,4]{0,1:T(4,128)(2,1)} %param.25) | copy-start | bytes 3076
  533.5 86.4 %copy-start.6 = (bf16[128,128]{1,0:T(8,128)(2,1)S(1)}, bf16[128,128]{1,0:T(8,128)(2,1)}, u32[]{:S(2)}) copy-start(bf16[128,128]{1,0:T(8,128)(2,1)} %param.22) | copy-start | bytes 98308
  535.2 85.0 %copy-start.2 = (bf16[5,128,128]{2,1,0:T(8,128)(2,1)S(1)}, bf16[5,128,128]{2,1,0:T(8,128)(2,1)}, u32[]{:S(2)}) copy-start(bf16[5,128,128]{2,1,0:T(8,128)(2,1)} %param.15) | copy-start | bytes 491524
  (1 other events, 1.4 us)
Sparse Core Ops, SparseCore 0:
  12.9 53.2 all-gather.5
  67.9 40.1 all-gather.7
  109.9 41.5 all-gather.3
  246.0 285.2 all-reduce.2
  533.8 41.1 reduce-scatter.6
  577.6 41.1 reduce-scatter.8
where the time goes:
time: 632 us; the launch traced here: 629 us
  waiting for transfers between devices  483 us (76%)
  local copies, waits for them, and re-layouts  63.1 us (10%)
  matrix products  62.8 us (10%)
  between operations  15.3 us (2%)
    unnamed x9, waiting for transfers between devices  355 us
    all_gather x1, waiting for transfers between devices, per_device(): bias = lax.all_gather(local_bias, 'row', axis=2, tiled=True)  47.1 us
    all_gather x1, waiting for transfers between devices, per_device(): lax.all_gather(key_local, 'col', axis=1, tiled=True)  40.9 us
    all_gather x1, waiting for transfers between devices, per_device(): lax.all_gather(value_local, 'col', axis=1, tiled=True)  39.6 us
    dynamic_update_slice x10, local copies, waits for them, and re-layouts, per_device(): lax.scan(scan_row, jnp.zeros((HEADS, col_count, key_count), jnp.float32),...  27.9 us
    unnamed x49, local copies, waits for them, and re-layouts  18.6 us
    dot_general x5, matrix products, attention_row(): jnp.einsum('jhc,khc->hjk', grad_attended, value_row, preferred_element_ty...  17.1 us
  transfers between devices with their start and end apart: 6, of which 6 were waited for; matrix products, arithmetic and copies ran while one was open for 4% of the time, Pallas kernels for 0%

commit v1 on v0

v1 whole, which is shorter than its diff:
```python
import jax
import jax.numpy as jnp
from jax import lax
from jax.experimental import pallas as pl
from jax.experimental.pallas import tpu as pltpu
from jax.sharding import PartitionSpec as P

HEADS = 4
HEAD_DIM = 32
BLOCK = 128
EPS = 1e-05
SCALE = HEAD_DIM ** (-0.5)
VMEM_LIMIT = 48 * 1024 * 1024

bf16, f32 = jnp.bfloat16, jnp.float32
NT = (((1,), (1,)), ((), ()))
TN = (((0,), (0,)), ((), ()))


def split_high_low(value):
    high = value.astype(bf16)
    return high, (value - high.astype(f32)).astype(bf16)


def bias_kernel(pair_ref, gain_ref, shift_ref, weight_ref, out_ref, normed, heads):
    gain, shift = gain_ref[...], shift_ref[...]
    weight_t = jnp.concatenate(
        [weight_ref[...].astype(f32), jnp.zeros((BLOCK, BLOCK - HEADS), f32)], axis=1
    ).T[:16].astype(bf16)

    def rows(step, carry):
        x = pair_ref[pl.ds(step * 16, 16)].astype(f32).reshape(512, BLOCK)
        centered = x - jnp.mean(x, axis=-1, keepdims=True)
        reciprocal = lax.rsqrt(jnp.mean(centered * centered, axis=-1, keepdims=True) + EPS)
        low = (centered * reciprocal * gain + shift).astype(bf16).astype(f32)
        normed[pl.ds(pl.multiple_of(step * 512, 512), 512), :] = low
        return carry

    lax.fori_loop(0, 8, rows, 0)

    for k in range(32):
        block = normed[pl.ds(k, BLOCK, stride=32), :].astype(bf16)
        product = lax.dot_general(weight_t, block, NT, preferred_element_type=f32)
        for h in range(HEADS):
            heads[h, k : k + 1, :] = product[h : h + 1]
    for zh in range(4):
        out_ref[zh] = heads[...].astype(bf16)


def bias_call(pair, gain, shift, weight):
    return pl.pallas_call(
        bias_kernel,
        out_shape=jax.ShapeDtypeStruct((4, HEADS, 32, BLOCK), bf16),
        scratch_shapes=[pltpu.VMEM((4096, BLOCK), f32), pltpu.VMEM((HEADS, 32, BLOCK), f32)],
        compiler_params=pltpu.CompilerParams(vmem_limit_bytes=VMEM_LIMIT),
        cost_estimate=pl.CostEstimate(
            flops=20_000_000, bytes_accessed=1_200_000, transcendentals=4096
        ),
        name="pair_bias",
    )(pair, gain, shift, weight)


def project_kernel(
    group_ref, cot_ref, gain_ref, shift_ref, wq_ref, wk_ref, wv_ref, wg_ref, gb_ref, wo_ref,
    key_value, query_up, coef,
):
    gain, shift = gain_ref[...], shift_ref[...]
    turned = [w[...].astype(f32).T.astype(bf16) for w in (wq_ref, wk_ref, wv_ref, wg_ref)]
    gate_bias = jnp.broadcast_to(gb_ref[...], (BLOCK, BLOCK)).T
    rows = group_ref.shape[0]
    for i in range(rows):
        x = group_ref[i].astype(f32)
        centered = x - jnp.mean(x, axis=-1, keepdims=True)
        reciprocal = lax.rsqrt(jnp.mean(centered * centered, axis=-1, keepdims=True) + EPS)
        normed = (centered * reciprocal * gain + shift).astype(bf16)
        dots = [lax.dot_general(w, normed, NT, preferred_element_type=f32) for w in turned]
        gating = jax.nn.sigmoid(dots[3] + gate_bias)
        gated = lax.dot_general(wo_ref[...], cot_ref[i], NT, preferred_element_type=f32)
        upstream = gated * gating
        coef[i] = upstream * (1.0 - gating)
        for n, value in enumerate((dots[1], dots[2], dots[0] * SCALE, upstream)):
            value = value.astype(bf16).reshape(HEADS, HEAD_DIM, BLOCK)
            for h in range(HEADS):
                if n < 2:
                    key_value[0, h, n, i] = value[h]
                    key_value[1, h, n, i] = value[h]
                else:
                    query_up[h, n - 2, i] = value[h]


def project_call(group, cotangent, gain, shift, wq, wk, wv, wg, gb, wo):
    rows = group.shape[0]
    return pl.pallas_call(
        project_kernel,
        out_shape=(
            jax.ShapeDtypeStruct((2, HEADS, 2, rows, HEAD_DIM, BLOCK), bf16),
            jax.ShapeDtypeStruct((HEADS, 2, rows, HEAD_DIM, BLOCK), bf16),
            jax.ShapeDtypeStruct((rows, BLOCK, BLOCK), f32),
        ),
        compiler_params=pltpu.CompilerParams(vmem_limit_bytes=VMEM_LIMIT),
        cost_estimate=pl.CostEstimate(
            flops=110_000_000, bytes_accessed=2_000_000, transcendentals=100_000
        ),
        name="project",
    )(group, cotangent, gain, shift, wq, wk, wv, wg, gb, wo)


def attention_kernel(
    mask_ref, bias_own, bias_other, key_value, query_up, out_kv, out_q, keep, send,
    bias, grad, key_t, value_t, key_s, value_s,
):
    core = lax.axis_index("core")
    keys, queries = bias.shape
    rows = query_up.shape[2]

    for source, c in ((bias_own, core), (bias_other, 1 - core)):
        for n in range(16):
            at = pl.ds(pl.multiple_of(n * 64 + c * 32, 32), 32)
            for y in range(4):
                bias[at, y * BLOCK : (y + 1) * BLOCK] = source[n // 4, n % 4, y].astype(f32)
    for blk in range(keys // BLOCK):
        at = slice(blk * BLOCK, (blk + 1) * BLOCK)
        live = jnp.broadcast_to(mask_ref[blk : blk + 1, :].astype(f32), (BLOCK, BLOCK)).T
        for y in range(4):
            lanes = slice(y * BLOCK, (y + 1) * BLOCK)
            bias[at, lanes] = jnp.where(live > 0.0, bias[at, lanes], -jnp.inf)
        for i in range(rows):
            k, v = key_value[blk // 4, blk % 4, 0, i], key_value[blk // 4, blk % 4, 1, i]
            key_t[i, :, at] = k
            value_t[i, :, at] = v
            key_s[i, at, :] = k.astype(f32).T.astype(bf16)
            value_s[i, at, :] = v.astype(f32).T.astype(bf16)
    grad[...] = jnp.zeros_like(grad)

    width = 256

    def row(i, carry):
        grad_key = jnp.zeros((keys, HEAD_DIM), f32)
        grad_value = jnp.zeros((keys, HEAD_DIM), f32)
        for part in range(queries // width):
            lanes = slice(part * width, (part + 1) * width)
            blocks = range(part * (width // BLOCK), (part + 1) * (width // BLOCK))
            q = jnp.concatenate([query_up[n, 0, i] for n in blocks], axis=1)
            g = jnp.concatenate([query_up[n, 1, i] for n in blocks], axis=1)
            scores = jnp.dot(key_s[i], q, preferred_element_type=f32) + bias[:, lanes]
            raised = jnp.exp(scores)
            weights = raised * (1.0 / jnp.sum(raised, axis=0, keepdims=True))
            low = weights.astype(bf16)
            attended = jnp.dot(value_t[i], low, preferred_element_type=f32)
            delta = jnp.sum(g.astype(f32) * attended, axis=0, keepdims=True)
            grad_weights = jnp.dot(value_s[i], g, preferred_element_type=f32)
            grad_scores = weights * (grad_weights - delta)
            grad[:, lanes] += grad_scores
            scores_low = grad_scores.astype(bf16)
            grad_query = jnp.dot(key_t[i], scores_low, preferred_element_type=f32) * SCALE
            grad_key += lax.dot_general(scores_low, q, NT, preferred_element_type=f32)
            grad_value += lax.dot_general(low, g, NT, preferred_element_type=f32)
            for n, block in enumerate(blocks):
                at = slice(n * BLOCK, (n + 1) * BLOCK)
                out_q[block, 0, i] = grad_query[:, at].astype(bf16)
                out_q[block, 1, i] = attended[:, at].astype(bf16)
        both = jnp.concatenate([grad_key, grad_value], axis=1).T.astype(bf16)
        for blk in range(keys // BLOCK):
            at = slice(blk * BLOCK, (blk + 1) * BLOCK)
            out_kv[blk // 4, blk % 4, 0, i] = both[:HEAD_DIM, at]
            out_kv[blk // 4, blk % 4, 1, i] = both[HEAD_DIM:, at]
        return carry

    lax.fori_loop(0, rows, row, 0)

    for out, c in ((keep, core), (send, 1 - core)):
        for n in range(16):
            at = pl.ds(pl.multiple_of(n * 64 + c * 32, 32), 32)
            for y in range(4):
                piece = grad[at, y * BLOCK : (y + 1) * BLOCK]
                out[n // 4, n % 4, y] = piece.astype(out.dtype)


def attention_call(mask, bias_own, bias_other, key_value, query_up):
    rows = query_up.shape[2]
    keys = mask.shape[0] * mask.shape[1]
    queries = keys // 2
    return pl.pallas_call(
        attention_kernel,
        out_shape=(
            jax.ShapeDtypeStruct(key_value.shape, bf16),
            jax.ShapeDtypeStruct(query_up.shape, bf16),
            jax.ShapeDtypeStruct(bias_own.shape, f32),
            jax.ShapeDtypeStruct(bias_own.shape, bf16),
        ),
        scratch_shapes=[
            pltpu.VMEM((keys, queries), f32),
            pltpu.VMEM((keys, queries), f32),
            pltpu.VMEM((rows, HEAD_DIM, keys), bf16),
            pltpu.VMEM((rows, HEAD_DIM, keys), bf16),
            pltpu.VMEM((rows, keys, HEAD_DIM), bf16),
            pltpu.VMEM((rows, keys, HEAD_DIM), bf16),
        ],
        compiler_params=pltpu.CompilerParams(vmem_limit_bytes=VMEM_LIMIT),
        cost_estimate=pl.CostEstimate(
            flops=8_000_000_000, bytes_accessed=6_000_000, transcendentals=2_700_000
        ),
        name="attention",
    )(mask, bias_own, bias_other, key_value, query_up)


def add_two_kernel(keep, came, out):
    out[...] = (keep[...] + came[...].astype(f32)).astype(bf16)


def add_four_kernel(came, out):
    wide = [came[n].astype(f32) for n in range(4)]
    out[...] = ((wide[0] + wide[1]) + (wide[2] + wide[3])).astype(bf16)


def add_call(kernel, shape, *values):
    return pl.pallas_call(
        kernel,
        out_shape=jax.ShapeDtypeStruct(shape, bf16),
        compiler_params=pltpu.CompilerParams(vmem_limit_bytes=VMEM_LIMIT),
        name="add_bias_gradient",
    )(*values)


def group_kernel(
    group_ref, gain_ref, wq_ref, wk_ref, wv_ref, wg_ref, coef, grad_kv, grad_q, out_ref
):
    gain = gain_ref[...]
    wq, wk, wv, wg = wq_ref[...], wk_ref[...], wv_ref[...], wg_ref[...]
    weights = jnp.concatenate([wq, wk, wk, wv, wv, wg, wg], axis=1)
    for i in range(group_ref.shape[0]):
        parts = [[] for _ in range(7)]
        for h in range(HEADS):
            gate = coef[i, h * HEAD_DIM : (h + 1) * HEAD_DIM, :] * grad_q[h, 1, i].astype(f32)
            high, low = split_high_low(gate)
            pieces = (
                grad_q[h, 0, i],
                grad_kv[0, h, 0, i], grad_kv[1, h, 0, i],
                grad_kv[0, h, 1, i], grad_kv[1, h, 1, i],
                high, low,
            )
            for part, piece in zip(parts, pieces):
                part.append(piece)
        stacked = jnp.concatenate(sum(parts, []), axis=0)
        upstream = jnp.dot(weights, stacked, preferred_element_type=f32).T
        x = group_ref[i].astype(f32)
        centered = x - jnp.mean(x, axis=-1, keepdims=True)
        reciprocal = lax.rsqrt(jnp.mean(centered * centered, axis=-1, keepdims=True) + EPS)
        normalized = centered * reciprocal
        scaled = upstream * gain
        first = jnp.mean(scaled, axis=-1, keepdims=True)
        second = jnp.mean(scaled * normalized, axis=-1, keepdims=True)
        out_ref[i] = (reciprocal * (scaled - first - normalized * second)).astype(bf16)


def group_call(group, gain, wq, wk, wv, wg, coef, grad_kv, grad_q):
    return pl.pallas_call(
        group_kernel,
        out_shape=jax.ShapeDtypeStruct(group.shape, bf16),
        compiler_params=pltpu.CompilerParams(vmem_limit_bytes=VMEM_LIMIT),
        cost_estimate=pl.CostEstimate(
            flops=160_000_000, bytes_accessed=2_000_000, transcendentals=1000
        ),
        name="group_backward",
    )(group, gain, wq, wk, wv, wg, coef, grad_kv, grad_q)


def pair_kernel(pair_ref, gain_ref, weight_ref, came, out_ref, xhat, recip, grad, db):
    weight = jnp.concatenate(
        [weight_ref[...].astype(f32), jnp.zeros((BLOCK, BLOCK - HEADS), f32)], axis=1
    ).T[:8] * gain_ref[...]
    high, low = split_high_low(weight)
    weights = jnp.concatenate([high, high, low, jnp.zeros((8, BLOCK), bf16)], axis=0)
    db[...] = jnp.zeros_like(db)
    for h in range(HEADS):
        wide = [came[zh, h].astype(f32) for zh in range(4)]
        value = (wide[0] + wide[1]) + (wide[2] + wide[3])
        for k in range(32):
            db[k, h : h + 1, :] = value[k : k + 1]

    def rows(step, carry):
        x = pair_ref[pl.ds(step * 16, 16)].astype(f32).reshape(512, BLOCK)
        centered = x - jnp.mean(x, axis=-1, keepdims=True)
        reciprocal = lax.rsqrt(jnp.mean(centered * centered, axis=-1, keepdims=True) + EPS)
        at = pl.ds(pl.multiple_of(step * 512, 512), 512)
        xhat[at, :] = centered * reciprocal
        recip[at, :] = jnp.broadcast_to(reciprocal, (512, BLOCK))
        return carry

    lax.fori_loop(0, 8, rows, 0)
    for k in range(32):
        db_high, db_low = split_high_low(db[k])
        left = jnp.concatenate([db_high, db_low, db_high, jnp.zeros((8, BLOCK), bf16)], axis=0)
        scaled = lax.dot_general(left, weights, TN, preferred_element_type=f32)
        at = pl.ds(k, BLOCK, stride=32)
        normalized = xhat[at, :]
        first = jnp.mean(scaled, axis=-1, keepdims=True)
        second = jnp.mean(scaled * normalized, axis=-1, keepdims=True)
        grad[at, :] = recip[at, :] * (scaled - first - normalized * second)

    def store(step, carry):
        at = pl.ds(pl.multiple_of(step * 512, 512), 512)
        out_ref[pl.ds(step * 16, 16)] = grad[at, :].astype(bf16).reshape(16, 32, BLOCK)
        return carry

    lax.fori_loop(0, 8, store, 0)


def pair_call(pair, gain, weight, came):
    big = pltpu.VMEM((4096, BLOCK), f32)
    return pl.pallas_call(
        pair_kernel,
        out_shape=jax.ShapeDtypeStruct(pair.shape, bf16),
        scratch_shapes=[big, big, big, pltpu.VMEM((32, 8, BLOCK), f32)],
        compiler_params=pltpu.CompilerParams(vmem_limit_bytes=VMEM_LIMIT),
        cost_estimate=pl.CostEstimate(
            flops=60_000_000, bytes_accessed=2_200_000, transcendentals=4096
        ),
        name="pair_backward",
    )(pair, gain, weight, came)


def exchange(value, axes):
    return lax.all_to_all(value, axes, split_axis=0, concat_axis=0, tiled=True)


def other_core(value):
    return lax.ppermute(value, "core", [(0, 1), (1, 0)])


def per_device(
    group, pair, mask, ln_gain, ln_shift, w_query, w_key, w_value, w_gate, gate_bias, w_bias,
    w_out, cotangent,
):
    gain, shift = ln_gain.reshape(1, BLOCK), ln_shift.reshape(1, BLOCK)
    pieces = bias_call(pair, gain, shift, w_bias)
    near = exchange(pieces.reshape(16, 32, BLOCK), ("zh", "y")).reshape(1, 4, 4, 32, BLOCK)
    plane = exchange(jnp.broadcast_to(near, (4, 4, 4, 32, BLOCK)), "x")
    other = other_core(plane)

    key_value, query_up, coef = project_call(
        group, cotangent, gain, shift, w_query, w_key, w_value, w_gate,
        gate_bias.reshape(1, BLOCK), w_out,
    )
    kv_shape = key_value.shape
    flat = (8,) + kv_shape[2:]
    key_value = exchange(key_value.reshape(flat), ("z", "y")).reshape(kv_shape)
    query_up = exchange(query_up, "y")

    grad_kv, grad_q, keep, send = attention_call(
        mask.reshape(-1, BLOCK), plane, other, key_value, query_up
    )

    both = add_call(add_two_kernel, keep.shape, keep, other_core(send))
    line = add_call(add_four_kernel, keep.shape[1:], exchange(both, "x"))
    came = exchange(line.reshape(16, 32, BLOCK), ("zh", "y")).reshape(line.shape)

    grad_kv = exchange(grad_kv.reshape(flat), ("z", "y")).reshape(kv_shape)
    grad_q = exchange(grad_q, "y")
    grad_group = group_call(group, gain, w_query, w_key, w_value, w_gate, coef, grad_kv, grad_q)
    grad_pair = pair_call(pair, gain, w_bias, came)
    return (grad_group, grad_pair)


def solution(mesh):
    fine = jax.sharding.Mesh(mesh.devices.reshape(4, 4, 2, 2, 4), ("x", "zh", "core", "z", "y"))
    row, col = ("x", "zh", "core"), ("z", "y")
    placed = (
        P(row, col, None),
        P(col, row, None),
        P(), P(), P(), P(), P(), P(), P(), P(), P(), P(),
        P(row, col, None),
    )
    return jax.shard_map(
        per_device,
        mesh=fine,
        in_specs=placed,
        out_specs=(P(row, col, None), P(col, row, None)),
        check_vma=False,
    )
```

time: 632 us -> 140 us (0.22)
  waiting for transfers between devices: 483 us -> 40.8 us
  matrix products: 62.8 us -> 0 us
  local copies, waits for them, and re-layouts: 63.1 us -> 5.24 us
  blocking collectives: 0 us -> 33.8 us
  Pallas kernels: 0 us -> 31.9 us
  starting transfers between devices: 0.43 us -> 26.4 us
  between operations: 15.3 us -> 0.77 us
    unnamed x9 -> x0, waiting for transfers between devices: 355 us -> none
    all_gather x3 -> x0, waiting for transfers between devices: 128 us -> none  [the longest x1 47.1 us: per_device(): bias = lax.all_gather(local_bias, 'row', axis=2, tiled=True)]
    dot_general x36 -> x0, matrix products: 52.3 us -> none  [the longest x5 17.1 us: attention_row(): jnp.einsum('jhc,khc->hjk', grad_attended, value_row, preferred_element_ty...]
    all_to_all x0 -> x5, waiting for transfers between devices: none -> 40.8 us  [exchange(): return lax.all_to_all(value, axes, split_axis=0, concat_axis=0, tiled=True)]
    all_to_all x0 -> x3, blocking collectives: none -> 33.8 us  [exchange(): return lax.all_to_all(value, axes, split_axis=0, concat_axis=0, tiled=True)]
    pallas_call x0 -> x7, Pallas kernels: none -> 31.9 us  [the longest x1 16 us: attention_call(): pl.pallas_call(attention_kernel, out_shape=(jax.ShapeDtypeStruct(key_valu...]
    dynamic_update_slice x10 -> x0, local copies, waits for them, and re-layouts: 27.9 us -> none  [per_device(): lax.scan(scan_row, jnp.zeros((HEADS, col_count, key_count), jnp.float32),...]
    all_to_all x0 -> x5, starting transfers between devices: none -> 26.4 us  [exchange(): return lax.all_to_all(value, axes, split_axis=0, concat_axis=0, tiled=True)]
  transfers between devices with their start and end apart: 6 -> 7, of which waited for: 6 -> 5; matrix products, arithmetic and copies ran while one was open for 4% -> 0% of each run, Pallas kernels for 0% -> 3%
where the time goes in v1:
time: 140 us; the launch traced here: 139 us
  waiting for transfers between devices  40.8 us (29%)
  blocking collectives  33.8 us (24%)
  Pallas kernels  31.9 us (23%)
  starting transfers between devices  26.4 us (19%)
  local copies, waits for them, and re-layouts  5.24 us (4%)
    all_to_all x5, waiting for transfers between devices, exchange(): return lax.all_to_all(value, axes, split_axis=0, concat_axis=0, tiled=True)  40.8 us
    all_to_all x3, blocking collectives, exchange(): return lax.all_to_all(value, axes, split_axis=0, concat_axis=0, tiled=True)  33.8 us
    all_to_all x5, starting transfers between devices, exchange(): return lax.all_to_all(value, axes, split_axis=0, concat_axis=0, tiled=True)  26.4 us
    pallas_call x1, Pallas kernels, attention_call(): pl.pallas_call(attention_kernel, out_shape=(jax.ShapeDtypeStruct(key_valu...  16 us
    pallas_call x1, Pallas kernels, pair_call(): pl.pallas_call(pair_kernel, out_shape=jax.ShapeDtypeStruct(pair.shape, bf...  7.62 us
    unnamed x31, local copies, waits for them, and re-layouts  5.15 us
    pallas_call x1, Pallas kernels, bias_call(): pl.pallas_call(bias_kernel, out_shape=jax.ShapeDtypeStruct((4, HEADS, 32,...  3.87 us
  transfers between devices with their start and end apart: 7, of which 5 were waited for; matrix products, arithmetic and copies ran while one was open for 0% of the time, Pallas kernels for 3%

profile of v1, /device:TPU:32, one launch (start us, length us, event | category | flops | bytes accessed | tf_op | source)
XLA Modules:
  0.0 139.0 jit_solution(13309232120600162097)
XLA Ops:
  0.6 0.8 copy.15.weight_ref
  1.5 0.6 copy-done.9
  2.1 1.2 copy-done
  3.3 3.9 %pair_bias.1 = bf16[4,4,32,128]{3,2,1,0:T(8,128)(2,1)} custom-call(bf16[128,32,128]{2,1,0:T(8,128)(2,1)S(1)} %copy-done, f32[1,128]{1,0:T(1,128)S(1)} %bitcast.15, f32[1,128]{1,0:T(1,128)S(1)} %bitcast.19, bf16[128,4]{1,0:T(8,128)(2,1)S(1)} %copy.15.weight_ref), custom_call_target="tpu_custom_call" | custom-call | flops 20000000 | bytes 1200000 | tf_op jit(solution)/shard_map/pair_bias/pallas_call | solution.py:51
  7.2 10.4 %all-to-all-start = ((bf16[16,32,128]{2,1,0:T(8,128)(2,1)}), bf16[16,32,128]{2,1,0:T(8,128)(2,1)S(1)}, u32[]{:S(2)}, u32[]{:S(2)}) async-start(bf16[16,32,128]{2,1,0:T(8,128)(2,1)} %bitcast.4), calls=%async_computation | async-start | bytes 262144 | tf_op jit(solution)/shard_map/all_to_all | solution.py:324
  18.3 1.7 %project.1 = (bf16[2,4,2,5,32,128]{5,4,3,2,1,0:T(8,128)(2,1)}, bf16[4,2,5,32,128]{4,3,2,1,0:T(8,128)(2,1)S(1)}, f32[5,128,128]{2,1,0:T(8,128)S(1)}) custom-call(bf16[5,128,128]{2,1,0:T(8,128)(2,1)S(1)} %copy-done.2, bf16[5,128,128]{2,1,0:T(8,128)(2,1)S(1)} %copy-done.3, f32[1,128]{1,0:T(1,128)S(1)} %bitcast.16, f32[1,128]{1,0:T(1,128)S(1)} %bitcast.20, ...), custom_call_target="tpu_custom_call" | custom-call | flops 110000000 | bytes 2000000 | tf_op jit(solution)/shard_map/project/pallas_call | solution.py:93
  20.0 8.1 %all-to-all-done = bf16[16,32,128]{2,1,0:T(8,128)(2,1)S(1)} async-done(((bf16[16,32,128]{2,1,0:T(8,128)(2,1)}), bf16[16,32,128]{2,1,0:T(8,128)(2,1)S(1)}, u32[]{:S(2)}, u32[]{:S(2)}) %all-to-all-start) | async-done | bytes 131104 | tf_op jit(solution)/shard_map/all_to_all | solution.py:324
  28.2 9.6 %all_to_all.40.query_up = bf16[4,2,5,32,128]{4,3,2,1,0:T(8,128)(2,1)S(1)} all-to-all(bf16[4,2,5,32,128]{4,3,2,1,0:T(8,128)(2,1)S(1)} %get-tuple-element.11), channel_id=1, replica_groups=mesh['x'=4,'zh'=4,'core'=2,'z'=2,'y'=4] {'y'}, dimensions={0} | all-to-all | bytes 655360 | tf_op jit(solution)/shard_map/all_to_all | solution.py:324
  37.9 12.2 %all_to_all.41.bias_own = bf16[4,4,4,32,128]{4,3,2,1,0:T(8,128)(2,1)S(1)} all-to-all(bf16[4,4,4,32,128]{4,3,2,1,0:T(8,128)(2,1)S(1)} %broadcast_in_dim.8), channel_id=1, replica_groups=mesh['x'=4,'zh'=4,'core'=2,'z'=2,'y'=4] {'x'}, dimensions={0} | all-to-all | bytes 1048576 | tf_op jit(solution)/shard_map/all_to_all | solution.py:324
  50.1 4.5 %all-to-all-start.2 = ((bf16[8,2,5,32,128]{4,3,2,1,0:T(8,128)(2,1)}), bf16[8,2,5,32,128]{4,3,2,1,0:T(8,128)(2,1)S(1)}, u32[]{:S(2)}, u32[]{:S(2)}) async-start(bf16[8,2,5,32,128]{4,3,2,1,0:T(8,128)(2,1)} %bitcast.6), calls=%async_computation.2 | async-start | bytes 1310720 | tf_op jit(solution)/shard_map/all_to_all | solution.py:324
  54.6 7.9 %all-to-all-done.2 = bf16[8,2,5,32,128]{4,3,2,1,0:T(8,128)(2,1)S(1)} async-done(((bf16[8,2,5,32,128]{4,3,2,1,0:T(8,128)(2,1)}), bf16[8,2,5,32,128]{4,3,2,1,0:T(8,128)(2,1)S(1)}, u32[]{:S(2)}, u32[]{:S(2)}) %all-to-all-start.2) | async-done | bytes 655392 | tf_op jit(solution)/shard_map/all_to_all | solution.py:324
  62.5 0.8 copy-done.12
  63.3 1.0 copy-done.13
  64.4 16.0 %attention.1 = (bf16[2,4,2,5,32,128]{5,4,3,2,1,0:T(8,128)(2,1)}, bf16[4,2,5,32,128]{4,3,2,1,0:T(8,128)(2,1)}, f32[4,4,4,32,128]{4,3,2,1,0:T(8,128)S(1)}, bf16[4,4,4,32,128]{4,3,2,1,0:T(8,128)(2,1)}) custom-call(s32[8,128]{1,0:T(8,128)S(1)} %bitcast.22, bf16[4,4,4,32,128]{4,3,2,1,0:T(8,128)(2,1)S(1)} %all_to_all.41.bias_own, ...), custom_call_target="tpu_custom_call" | custom-call | flops 8000000000 | bytes 6000000 | tf_op jit(solution)/shard_map/attention/pallas_call | solution.py:183
  80.4 3.5 %all-to-all-start.5 = ((bf16[4,2,5,32,128]{4,3,2,1,0:T(8,128)(2,1)}), bf16[4,2,5,32,128]{4,3,2,1,0:T(8,128)(2,1)S(1)}, u32[]{:S(2)}, u32[]{:S(2)}) async-start(bf16[4,2,5,32,128]{4,3,2,1,0:T(8,128)(2,1)} %get-tuple-element.13), calls=%async_computation.5 | async-start | bytes 655360 | tf_op jit(solution)/shard_map/all_to_all | solution.py:324
  83.9 8.2 %all-to-all-done.5.grad_q = bf16[4,2,5,32,128]{4,3,2,1,0:T(8,128)(2,1)S(1)} async-done(((bf16[4,2,5,32,128]{4,3,2,1,0:T(8,128)(2,1)}), bf16[4,2,5,32,128]{4,3,2,1,0:T(8,128)(2,1)S(1)}, u32[]{:S(2)}, u32[]{:S(2)}) %all-to-all-start.5) | async-done | bytes 327712 | tf_op jit(solution)/shard_map/all_to_all | solution.py:324
  92.1 12.0 %all_to_all.42.came = bf16[4,4,4,32,128]{4,3,2,1,0:T(8,128)(2,1)S(1)} all-to-all(bf16[4,4,4,32,128]{4,3,2,1,0:T(8,128)(2,1)S(1)} %add_bias_gradient.2), channel_id=1, replica_groups=mesh['x'=4,'zh'=4,'core'=2,'z'=2,'y'=4] {'x'}, dimensions={0} | all-to-all | bytes 1048576 | tf_op jit(solution)/shard_map/all_to_all | solution.py:324
  104.2 4.3 %all-to-all-start.4 = ((bf16[8,2,5,32,128]{4,3,2,1,0:T(8,128)(2,1)}), bf16[8,2,5,32,128]{4,3,2,1,0:T(8,128)(2,1)S(1)}, u32[]{:S(2)}, u32[]{:S(2)}) async-start(bf16[8,2,5,32,128]{4,3,2,1,0:T(8,128)(2,1)} %bitcast.8), calls=%async_computation.4 | async-start | bytes 1310720 | tf_op jit(solution)/shard_map/all_to_all | solution.py:324
  108.5 0.7 add_bias_gradient.3
  109.2 8.3 %all-to-all-done.4 = bf16[8,2,5,32,128]{4,3,2,1,0:T(8,128)(2,1)S(1)} async-done(((bf16[8,2,5,32,128]{4,3,2,1,0:T(8,128)(2,1)}), bf16[8,2,5,32,128]{4,3,2,1,0:T(8,128)(2,1)S(1)}, u32[]{:S(2)}, u32[]{:S(2)}) %all-to-all-start.4) | async-done | bytes 655392 | tf_op jit(solution)/shard_map/all_to_all | solution.py:324
  117.6 3.7 %all-to-all-start.7 = ((bf16[16,32,128]{2,1,0:T(8,128)(2,1)}), bf16[16,32,128]{2,1,0:T(8,128)(2,1)S(1)}, u32[]{:S(2)}, u32[]{:S(2)}) async-start(bf16[16,32,128]{2,1,0:T(8,128)(2,1)} %bitcast.10), calls=%async_computation.7 | async-start | bytes 262144 | tf_op jit(solution)/shard_map/all_to_all | solution.py:324
  121.3 1.9 %group_backward.1 = bf16[5,128,128]{2,1,0:T(8,128)(2,1)} custom-call(bf16[5,128,128]{2,1,0:T(8,128)(2,1)S(1)} %copy-done.2, f32[1,128]{1,0:T(1,128)S(1)} %bitcast.17, bf16[128,128]{1,0:T(8,128)(2,1)S(1)} %copy-done.4, bf16[128,128]{1,0:T(8,128)(2,1)S(1)} %copy-done.5, bf16[128,128]{1,0:T(8,128)(2,1)S(1)} %copy-done.6, bf16[128,128]{1,0:T(8,128)(2,1)S(1)} %copy-done.7, ...), custom_call_target="tpu_custom_call" | custom-call | flops 160000000 | bytes 2000000 | tf_op jit(solution)/shard_map/group_backward/pallas_call | solution.py:257
  123.2 8.2 %all-to-all-done.7 = bf16[16,32,128]{2,1,0:T(8,128)(2,1)S(1)} async-done(((bf16[16,32,128]{2,1,0:T(8,128)(2,1)}), bf16[16,32,128]{2,1,0:T(8,128)(2,1)S(1)}, u32[]{:S(2)}, u32[]{:S(2)}) %all-to-all-start.7) | async-done | bytes 131104 | tf_op jit(solution)/shard_map/all_to_all | solution.py:324
  131.3 7.6 %pair_backward.1 = bf16[128,32,128]{2,1,0:T(8,128)(2,1)} custom-call(bf16[128,32,128]{2,1,0:T(8,128)(2,1)S(1)} %copy-done.1, f32[1,128]{1,0:T(1,128)S(1)} %bitcast.18, bf16[128,4]{1,0:T(8,128)(2,1)S(1)} %copy.15.weight_ref, bf16[4,4,32,128]{3,2,1,0:T(8,128)(2,1)S(1)} %bitcast.14), custom_call_target="tpu_custom_call" | custom-call | flops 60000000 | bytes 2200000 | tf_op jit(solution)/shard_map/pair_backward/pallas_call | solution.py:311
  (32 shorter events, 0.8 us)
Async XLA Ops:
  1.4 0.7 copy-start.9
  1.4 0.7 copy-start.10
  2.1 1.2 copy-start
  3.3 14.4 %copy-start.3 = (bf16[5,128,128]{2,1,0:T(8,128)(2,1)S(1)}, bf16[5,128,128]{2,1,0:T(8,128)(2,1)}, u32[]{:S(2)}) copy-start(bf16[5,128,128]{2,1,0:T(8,128)(2,1)} %cot_ref.1) | copy-start | bytes 491524
  3.3 14.4 %copy-start.7 = (bf16[128,128]{1,0:T(8,128)(2,1)S(1)}, bf16[128,128]{1,0:T(8,128)(2,1)}, u32[]{:S(2)}) copy-start(bf16[128,128]{1,0:T(8,128)(2,1)} %wg_ref.3) | copy-start | bytes 98308
  3.3 14.4 %copy-start.8 = (bf16[128,128]{1,0:T(8,128)(2,1)S(1)}, bf16[128,128]{1,0:T(8,128)(2,1)}, u32[]{:S(2)}) copy-start(bf16[128,128]{1,0:T(8,128)(2,1)} %wo_ref.1) | copy-start | bytes 98308
  7.2 10.5 %copy-start.2 = (bf16[5,128,128]{2,1,0:T(8,128)(2,1)S(1)}, bf16[5,128,128]{2,1,0:T(8,128)(2,1)}, u32[]{:S(2)}) copy-start(bf16[5,128,128]{2,1,0:T(8,128)(2,1)} %group_ref.3) | copy-start | bytes 491524
  7.2 10.5 %copy-start.4 = (bf16[128,128]{1,0:T(8,128)(2,1)S(1)}, bf16[128,128]{1,0:T(8,128)(2,1)}, u32[]{:S(2)}) copy-start(bf16[128,128]{1,0:T(8,128)(2,1)} %wq_ref.3) | copy-start | bytes 98308
  7.2 10.5 %copy-start.5 = (bf16[128,128]{1,0:T(8,128)(2,1)S(1)}, bf16[128,128]{1,0:T(8,128)(2,1)}, u32[]{:S(2)}) copy-start(bf16[128,128]{1,0:T(8,128)(2,1)} %wk_ref.3) | copy-start | bytes 98308
  7.2 10.5 %copy-start.6 = (bf16[128,128]{1,0:T(8,128)(2,1)S(1)}, bf16[128,128]{1,0:T(8,128)(2,1)}, u32[]{:S(2)}) copy-start(bf16[128,128]{1,0:T(8,128)(2,1)} %wv_ref.3) | copy-start | bytes 98308
  7.2 20.9 %all-to-all-start = ((bf16[16,32,128]{2,1,0:T(8,128)(2,1)}), bf16[16,32,128]{2,1,0:T(8,128)(2,1)S(1)}, u32[]{:S(2)}, u32[]{:S(2)}) async-start(bf16[16,32,128]{2,1,0:T(8,128)(2,1)} %bitcast.4), calls=%async_computation | async-start | bytes 262144 | tf_op jit(solution)/shard_map/all_to_all | solution.py:324
  17.7 0.7 copy-start.11
  50.1 13.3 %copy-start.14 = (s32[1024]{0:T(1024)S(1)}, s32[1024]{0:T(1024)}, u32[]{:S(2)}) copy-start(s32[1024]{0:T(1024)} %param.15) | copy-start | bytes 12292
  50.1 12.5 %all-to-all-start.2 = ((bf16[8,2,5,32,128]{4,3,2,1,0:T(8,128)(2,1)}), bf16[8,2,5,32,128]{4,3,2,1,0:T(8,128)(2,1)S(1)}, u32[]{:S(2)}, u32[]{:S(2)}) async-start(bf16[8,2,5,32,128]{4,3,2,1,0:T(8,128)(2,1)} %bitcast.6), calls=%async_computation.2 | async-start | bytes 1310720 | tf_op jit(solution)/shard_map/all_to_all | solution.py:324
  54.6 8.0 %collective-permute-start = (bf16[4,4,4,32,128]{4,3,2,1,0:T(8,128)(2,1)S(1)}, bf16[4,4,4,32,128]{4,3,2,1,0:T(8,128)(2,1)S(1)}, u32[]{:S(2)}, u32[]{:S(2)}) collective-permute-start(bf16[4,4,4,32,128]{4,3,2,1,0:T(8,128)(2,1)S(1)} %all_to_all.41.bias_own), channel_id=1, source_target_pairs={{0,8},{8,0},{1,9},{9,1},{2,10},{10,2},{3,11},{11,3},{4,12},{12,4},... | collective-permute-start | bytes 1572872 | tf_op jit(solution)/shard_map/ppermute | solution.py:328
  62.5 0.8 copy-start.12
  63.3 1.0 copy-start.13
  80.4 3.5 %collective-permute-start.1 = (bf16[4,4,4,32,128]{4,3,2,1,0:T(8,128)(2,1)}, bf16[4,4,4,32,128]{4,3,2,1,0:T(8,128)(2,1)S(1)}, u32[]{:S(2)}, u32[]{:S(2)}) collective-permute-start(bf16[4,4,4,32,128]{4,3,2,1,0:T(8,128)(2,1)} %get-tuple-element.15), channel_id=1, source_target_pairs={{0,8},{8,0},{1,9},{9,1},{2,10},{10,2},{3,11},{11,3},{4,12},{12,4},... | collective-permute-start | bytes 1572872 | tf_op jit(solution)/shard_map/ppermute | solution.py:328
  80.4 11.7 %all-to-all-start.5 = ((bf16[4,2,5,32,128]{4,3,2,1,0:T(8,128)(2,1)}), bf16[4,2,5,32,128]{4,3,2,1,0:T(8,128)(2,1)S(1)}, u32[]{:S(2)}, u32[]{:S(2)}) async-start(bf16[4,2,5,32,128]{4,3,2,1,0:T(8,128)(2,1)} %get-tuple-element.13), calls=%async_computation.5 | async-start | bytes 655360 | tf_op jit(solution)/shard_map/all_to_all | solution.py:324
  104.2 13.4 %all-to-all-start.4 = ((bf16[8,2,5,32,128]{4,3,2,1,0:T(8,128)(2,1)}), bf16[8,2,5,32,128]{4,3,2,1,0:T(8,128)(2,1)S(1)}, u32[]{:S(2)}, u32[]{:S(2)}) async-start(bf16[8,2,5,32,128]{4,3,2,1,0:T(8,128)(2,1)} %bitcast.8), calls=%async_computation.4 | async-start | bytes 1310720 | tf_op jit(solution)/shard_map/all_to_all | solution.py:324
  109.2 22.1 %copy-start.1 = (bf16[128,32,128]{2,1,0:T(8,128)(2,1)S(1)}, bf16[128,32,128]{2,1,0:T(8,128)(2,1)}, u32[]{:S(2)}) copy-start(bf16[128,32,128]{2,1,0:T(8,128)(2,1)} %pair_ref.3) | copy-start | bytes 3145732
  117.6 13.8 %all-to-all-start.7 = ((bf16[16,32,128]{2,1,0:T(8,128)(2,1)}), bf16[16,32,128]{2,1,0:T(8,128)(2,1)S(1)}, u32[]{:S(2)}, u32[]{:S(2)}) async-start(bf16[16,32,128]{2,1,0:T(8,128)(2,1)} %bitcast.10), calls=%async_computation.7 | async-start | bytes 262144 | tf_op jit(solution)/shard_map/all_to_all | solution.py:324

commit v2 on v1

v2 whole, which is shorter than its diff:
```python
import jax
import jax.numpy as jnp
from jax import lax
from jax.experimental import pallas as pl
from jax.experimental.pallas import tpu as pltpu
from jax.sharding import PartitionSpec as P

HEADS = 4
HEAD_DIM = 32
BLOCK = 128
EPS = 1e-05
SCALE = HEAD_DIM ** (-0.5)
VMEM_LIMIT = 48 * 1024 * 1024

bf16, f32 = jnp.bfloat16, jnp.float32
NT = (((1,), (1,)), ((), ()))
TN = (((0,), (0,)), ((), ()))


def place():
    return tuple(lax.axis_index(name) for name in ("x", "zh", "core", "z", "y"))


def split_high_low(value):
    high = value.astype(bf16)
    return high, (value - high.astype(f32)).astype(bf16)


def front_kernel(
    group_ref, cot_ref, pair_ref, gain_ref, shift_ref, wq_ref, wk_ref, wv_ref, wg_ref, gb_ref,
    wo_ref, wb_ref, s0, s1, s2, s3, coef, normed, heads, parts,
):
    _, _, _, _, y = place()
    gain, shift = gain_ref[...], shift_ref[...]
    turned = [w[...].astype(f32).T.astype(bf16) for w in (wq_ref, wk_ref, wv_ref, wg_ref)]
    gate_bias = jnp.broadcast_to(gb_ref[...], (BLOCK, BLOCK)).T
    rows = group_ref.shape[0]
    for i in range(rows):
        x = group_ref[i].astype(f32)
        centered = x - jnp.mean(x, axis=-1, keepdims=True)
        reciprocal = lax.rsqrt(jnp.mean(centered * centered, axis=-1, keepdims=True) + EPS)
        low = (centered * reciprocal * gain + shift).astype(bf16)
        dots = [lax.dot_general(w, low, NT, preferred_element_type=f32) for w in turned]
        gating = jax.nn.sigmoid(dots[3] + gate_bias)
        gated = lax.dot_general(wo_ref[...], cot_ref[i], NT, preferred_element_type=f32)
        upstream = gated * gating
        coef[i] = upstream * (1.0 - gating)
        for n, value in enumerate((dots[1], dots[2], dots[0] * SCALE, upstream)):
            value = value.astype(bf16).reshape(HEADS, HEAD_DIM, BLOCK)
            for h in range(HEADS):
                parts[h, n * rows + i] = value[h]

    weight_t = jnp.concatenate(
        [wb_ref[...].astype(f32), jnp.zeros((BLOCK, BLOCK - HEADS), f32)], axis=1
    ).T[:16].astype(bf16)

    def norm_rows(step, carry):
        x = pair_ref[pl.ds(step * 16, 16)].astype(f32).reshape(512, BLOCK)
        centered = x - jnp.mean(x, axis=-1, keepdims=True)
        reciprocal = lax.rsqrt(jnp.mean(centered * centered, axis=-1, keepdims=True) + EPS)
        low = (centered * reciprocal * gain + shift).astype(bf16).astype(f32)
        normed[pl.ds(pl.multiple_of(step * 512, 512), 512), :] = low
        return carry

    lax.fori_loop(0, 8, norm_rows, 0)

    for k in range(32):
        block = normed[pl.ds(k, BLOCK, stride=32), :].astype(bf16)
        product = lax.dot_general(weight_t, block, NT, preferred_element_type=f32)
        for h in range(HEADS):
            heads[h, k : k + 1, :] = product[h : h + 1]
    for h in range(HEADS):
        parts[h, 4 * rows] = heads[h].astype(bf16)
    for step, out in enumerate((s0, s1, s2, s3)):
        out[...] = parts[lax.rem(y + step, 4)]


def front_call(group, cotangent, pair, *small):
    rows = group.shape[0]
    sent = jax.ShapeDtypeStruct((4 * rows + 1, HEAD_DIM, BLOCK), bf16)
    return pl.pallas_call(
        front_kernel,
        out_shape=(sent,) * 4 + (jax.ShapeDtypeStruct((rows, BLOCK, BLOCK), f32),),
        scratch_shapes=[
            pltpu.VMEM((4096, BLOCK), f32),
            pltpu.VMEM((HEADS, 32, BLOCK), f32),
            pltpu.VMEM((HEADS, 4 * rows + 1, HEAD_DIM, BLOCK), bf16),
        ],
        compiler_params=pltpu.CompilerParams(vmem_limit_bytes=VMEM_LIMIT),
        cost_estimate=pl.CostEstimate(
            flops=130_000_000, bytes_accessed=3_000_000, transcendentals=100_000
        ),
        name="front",
    )(group, cotangent, pair, *small)


def attention_kernel(
    mask_ref, bias_own, bias_other, s0, s1, s2, s3, kv_other,
    out_own, out_other, out_q, keep, send,
    bias, grad, key_t, value_t, key_s, value_s, query_t, up_t, key_out,
):
    x, zh, core, z, y = place()
    keys, queries = bias.shape
    rows = key_t.shape[0]

    for blk in range(keys // BLOCK):
        live = jnp.broadcast_to(mask_ref[blk : blk + 1, :].astype(f32), (BLOCK, BLOCK)).T
        bias[blk * BLOCK : (blk + 1) * BLOCK, :] = jnp.concatenate([live] * (queries // BLOCK), 1)
    for source, c in ((bias_own, core), (bias_other, 1 - core)):
        for dx in range(4):
            for dz in range(4):
                r = lax.rem(x - dx + 4, 4) * 8 + lax.rem(zh - dz + 4, 4) * 2 + c
                at = pl.ds(pl.multiple_of(r * 32, 32), 32)
                for dy in range(4):
                    lanes = slice(dy * BLOCK, (dy + 1) * BLOCK)
                    bias[at, lanes] = jnp.where(
                        bias[at, lanes] > 0.0, source[dx, dz, dy].astype(f32), -jnp.inf
                    )
    grad[...] = jnp.zeros_like(grad)

    for step, own in enumerate((s0, s1, s2, s3)):
        yy = lax.rem(y - step + 4, 4)
        for source, c in ((own, z * 4 + yy), (kv_other.at[step], (1 - z) * 4 + yy)):
            at = pl.ds(pl.multiple_of(c * BLOCK, BLOCK), BLOCK)
            for i in range(rows):
                k, v = source[i], source[rows + i]
                key_t[i, :, at] = k
                value_t[i, :, at] = v
                key_s[i, at, :] = k.astype(f32).T.astype(bf16)
                value_s[i, at, :] = v.astype(f32).T.astype(bf16)
        for i in range(rows):
            query_t[i, :, step * BLOCK : (step + 1) * BLOCK] = own[2 * rows + i]
            up_t[i, :, step * BLOCK : (step + 1) * BLOCK] = own[3 * rows + i]

    width = 256

    def row(i, carry):
        grad_key = jnp.zeros((keys, HEAD_DIM), f32)
        grad_value = jnp.zeros((keys, HEAD_DIM), f32)
        for part in range(queries // width):
            lanes = slice(part * width, (part + 1) * width)
            q, g = query_t[i, :, lanes], up_t[i, :, lanes]
            scores = jnp.dot(key_s[i], q, preferred_element_type=f32) + bias[:, lanes]
            raised = jnp.exp(scores)
            weights = raised * (1.0 / jnp.sum(raised, axis=0, keepdims=True))
            low = weights.astype(bf16)
            attended = jnp.dot(value_t[i], low, preferred_element_type=f32)
            delta = jnp.sum(g.astype(f32) * attended, axis=0, keepdims=True)
            grad_weights = jnp.dot(value_s[i], g, preferred_element_type=f32)
            grad_scores = weights * (grad_weights - delta)
            grad[:, lanes] += grad_scores
            scores_low = grad_scores.astype(bf16)
            grad_query = jnp.dot(key_t[i], scores_low, preferred_element_type=f32) * SCALE
            grad_key += lax.dot_general(scores_low, q, NT, preferred_element_type=f32)
            grad_value += lax.dot_general(low, g, NT, preferred_element_type=f32)
            for n in range(width // BLOCK):
                block, at = part * (width // BLOCK) + n, slice(n * BLOCK, (n + 1) * BLOCK)
                out_q[block, i] = grad_query[:, at].astype(bf16)
                out_q[block, rows + i] = attended[:, at].astype(bf16)
        both = jnp.concatenate([grad_key, grad_value], axis=1).T.astype(bf16)
        key_out[i, 0] = both[:HEAD_DIM]
        key_out[i, 1] = both[HEAD_DIM:]
        return carry

    lax.fori_loop(0, rows, row, 0)

    for step in range(4):
        yy = lax.rem(y - step + 4, 4)
        for out, c in ((out_own, z * 4 + yy), (out_other, (1 - z) * 4 + yy)):
            at = pl.ds(pl.multiple_of(c * BLOCK, BLOCK), BLOCK)
            for i in range(rows):
                out[step, i] = key_out[i, 0, :, at]
                out[step, rows + i] = key_out[i, 1, :, at]
    for out, c in ((keep, core), (send, 1 - core)):
        for dx in range(4):
            for dz in range(4):
                r = lax.rem(x - dx + 4, 4) * 8 + lax.rem(zh - dz + 4, 4) * 2 + c
                at = pl.ds(pl.multiple_of(r * 32, 32), 32)
                for dy in range(4):
                    out[dx, dz, dy] = grad[at, dy * BLOCK : (dy + 1) * BLOCK].astype(out.dtype)


def attention_call(mask, bias_own, bias_other, pieces, kv_other):
    rows = kv_other.shape[1] // 2
    keys = mask.shape[0] * mask.shape[1]
    queries = keys // 2
    part = jax.ShapeDtypeStruct(kv_other.shape, bf16)
    return pl.pallas_call(
        attention_kernel,
        out_shape=(
            part, part, part,
            jax.ShapeDtypeStruct(bias_own.shape, f32),
            jax.ShapeDtypeStruct(bias_own.shape, bf16),
        ),
        scratch_shapes=[
            pltpu.VMEM((keys, queries), f32),
            pltpu.VMEM((keys, queries), f32),
            pltpu.VMEM((rows, HEAD_DIM, keys), bf16),
            pltpu.VMEM((rows, HEAD_DIM, keys), bf16),
            pltpu.VMEM((rows, keys, HEAD_DIM), bf16),
            pltpu.VMEM((rows, keys, HEAD_DIM), bf16),
            pltpu.VMEM((rows, HEAD_DIM, queries), bf16),
            pltpu.VMEM((rows, HEAD_DIM, queries), bf16),
            pltpu.VMEM((rows, 2, HEAD_DIM, keys), bf16),
        ],
        compiler_params=pltpu.CompilerParams(vmem_limit_bytes=VMEM_LIMIT),
        cost_estimate=pl.CostEstimate(
            flops=8_000_000_000, bytes_accessed=6_000_000, transcendentals=2_700_000
        ),
        name="attention",
    )(mask, bias_own, bias_other, *pieces, kv_other)


def add_core_kernel(keep, came, k0, s1, s2, s3):
    for n, out in enumerate((k0, s1, s2, s3)):
        out[...] = (keep[n] + came[n].astype(f32)).astype(out.dtype)


def add_core(keep, came):
    shape = keep.shape[1:]
    return pl.pallas_call(
        add_core_kernel,
        out_shape=(jax.ShapeDtypeStruct(shape, f32),) + (jax.ShapeDtypeStruct(shape, bf16),) * 3,
        compiler_params=pltpu.CompilerParams(vmem_limit_bytes=VMEM_LIMIT),
        name="add_core",
    )(keep, came)


def add_four_kernel(keep, c1, c2, c3, k0, s1, s2, s3):
    for n, out in enumerate((k0, s1, s2, s3)):
        total = keep[n] + c1[n].astype(f32) + c2[n].astype(f32) + c3[n].astype(f32)
        out[...] = total.astype(out.dtype)


def add_four(keep, c1, c2, c3):
    shape = keep.shape[1:]
    return pl.pallas_call(
        add_four_kernel,
        out_shape=(jax.ShapeDtypeStruct(shape, f32),) + (jax.ShapeDtypeStruct(shape, bf16),) * 3,
        compiler_params=pltpu.CompilerParams(vmem_limit_bytes=VMEM_LIMIT),
        name="add_four",
    )(keep, c1, c2, c3)


def pack_kernel(keep, c1, c2, c3, own, came, query, t0, t1, t2, t3):
    half = own.shape[1]
    for n, out in enumerate((t0, t1, t2, t3)):
        out[:half] = (own[n].astype(f32) + came[n].astype(f32)).astype(bf16)
        out[half : 2 * half] = query[n]
        total = keep[n] + c1[n].astype(f32) + c2[n].astype(f32) + c3[n].astype(f32)
        out[2 * half] = total.astype(bf16)


def pack_call(keep, c1, c2, c3, own, came, query):
    half, *tile = own.shape[1:]
    return pl.pallas_call(
        pack_kernel,
        out_shape=(jax.ShapeDtypeStruct((2 * half + 1, *tile), bf16),) * 4,
        compiler_params=pltpu.CompilerParams(vmem_limit_bytes=VMEM_LIMIT),
        name="pack",
    )(keep, c1, c2, c3, own, came, query)


def group_kernel(
    group_ref, gain_ref, wq_ref, wk_ref, wv_ref, wg_ref, coef,
    t0, t1, t2, t3, out_ref,
):
    _, _, _, _, y = place()
    gain = gain_ref[...]
    turn = lax.rem(4 - y, 4) * HEAD_DIM
    wq, wk, wv, wg = (
        pltpu.roll(w[...].astype(f32), turn, 1).astype(bf16)
        for w in (wq_ref, wk_ref, wv_ref, wg_ref)
    )
    weights = jnp.concatenate([wk, wv, wq, wg, wg], axis=1)
    rows = group_ref.shape[0]
    for i in range(rows):
        parts = [[] for _ in range(5)]
        for step, t in enumerate((t0, t1, t2, t3)):
            h = lax.rem(y + step, 4)
            at = pl.multiple_of(h * HEAD_DIM, HEAD_DIM)
            gate = coef[i, pl.ds(at, HEAD_DIM), :] * t[3 * rows + i].astype(f32)
            high, low = split_high_low(gate)
            pieces = (t[i], t[rows + i], t[2 * rows + i], high, low)
            for part, piece in zip(parts, pieces):
                part.append(piece)
        stacked = jnp.concatenate(sum(parts, []), axis=0)
        upstream = jnp.dot(weights, stacked, preferred_element_type=f32).T
        x = group_ref[i].astype(f32)
        centered = x - jnp.mean(x, axis=-1, keepdims=True)
        reciprocal = lax.rsqrt(jnp.mean(centered * centered, axis=-1, keepdims=True) + EPS)
        normalized = centered * reciprocal
        scaled = upstream * gain
        first = jnp.mean(scaled, axis=-1, keepdims=True)
        second = jnp.mean(scaled * normalized, axis=-1, keepdims=True)
        out_ref[i] = (reciprocal * (scaled - first - normalized * second)).astype(bf16)


def group_call(group, gain, wq, wk, wv, wg, coef, pieces):
    return pl.pallas_call(
        group_kernel,
        out_shape=jax.ShapeDtypeStruct(group.shape, bf16),
        compiler_params=pltpu.CompilerParams(vmem_limit_bytes=VMEM_LIMIT),
        cost_estimate=pl.CostEstimate(
            flops=160_000_000, bytes_accessed=2_000_000, transcendentals=1000
        ),
        name="group_backward",
    )(group, gain, wq, wk, wv, wg, coef, *pieces)


def pair_kernel(pair_ref, gain_ref, weight_ref, t0, t1, t2, t3, out_ref, grad, db):
    _, _, _, _, y = place()
    weight = jnp.concatenate(
        [weight_ref[...].astype(f32), jnp.zeros((BLOCK, BLOCK - HEADS), f32)], axis=1
    ).T[:8] * gain_ref[...]
    weight = weight - jnp.mean(weight, axis=-1, keepdims=True)
    high, low = split_high_low(weight)
    weights = jnp.concatenate([high, high, low, jnp.zeros((8, BLOCK), bf16)], axis=0)
    db[...] = jnp.zeros_like(db)
    last = t0.shape[0] - 1
    for step, t in enumerate((t0, t1, t2, t3)):
        h = lax.rem(y + step, 4)
        value = t[last].astype(f32)
        for k in range(32):
            db[k, pl.ds(h, 1), :] = value[k : k + 1]

    for k in range(32):
        db_high, db_low = split_high_low(db[k])
        left = jnp.concatenate([db_high, db_low, db_high, jnp.zeros((8, BLOCK), bf16)], axis=0)
        grad[pl.ds(k, BLOCK, stride=32), :] = lax.dot_general(
            left, weights, TN, preferred_element_type=f32
        )

    def rows(step, carry):
        x = pair_ref[pl.ds(step * 16, 16)].astype(f32).reshape(512, BLOCK)
        centered = x - jnp.mean(x, axis=-1, keepdims=True)
        reciprocal = lax.rsqrt(jnp.mean(centered * centered, axis=-1, keepdims=True) + EPS)
        normalized = centered * reciprocal
        scaled = grad[pl.ds(pl.multiple_of(step * 512, 512), 512), :]
        second = jnp.mean(scaled * normalized, axis=-1, keepdims=True)
        result = reciprocal * (scaled - normalized * second)
        out_ref[pl.ds(step * 16, 16)] = result.astype(bf16).reshape(16, 32, BLOCK)
        return carry

    lax.fori_loop(0, 8, rows, 0)


def pair_call(pair, gain, weight, pieces):
    return pl.pallas_call(
        pair_kernel,
        out_shape=jax.ShapeDtypeStruct(pair.shape, bf16),
        scratch_shapes=[pltpu.VMEM((4096, BLOCK), f32), pltpu.VMEM((32, 8, BLOCK), f32)],
        compiler_params=pltpu.CompilerParams(vmem_limit_bytes=VMEM_LIMIT),
        cost_estimate=pl.CostEstimate(
            flops=60_000_000, bytes_accessed=2_200_000, transcendentals=4096
        ),
        name="pair_backward",
    )(pair, gain, weight, *pieces)


def along(value, axis, step):
    size = 2 if axis in ("core", "z") else 4
    return lax.ppermute(value, axis, [(p, (p + step) % size) for p in range(size)])


def per_device(
    group, pair, mask, ln_gain, ln_shift, w_query, w_key, w_value, w_gate, gate_bias, w_bias,
    w_out, cotangent,
):
    gain, shift = ln_gain.reshape(1, BLOCK), ln_shift.reshape(1, BLOCK)
    half = 2 * group.shape[0]
    *sent, coef = front_call(
        group, cotangent, pair, gain, shift, w_query, w_key, w_value, w_gate,
        gate_bias.reshape(1, BLOCK), w_out, w_bias,
    )
    pieces = [sent[0]] + [along(sent[d], "y", d) for d in range(1, 4)]
    own = jnp.stack([p[2 * half] for p in pieces])
    gathered = [own] + [along(own, "zh", d) for d in range(1, 4)]
    key_value = jnp.stack([p[:half] for p in pieces])
    gathered, key_value = lax.optimization_barrier((gathered, key_value))
    near = jnp.stack(gathered)
    line, kv_other = lax.optimization_barrier(
        ([near] + [along(near, "x", d) for d in range(1, 4)], along(key_value, "z", 1))
    )
    plane = jnp.stack(line)
    other = along(plane, "core", 1)

    out_own, out_other, out_q, keep, send = attention_call(
        mask.reshape(-1, BLOCK), plane, other, pieces, kv_other
    )

    first = add_core(keep, along(send, "core", 1))
    came = along(out_other, "z", 1)
    second = add_four(first[0], *(along(first[d], "x", -d) for d in range(1, 4)))
    third = [along(second[d], "zh", -d) for d in range(1, 4)]
    packed = pack_call(second[0], *third, out_own, came, out_q)
    back = [packed[0]] + [along(packed[d], "y", -d) for d in range(1, 4)]

    grad_group = group_call(group, gain, w_query, w_key, w_value, w_gate, coef, back)
    grad_pair = pair_call(pair, gain, w_bias, back)
    return (grad_group, grad_pair)


def solution(mesh):
    fine = jax.sharding.Mesh(mesh.devices.reshape(4, 4, 2, 2, 4), ("x", "zh", "core", "z", "y"))
    row, col = ("x", "zh", "core"), ("z", "y")
    placed = (
        P(row, col, None),
        P(col, row, None),
        P(), P(), P(), P(), P(), P(), P(), P(), P(), P(),
        P(row, col, None),
    )
    return jax.shard_map(
        per_device,
        mesh=fine,
        in_specs=placed,
        out_specs=(P(row, col, None), P(col, row, None)),
        check_vma=False,
    )
```

time: 140 us -> 111 us (0.79)
  blocking collectives: 33.8 us -> 0 us
  starting transfers between devices: 26.4 us -> 35.7 us
  Pallas kernels: 31.9 us -> 26.8 us
  local copies, waits for them, and re-layouts: 5.24 us -> 7.62 us
  waiting for transfers between devices: 40.8 us -> 38.7 us
    all_to_all x5 -> x0, waiting for transfers between devices: 40.8 us -> none  [exchange(): return lax.all_to_all(value, axes, split_axis=0, concat_axis=0, tiled=True)]
    ppermute x2 -> x22, waiting for transfers between devices: 0.01 us -> 38.7 us  [along(): lax.ppermute(value, axis, [(p, (p + step) % size) for p in range(size)])]
    ppermute x2 -> x22, starting transfers between devices: 0.01 us -> 35.7 us  [along(): lax.ppermute(value, axis, [(p, (p + step) % size) for p in range(size)])]
    all_to_all x3 -> x0, blocking collectives: 33.8 us -> none  [exchange(): return lax.all_to_all(value, axes, split_axis=0, concat_axis=0, tiled=True)]
    all_to_all x5 -> x0, starting transfers between devices: 26.4 us -> none  [exchange(): return lax.all_to_all(value, axes, split_axis=0, concat_axis=0, tiled=True)]
    pallas_call x5, Pallas kernels: 22.4 us -> 19.8 us  [the longest x1 15.4 us: attention_call(): pl.pallas_call(attention_kernel, out_shape=(part, part, part, jax.ShapeDt...]
    unnamed x31 -> x35, local copies, waits for them, and re-layouts: 5.15 us -> 7.59 us
    pallas_call x1, Pallas kernels: 7.62 us -> 5.27 us  [pair_call(): pl.pallas_call(pair_kernel, out_shape=jax.ShapeDtypeStruct(pair.shape, bf...]
  transfers between devices with their start and end apart: 7 -> 22, of which waited for: 5 -> 16; matrix products, arithmetic and copies ran while one was open for 0% -> 0% of each run, Pallas kernels for 3% -> 0%
where the time goes in v2:
time: 111 us; the launch traced here: 110 us
  waiting for transfers between devices  38.7 us (35%)
  starting transfers between devices  35.7 us (32%)
  Pallas kernels  26.8 us (24%)
  local copies, waits for them, and re-layouts  7.62 us (7%)
    ppermute x22, waiting for transfers between devices, along(): lax.ppermute(value, axis, [(p, (p + step) % size) for p in range(size)])  38.7 us
    ppermute x22, starting transfers between devices, along(): lax.ppermute(value, axis, [(p, (p + step) % size) for p in range(size)])  35.7 us
    pallas_call x1, Pallas kernels, attention_call(): pl.pallas_call(attention_kernel, out_shape=(part, part, part, jax.ShapeDt...  15.4 us
    unnamed x35, local copies, waits for them, and re-layouts  7.59 us
    pallas_call x1, Pallas kernels, pair_call(): pl.pallas_call(pair_kernel, out_shape=jax.ShapeDtypeStruct(pair.shape, bf...  5.27 us
    pallas_call x1, Pallas kernels, front_call(): pl.pallas_call(front_kernel, out_shape=(sent,) * 4 + (jax.ShapeDtypeStruc...  4.08 us
  transfers between devices with their start and end apart: 22, of which 16 were waited for; matrix products, arithmetic and copies ran while one was open for 0% of the time, Pallas kernels for 0%

profile of v2, /device:TPU:32, one launch (start us, length us, event | category | flops | bytes accessed | tf_op | source)
XLA Modules:
  0.0 109.8 jit_solution(16280014494563893383)
XLA Ops:
  8.2 4.1 %front.1 = (bf16[21,32,128]{2,1,0:T(8,128)(2,1)S(1)}, bf16[21,32,128]{2,1,0:T(8,128)(2,1)S(1)}, bf16[21,32,128]{2,1,0:T(8,128)(2,1)S(1)}, bf16[21,32,128]{2,1,0:T(8,128)(2,1)S(1)}, f32[5,128,128]{2,1,0:T(8,128)S(1)}) custom-call(bf16[5,128,128]{2,1,0:T(8,128)(2,1)S(1)} %copy-done.2, bf16[5,128,128]{2,1,0:T(8,128)(2,1)S(1)} %copy-done.4, ...), custom_call_target="tpu_custom_call" | custom-call | flops 130000000 | bytes 3000000 | tf_op jit(solution)/shard_map/front/pallas_call | solution.py:81
  14.0 2.9 %collective-permute-start.1 = (bf16[21,32,128]{2,1,0:T(8,128)(2,1)S(1)}, bf16[21,32,128]{2,1,0:T(8,128)(2,1)S(1)}, u32[]{:S(2)}, u32[]{:S(2)}) collective-permute-start(bf16[21,32,128]{2,1,0:T(8,128)(2,1)S(1)} %get-tuple-element.37), channel_id=1, source_target_pairs={{0,2},{1,3},{2,0},{3,1},{4,6},{5,7},{6,4},{7,5},{8,10},{9,11},{10,... | collective-permute-start | bytes 516104 | tf_op jit(solution)/shard_map/ppermute | solution.py:363
  19.8 4.9 %collective-permute-done.1.s2 = bf16[21,32,128]{2,1,0:T(8,128)(2,1)S(1)} collective-permute-done((bf16[21,32,128]{2,1,0:T(8,128)(2,1)S(1)}, bf16[21,32,128]{2,1,0:T(8,128)(2,1)S(1)}, u32[]{:S(2)}, u32[]{:S(2)}) %collective-permute-start.1) | collective-permute-done | bytes 172064 | tf_op jit(solution)/shard_map/ppermute | solution.py:363
  24.7 5.5 %collective-permute-start.5 = (bf16[4,32,128]{2,1,0:T(8,128)(2,1)S(1)}, bf16[4,32,128]{2,1,0:T(8,128)(2,1)S(1)}, u32[]{:S(2)}, u32[]{:S(2)}) collective-permute-start(bf16[4,32,128]{2,1,0:T(8,128)(2,1)S(1)} %pad_maximum_fusion.3), channel_id=1, source_target_pairs={{0,48},{16,0},{32,16},{48,32},{1,49},{17,1},{33,17},{49,33},{2,50}... | collective-permute-start | bytes 98312 | tf_op jit(solution)/shard_map/ppermute | solution.py:363
  31.6 2.4 %collective-permute-start.3 = (bf16[4,32,128]{2,1,0:T(8,128)(2,1)S(1)}, bf16[4,32,128]{2,1,0:T(8,128)(2,1)S(1)}, u32[]{:S(2)}, u32[]{:S(2)}) collective-permute-start(bf16[4,32,128]{2,1,0:T(8,128)(2,1)S(1)} %pad_maximum_fusion.3), channel_id=1, source_target_pairs={{0,16},{16,32},{32,48},{48,0},{1,17},{17,33},{33,49},{49,1},{2,18}... | collective-permute-start | bytes 98312 | tf_op jit(solution)/shard_map/ppermute | solution.py:363
  34.0 3.9 %collective-permute-done.4 = bf16[4,32,128]{2,1,0:T(8,128)(2,1)S(1)} collective-permute-done((bf16[4,32,128]{2,1,0:T(8,128)(2,1)S(1)}, bf16[4,32,128]{2,1,0:T(8,128)(2,1)S(1)}, u32[]{:S(2)}, u32[]{:S(2)}) %collective-permute-start.4) | collective-permute-done | bytes 32800 | tf_op jit(solution)/shard_map/ppermute | solution.py:363
  39.0 2.8 %collective-permute-start.8 = (bf16[4,4,32,128]{3,2,1,0:T(8,128)(2,1)S(1)}, bf16[4,4,32,128]{3,2,1,0:T(8,128)(2,1)S(1)}, u32[]{:S(2)}, u32[]{:S(2)}) collective-permute-start(bf16[4,4,32,128]{3,2,1,0:T(8,128)(2,1)S(1)} %pad_maximum_fusion.2), channel_id=1, source_target_pairs={{0,192},{64,0},{128,64},{192,128},{1,193},{65,1},{129,65},{193,129... | collective-permute-start | bytes 393224 | tf_op jit(solution)/shard_map/ppermute | solution.py:363
  43.5 2.2 %collective-permute-done.8 = bf16[4,4,32,128]{3,2,1,0:T(8,128)(2,1)S(1)} collective-permute-done((bf16[4,4,32,128]{3,2,1,0:T(8,128)(2,1)S(1)}, bf16[4,4,32,128]{3,2,1,0:T(8,128)(2,1)S(1)}, u32[]{:S(2)}, u32[]{:S(2)}) %collective-permute-start.8) | collective-permute-done | bytes 131104 | tf_op jit(solution)/shard_map/ppermute | solution.py:363
  45.7 2.6 %collective-permute-done.7 = bf16[4,4,32,128]{3,2,1,0:T(8,128)(2,1)S(1)} collective-permute-done((bf16[4,4,32,128]{3,2,1,0:T(8,128)(2,1)S(1)}, bf16[4,4,32,128]{3,2,1,0:T(8,128)(2,1)S(1)}, u32[]{:S(2)}, u32[]{:S(2)}) %collective-permute-start.7) | collective-permute-done | bytes 131104 | tf_op jit(solution)/shard_map/ppermute | solution.py:363
  50.1 1.9 %collective-permute-done.10.bias_other = bf16[4,4,4,32,128]{4,3,2,1,0:T(8,128)(2,1)S(1)} collective-permute-done((bf16[4,4,4,32,128]{4,3,2,1,0:T(8,128)(2,1)S(1)}, bf16[4,4,4,32,128]{4,3,2,1,0:T(8,128)(2,1)S(1)}, u32[]{:S(2)}, u32[]{:S(2)}) %collective-permute-start.10) | collective-permute-done | bytes 524320 | tf_op jit(solution)/shard_map/ppermute | solution.py:363
  52.0 15.4 %attention.1 = (bf16[4,10,32,128]{3,2,1,0:T(8,128)(2,1)S(1)}, bf16[4,10,32,128]{3,2,1,0:T(8,128)(2,1)S(1)}, bf16[4,10,32,128]{3,2,1,0:T(8,128)(2,1)S(1)}, f32[4,...) custom-call(s32[8,128]{1,0:T(8,128)S(1)} %bitcast.25, ...), custom_call_target="tpu_custom_call" | custom-call | flops 8000000000 | bytes 6000000 | tf_op jit(solution)/shard_map/attention/pallas_call | solution.py:188
  71.8 4.1 %collective-permute-done.12.c1 = bf16[4,4,32,128]{3,2,1,0:T(8,128)(2,1)S(1)} collective-permute-done((bf16[4,4,32,128]{3,2,1,0:T(8,128)(2,1)S(1)}, bf16[4,4,32,128]{3,2,1,0:T(8,128)(2,1)S(1)}, u32[]{:S(2)}, u32[]{:S(2)}) %collective-permute-start.12) | collective-permute-done | bytes 131104 | tf_op jit(solution)/shard_map/ppermute | solution.py:363
  75.9 2.0 %collective-permute-done.13.c2 = bf16[4,4,32,128]{3,2,1,0:T(8,128)(2,1)S(1)} collective-permute-done((bf16[4,4,32,128]{3,2,1,0:T(8,128)(2,1)S(1)}, bf16[4,4,32,128]{3,2,1,0:T(8,128)(2,1)S(1)}, u32[]{:S(2)}, u32[]{:S(2)}) %collective-permute-start.13) | collective-permute-done | bytes 131104 | tf_op jit(solution)/shard_map/ppermute | solution.py:363
  78.0 1.7 %collective-permute-done.14.c3 = bf16[4,4,32,128]{3,2,1,0:T(8,128)(2,1)S(1)} collective-permute-done((bf16[4,4,32,128]{3,2,1,0:T(8,128)(2,1)S(1)}, bf16[4,4,32,128]{3,2,1,0:T(8,128)(2,1)S(1)}, u32[]{:S(2)}, u32[]{:S(2)}) %collective-permute-start.14) | collective-permute-done | bytes 131104 | tf_op jit(solution)/shard_map/ppermute | solution.py:363
  79.8 2.3 %collective-permute-start.15 = (bf16[4,32,128]{2,1,0:T(8,128)(2,1)S(1)}, bf16[4,32,128]{2,1,0:T(8,128)(2,1)S(1)}, u32[]{:S(2)}, u32[]{:S(2)}) collective-permute-start(bf16[4,32,128]{2,1,0:T(8,128)(2,1)S(1)} %get-tuple-element.56), channel_id=1, source_target_pairs={{0,48},{16,0},{32,16},{48,32},{1,49},{17,1},{33,17},{49,33},{2,50}... | collective-permute-start | bytes 98312 | tf_op jit(solution)/shard_map/ppermute | solution.py:363
  82.1 2.2 %collective-permute-start.16 = (bf16[4,32,128]{2,1,0:T(8,128)(2,1)S(1)}, bf16[4,32,128]{2,1,0:T(8,128)(2,1)S(1)}, u32[]{:S(2)}, u32[]{:S(2)}) collective-permute-start(bf16[4,32,128]{2,1,0:T(8,128)(2,1)S(1)} %get-tuple-element.57), channel_id=1, source_target_pairs={{0,32},{16,48},{32,0},{48,16},{1,33},{17,49},{33,1},{49,17},{2,34}... | collective-permute-start | bytes 98312 | tf_op jit(solution)/shard_map/ppermute | solution.py:363
  84.3 2.7 %collective-permute-start.17 = (bf16[4,32,128]{2,1,0:T(8,128)(2,1)S(1)}, bf16[4,32,128]{2,1,0:T(8,128)(2,1)S(1)}, u32[]{:S(2)}, u32[]{:S(2)}) collective-permute-start(bf16[4,32,128]{2,1,0:T(8,128)(2,1)S(1)} %get-tuple-element.58), channel_id=1, source_target_pairs={{0,16},{16,32},{32,48},{48,0},{1,17},{17,33},{33,49},{49,1},{2,18}... | collective-permute-start | bytes 98312 | tf_op jit(solution)/shard_map/ppermute | solution.py:363
  86.9 3.3 %collective-permute-done.16.c2 = bf16[4,32,128]{2,1,0:T(8,128)(2,1)S(1)} collective-permute-done((bf16[4,32,128]{2,1,0:T(8,128)(2,1)S(1)}, bf16[4,32,128]{2,1,0:T(8,128)(2,1)S(1)}, u32[]{:S(2)}, u32[]{:S(2)}) %collective-permute-start.16) | collective-permute-done | bytes 32800 | tf_op jit(solution)/shard_map/ppermute | solution.py:363
  90.6 2.0 %collective-permute-start.19 = (bf16[21,32,128]{2,1,0:T(8,128)(2,1)S(1)}, bf16[21,32,128]{2,1,0:T(8,128)(2,1)S(1)}, u32[]{:S(2)}, u32[]{:S(2)}) collective-permute-start(bf16[21,32,128]{2,1,0:T(8,128)(2,1)S(1)} %get-tuple-element.63), channel_id=1, source_target_pairs={{0,3},{1,0},{2,1},{3,2},{4,7},{5,4},{6,5},{7,6},{8,11},{9,8},{10,9... | collective-permute-start | bytes 516104 | tf_op jit(solution)/shard_map/ppermute | solution.py:363
  94.6 4.5 %collective-permute-done.19.t1 = bf16[21,32,128]{2,1,0:T(8,128)(2,1)S(1)} collective-permute-done((bf16[21,32,128]{2,1,0:T(8,128)(2,1)S(1)}, bf16[21,32,128]{2,1,0:T(8,128)(2,1)S(1)}, u32[]{:S(2)}, u32[]{:S(2)}) %collective-permute-start.19) | collective-permute-done | bytes 172064 | tf_op jit(solution)/shard_map/ppermute | solution.py:363
  99.1 1.9 %collective-permute-done.20.t2 = bf16[21,32,128]{2,1,0:T(8,128)(2,1)S(1)} collective-permute-done((bf16[21,32,128]{2,1,0:T(8,128)(2,1)S(1)}, bf16[21,32,128]{2,1,0:T(8,128)(2,1)S(1)}, u32[]{:S(2)}, u32[]{:S(2)}) %collective-permute-start.20) | collective-permute-done | bytes 172064 | tf_op jit(solution)/shard_map/ppermute | solution.py:363
  100.9 1.8 %collective-permute-done.21.t3 = bf16[21,32,128]{2,1,0:T(8,128)(2,1)S(1)} collective-permute-done((bf16[21,32,128]{2,1,0:T(8,128)(2,1)S(1)}, bf16[21,32,128]{2,1,0:T(8,128)(2,1)S(1)}, u32[]{:S(2)}, u32[]{:S(2)}) %collective-permute-start.21) | collective-permute-done | bytes 172064 | tf_op jit(solution)/shard_map/ppermute | solution.py:363
  102.8 5.3 %pair_backward.1 = bf16[128,32,128]{2,1,0:T(8,128)(2,1)} custom-call(bf16[128,32,128]{2,1,0:T(8,128)(2,1)S(1)} %copy-done.1, f32[1,128]{1,0:T(1,128)S(1)} %bitcast.21, bf16[128,4]{1,0:T(8,128)(2,1)S(1)} %copy.15.wb_ref.weight_ref, bf16[21,32,128]{2,1,0:T(8,128)(2,1)S(1)} %get-tuple-element.62.t0, bf16[21,32,128]{2,1,0:T(8,128)(2,1)S(1)} %collective-permute-done.19.t1, ...), custom_call_target="tpu_custom_call" | custom-call | flops 60000000 | bytes 2200000 | tf_op jit(solution)/shard_map/pair_backward/pallas_call | solution.py:349
  108.0 1.7 %group_backward.1 = bf16[5,128,128]{2,1,0:T(8,128)(2,1)} custom-call(bf16[5,128,128]{2,1,0:T(8,128)(2,1)S(1)} %copy-done.3, f32[1,128]{1,0:T(1,128)S(1)} %bitcast.22, bf16[128,128]{1,0:T(8,128)(2,1)S(1)} %copy-done.5, bf16[128,128]{1,0:T(8,128)(2,1)S(1)} %copy-done.7, bf16[128,128]{1,0:T(8,128)(2,1)S(1)} %copy-done.9, bf16[128,128]{1,0:T(8,128)(2,1)S(1)} %copy-done.11, ...), custom_call_target="tpu_custom_call" | custom-call | flops 160000000 | bytes 2000000 | tf_op jit(solution)/shard_map/group_backward/pallas_call | solution.py:300
  (74 shorter events, 24.8 us)
Async XLA Ops:
  12.3 7.5 %collective-permute-start = (bf16[21,32,128]{2,1,0:T(8,128)(2,1)S(1)}, bf16[21,32,128]{2,1,0:T(8,128)(2,1)S(1)}, u32[]{:S(2)}, u32[]{:S(2)}) collective-permute-start(bf16[21,32,128]{2,1,0:T(8,128)(2,1)S(1)} %get-tuple-element.36), channel_id=1, source_target_pairs={{0,1},{1,2},{2,3},{3,0},{4,5},{5,6},{6,7},{7,4},{8,9},{9,10},{10,1... | collective-permute-start | bytes 516104 | tf_op jit(solution)/shard_map/ppermute | solution.py:363
  14.0 10.7 %collective-permute-start.1 = (bf16[21,32,128]{2,1,0:T(8,128)(2,1)S(1)}, bf16[21,32,128]{2,1,0:T(8,128)(2,1)S(1)}, u32[]{:S(2)}, u32[]{:S(2)}) collective-permute-start(bf16[21,32,128]{2,1,0:T(8,128)(2,1)S(1)} %get-tuple-element.37), channel_id=1, source_target_pairs={{0,2},{1,3},{2,0},{3,1},{4,6},{5,7},{6,4},{7,5},{8,10},{9,11},{10,... | collective-permute-start | bytes 516104 | tf_op jit(solution)/shard_map/ppermute | solution.py:363
  16.9 7.8 %collective-permute-start.2 = (bf16[21,32,128]{2,1,0:T(8,128)(2,1)S(1)}, bf16[21,32,128]{2,1,0:T(8,128)(2,1)S(1)}, u32[]{:S(2)}, u32[]{:S(2)}) collective-permute-start(bf16[21,32,128]{2,1,0:T(8,128)(2,1)S(1)} %get-tuple-element.38), channel_id=1, source_target_pairs={{0,3},{1,0},{2,1},{3,2},{4,7},{5,4},{6,5},{7,6},{8,11},{9,8},{10,9... | collective-permute-start | bytes 516104 | tf_op jit(solution)/shard_map/ppermute | solution.py:363
  24.7 9.4 %collective-permute-start.5 = (bf16[4,32,128]{2,1,0:T(8,128)(2,1)S(1)}, bf16[4,32,128]{2,1,0:T(8,128)(2,1)S(1)}, u32[]{:S(2)}, u32[]{:S(2)}) collective-permute-start(bf16[4,32,128]{2,1,0:T(8,128)(2,1)S(1)} %pad_maximum_fusion.3), channel_id=1, source_target_pairs={{0,48},{16,0},{32,16},{48,32},{1,49},{17,1},{33,17},{49,33},{2,50}... | collective-permute-start | bytes 98312 | tf_op jit(solution)/shard_map/ppermute | solution.py:363
  30.1 7.8 %collective-permute-start.4 = (bf16[4,32,128]{2,1,0:T(8,128)(2,1)S(1)}, bf16[4,32,128]{2,1,0:T(8,128)(2,1)S(1)}, u32[]{:S(2)}, u32[]{:S(2)}) collective-permute-start(bf16[4,32,128]{2,1,0:T(8,128)(2,1)S(1)} %pad_maximum_fusion.3), channel_id=1, source_target_pairs={{0,32},{16,48},{32,0},{48,16},{1,33},{17,49},{33,1},{49,17},{2,34}... | collective-permute-start | bytes 98312 | tf_op jit(solution)/shard_map/ppermute | solution.py:363
  31.6 6.4 %collective-permute-start.3 = (bf16[4,32,128]{2,1,0:T(8,128)(2,1)S(1)}, bf16[4,32,128]{2,1,0:T(8,128)(2,1)S(1)}, u32[]{:S(2)}, u32[]{:S(2)}) collective-permute-start(bf16[4,32,128]{2,1,0:T(8,128)(2,1)S(1)} %pad_maximum_fusion.3), channel_id=1, source_target_pairs={{0,16},{16,32},{32,48},{48,0},{1,17},{17,33},{33,49},{49,1},{2,18}... | collective-permute-start | bytes 98312 | tf_op jit(solution)/shard_map/ppermute | solution.py:363
  38.0 11.7 %collective-permute-start.9 = (bf16[4,10,32,128]{3,2,1,0:T(8,128)(2,1)S(1)}, bf16[4,10,32,128]{3,2,1,0:T(8,128)(2,1)S(1)}, u32[]{:S(2)}, u32[]{:S(2)}) collective-permute-start(bf16[4,10,32,128]{3,2,1,0:T(8,128)(2,1)S(1)} %pad_maximum_fusion.1), channel_id=1, source_target_pairs={{0,4},{4,0},{1,5},{5,1},{2,6},{6,2},{3,7},{7,3},{8,12},{12,8},{9,1... | collective-permute-start | bytes 983048 | tf_op jit(solution)/shard_map/ppermute | solution.py:363
  39.0 6.8 %collective-permute-start.8 = (bf16[4,4,32,128]{3,2,1,0:T(8,128)(2,1)S(1)}, bf16[4,4,32,128]{3,2,1,0:T(8,128)(2,1)S(1)}, u32[]{:S(2)}, u32[]{:S(2)}) collective-permute-start(bf16[4,4,32,128]{3,2,1,0:T(8,128)(2,1)S(1)} %pad_maximum_fusion.2), channel_id=1, source_target_pairs={{0,192},{64,0},{128,64},{192,128},{1,193},{65,1},{129,65},{193,129... | collective-permute-start | bytes 393224 | tf_op jit(solution)/shard_map/ppermute | solution.py:363
  41.8 6.6 %collective-permute-start.7 = (bf16[4,4,32,128]{3,2,1,0:T(8,128)(2,1)S(1)}, bf16[4,4,32,128]{3,2,1,0:T(8,128)(2,1)S(1)}, u32[]{:S(2)}, u32[]{:S(2)}) collective-permute-start(bf16[4,4,32,128]{3,2,1,0:T(8,128)(2,1)S(1)} %pad_maximum_fusion.2), channel_id=1, source_target_pairs={{0,128},{64,192},{128,0},{192,64},{1,129},{65,193},{129,1},{193,65... | collective-permute-start | bytes 393224 | tf_op jit(solution)/shard_map/ppermute | solution.py:363
  42.6 7.1 %collective-permute-start.6 = (bf16[4,4,32,128]{3,2,1,0:T(8,128)(2,1)S(1)}, bf16[4,4,32,128]{3,2,1,0:T(8,128)(2,1)S(1)}, u32[]{:S(2)}, u32[]{:S(2)}) collective-permute-start(bf16[4,4,32,128]{3,2,1,0:T(8,128)(2,1)S(1)} %pad_maximum_fusion.2), channel_id=1, source_target_pairs={{0,64},{64,128},{128,192},{192,0},{1,65},{65,129},{129,193},{193,1... | collective-permute-start | bytes 393224 | tf_op jit(solution)/shard_map/ppermute | solution.py:363
  49.8 2.2 %collective-permute-start.10 = (bf16[4,4,4,32,128]{4,3,2,1,0:T(8,128)(2,1)S(1)}, bf16[4,4,4,32,128]{4,3,2,1,0:T(8,128)(2,1)S(1)}, u32[]{:S(2)}, u32[]{:S(2)}) collective-permute-start(bf16[4,4,4,32,128]{4,3,2,1,0:T(8,128)(2,1)S(1)} %pad_maximum_fusion.bias_own), channel_id=1, source_target_pairs={{0,8},{8,0},{1,9},{9,1},{2,10},{10,2},{3,11},{11,3},{4,12},{12,4},... | collective-permute-start | bytes 1572872 | tf_op jit(solution)/shard_map/ppermute | solution.py:363
  67.4 2.0 %collective-permute-start.11 = (bf16[4,4,4,32,128]{4,3,2,1,0:T(8,128)(2,1)S(1)}, bf16[4,4,4,32,128]{4,3,2,1,0:T(8,128)(2,1)S(1)}, u32[]{:S(2)}, u32[]{:S(2)}) collective-permute-start(bf16[4,4,4,32,128]{4,3,2,1,0:T(8,128)(2,1)S(1)} %get-tuple-element.50), channel_id=1, source_target_pairs={{0,8},{8,0},{1,9},{9,1},{2,10},{10,2},{3,11},{11,3},{4,12},{12,4},... | collective-permute-start | bytes 1572872 | tf_op jit(solution)/shard_map/ppermute | solution.py:363
  67.6 19.3 %collective-permute-start.18 = (bf16[4,10,32,128]{3,2,1,0:T(8,128)(2,1)S(1)}, bf16[4,10,32,128]{3,2,1,0:T(8,128)(2,1)S(1)}, u32[]{:S(2)}, u32[]{:S(2)}) collective-permute-start(bf16[4,10,32,128]{3,2,1,0:T(8,128)(2,1)S(1)} %get-tuple-element.60), channel_id=1, source_target_pairs={{0,4},{4,0},{1,5},{5,1},{2,6},{6,2},{3,7},{7,3},{8,12},{12,8},{9,1... | collective-permute-start | bytes 983048 | tf_op jit(solution)/shard_map/ppermute | solution.py:363
  69.5 33.2 %copy-start.1 = (bf16[128,32,128]{2,1,0:T(8,128)(2,1)S(1)}, bf16[128,32,128]{2,1,0:T(8,128)(2,1)}, u32[]{:S(2)}) copy-start(bf16[128,32,128]{2,1,0:T(8,128)(2,1)} %pair_ref.3) | copy-start | bytes 3145732
  69.5 6.4 %collective-permute-start.12 = (bf16[4,4,32,128]{3,2,1,0:T(8,128)(2,1)S(1)}, bf16[4,4,32,128]{3,2,1,0:T(8,128)(2,1)S(1)}, u32[]{:S(2)}, u32[]{:S(2)}) collective-permute-start(bf16[4,4,32,128]{3,2,1,0:T(8,128)(2,1)S(1)} %get-tuple-element.52), channel_id=1, source_target_pairs={{0,192},{64,0},{128,64},{192,128},{1,193},{65,1},{129,65},{193,129... | collective-permute-start | bytes 393224 | tf_op jit(solution)/shard_map/ppermute | solution.py:363
  70.2 7.8 %collective-permute-start.13 = (bf16[4,4,32,128]{3,2,1,0:T(8,128)(2,1)S(1)}, bf16[4,4,32,128]{3,2,1,0:T(8,128)(2,1)S(1)}, u32[]{:S(2)}, u32[]{:S(2)}) collective-permute-start(bf16[4,4,32,128]{3,2,1,0:T(8,128)(2,1)S(1)} %get-tuple-element.53), channel_id=1, source_target_pairs={{0,128},{64,192},{128,0},{192,64},{1,129},{65,193},{129,1},{193,65... | collective-permute-start | bytes 393224 | tf_op jit(solution)/shard_map/ppermute | solution.py:363
  71.0 8.8 %collective-permute-start.14 = (bf16[4,4,32,128]{3,2,1,0:T(8,128)(2,1)S(1)}, bf16[4,4,32,128]{3,2,1,0:T(8,128)(2,1)S(1)}, u32[]{:S(2)}, u32[]{:S(2)}) collective-permute-start(bf16[4,4,32,128]{3,2,1,0:T(8,128)(2,1)S(1)} %get-tuple-element.54), channel_id=1, source_target_pairs={{0,64},{64,128},{128,192},{192,0},{1,65},{65,129},{129,193},{193,1... | collective-permute-start | bytes 393224 | tf_op jit(solution)/shard_map/ppermute | solution.py:363
  79.8 7.1 %collective-permute-start.15 = (bf16[4,32,128]{2,1,0:T(8,128)(2,1)S(1)}, bf16[4,32,128]{2,1,0:T(8,128)(2,1)S(1)}, u32[]{:S(2)}, u32[]{:S(2)}) collective-permute-start(bf16[4,32,128]{2,1,0:T(8,128)(2,1)S(1)} %get-tuple-element.56), channel_id=1, source_target_pairs={{0,48},{16,0},{32,16},{48,32},{1,49},{17,1},{33,17},{49,33},{2,50}... | collective-permute-start | bytes 98312 | tf_op jit(solution)/shard_map/ppermute | solution.py:363
  82.1 8.2 %collective-permute-start.16 = (bf16[4,32,128]{2,1,0:T(8,128)(2,1)S(1)}, bf16[4,32,128]{2,1,0:T(8,128)(2,1)S(1)}, u32[]{:S(2)}, u32[]{:S(2)}) collective-permute-start(bf16[4,32,128]{2,1,0:T(8,128)(2,1)S(1)} %get-tuple-element.57), channel_id=1, source_target_pairs={{0,32},{16,48},{32,0},{48,16},{1,33},{17,49},{33,1},{49,17},{2,34}... | collective-permute-start | bytes 98312 | tf_op jit(solution)/shard_map/ppermute | solution.py:363
  84.3 6.2 %collective-permute-start.17 = (bf16[4,32,128]{2,1,0:T(8,128)(2,1)S(1)}, bf16[4,32,128]{2,1,0:T(8,128)(2,1)S(1)}, u32[]{:S(2)}, u32[]{:S(2)}) collective-permute-start(bf16[4,32,128]{2,1,0:T(8,128)(2,1)S(1)} %get-tuple-element.58), channel_id=1, source_target_pairs={{0,16},{16,32},{32,48},{48,0},{1,17},{17,33},{33,49},{49,1},{2,18}... | collective-permute-start | bytes 98312 | tf_op jit(solution)/shard_map/ppermute | solution.py:363
  90.6 8.5 %collective-permute-start.19 = (bf16[21,32,128]{2,1,0:T(8,128)(2,1)S(1)}, bf16[21,32,128]{2,1,0:T(8,128)(2,1)S(1)}, u32[]{:S(2)}, u32[]{:S(2)}) collective-permute-start(bf16[21,32,128]{2,1,0:T(8,128)(2,1)S(1)} %get-tuple-element.63), channel_id=1, source_target_pairs={{0,3},{1,0},{2,1},{3,2},{4,7},{5,4},{6,5},{7,6},{8,11},{9,8},{10,9... | collective-permute-start | bytes 516104 | tf_op jit(solution)/shard_map/ppermute | solution.py:363
  92.6 8.3 %collective-permute-start.20 = (bf16[21,32,128]{2,1,0:T(8,128)(2,1)S(1)}, bf16[21,32,128]{2,1,0:T(8,128)(2,1)S(1)}, u32[]{:S(2)}, u32[]{:S(2)}) collective-permute-start(bf16[21,32,128]{2,1,0:T(8,128)(2,1)S(1)} %get-tuple-element.64), channel_id=1, source_target_pairs={{0,2},{1,3},{2,0},{3,1},{4,6},{5,7},{6,4},{7,5},{8,10},{9,11},{10,... | collective-permute-start | bytes 516104 | tf_op jit(solution)/shard_map/ppermute | solution.py:363
  93.8 9.0 %collective-permute-start.21 = (bf16[21,32,128]{2,1,0:T(8,128)(2,1)S(1)}, bf16[21,32,128]{2,1,0:T(8,128)(2,1)S(1)}, u32[]{:S(2)}, u32[]{:S(2)}) collective-permute-start(bf16[21,32,128]{2,1,0:T(8,128)(2,1)S(1)} %get-tuple-element.65), channel_id=1, source_target_pairs={{0,1},{1,2},{2,3},{3,0},{4,5},{5,6},{6,7},{7,4},{8,9},{9,10},{10,1... | collective-permute-start | bytes 516104 | tf_op jit(solution)/shard_map/ppermute | solution.py:363
  102.7 5.3 %copy-start.9 = (bf16[128,128]{1,0:T(8,128)(2,1)S(1)}, bf16[128,128]{1,0:T(8,128)(2,1)}, u32[]{:S(2)}) copy-start(bf16[128,128]{1,0:T(8,128)(2,1)} %wv_ref.3) | copy-start | bytes 98308
  (15 other events, 27.1 us)

commit v3 on v2

--- a/solution.py
+++ b/solution.py
@@ -17,23 +17,80 @@
 TN = (((0,), (0,)), ((), ()))
 
 
-def place():
-    return tuple(lax.axis_index(name) for name in ("x", "zh", "core", "z", "y"))
-
-
 def split_high_low(value):
     high = value.astype(bf16)
     return high, (value - high.astype(f32)).astype(bf16)
 
 
-def front_kernel(
-    group_ref, cot_ref, pair_ref, gain_ref, shift_ref, wq_ref, wk_ref, wv_ref, wg_ref, gb_ref,
-    wo_ref, wb_ref, s0, s1, s2, s3, coef, normed, heads, parts,
+def fetch(pairs, sems):
+    copies = [pltpu.make_async_copy(src, dst, sems.at[n]) for n, (src, dst) in enumerate(pairs)]
+    for copy in copies:
+        copy.start()
+    return copies
+
+
+def bias_kernel(
+    pair_hbm, gain_ref, shift_ref, weight_ref, out_ref, pair_ref, normed, heads, sems
 ):
-    _, _, _, _, y = place()
+    chunks = [pl.ds(16 * n, 16) for n in range(8)]
+    copies = fetch([(pair_hbm.at[at], pair_ref.at[at]) for at in chunks], sems)
     gain, shift = gain_ref[...], shift_ref[...]
-    turned = [w[...].astype(f32).T.astype(bf16) for w in (wq_ref, wk_ref, wv_ref, wg_ref)]
+    weight_t = jnp.concatenate(
+        [weight_ref[...].astype(f32), jnp.zeros((16 - HEADS, BLOCK), f32)], axis=0
+    ).astype(bf16)
+
+    for n, copy in enumerate(copies):
+        copy.wait()
+        x = pair_ref[16 * n : 16 * (n + 1)].astype(f32).reshape(512, BLOCK)
+        centered = x - jnp.mean(x, axis=-1, keepdims=True)
+        reciprocal = lax.rsqrt(jnp.mean(centered * centered, axis=-1, keepdims=True) + EPS)
+        low = (centered * reciprocal * gain + shift).astype(bf16).astype(f32)
+        normed[512 * n : 512 * (n + 1), :] = low
+
+    for k in range(32):
+        block = normed[pl.ds(k, BLOCK, stride=32), :].astype(bf16)
+        product = lax.dot_general(weight_t, block, NT, preferred_element_type=f32)
+        for h in range(HEADS):
+            heads[h, k : k + 1, :] = product[h : h + 1]
+    for zh in range(4):
+        out_ref[zh] = heads[...].astype(bf16)
+
+
+def bias_call(pair, gain, shift, weight):
+    vmem, hbm = pl.BlockSpec(memory_space=pltpu.VMEM), pl.BlockSpec(memory_space=pltpu.HBM)
+    return pl.pallas_call(
+        bias_kernel,
+        out_shape=jax.ShapeDtypeStruct((4, HEADS, 32, BLOCK), bf16),
+        in_specs=[hbm, vmem, vmem, vmem],
+        scratch_shapes=[
+            pltpu.VMEM(pair.shape, bf16),
+            pltpu.VMEM((4096, BLOCK), f32),
+            pltpu.VMEM((HEADS, 32, BLOCK), f32),
+            pltpu.SemaphoreType.DMA((8,)),
+        ],
+        compiler_params=pltpu.CompilerParams(vmem_limit_bytes=VMEM_LIMIT),
+        cost_estimate=pl.CostEstimate(
+            flops=20_000_000, bytes_accessed=1_200_000, transcendentals=4096
+        ),
+        name="pair_bias",
+    )(pair, gain, shift, weight)
+
+
+def project_kernel(
+    group_hbm, cot_hbm, gain_ref, shift_ref, wq_hbm, wk_hbm, wv_hbm, wg_hbm, gb_ref, wo_hbm,
+    s0, s1, s2, s3, coef, group_ref, cot_ref, square, parts, sems,
+):
+    copies = fetch(
+        [(wq_hbm, square.at[0]), (wk_hbm, square.at[1]), (wv_hbm, square.at[2]),
+         (wg_hbm, square.at[3]), (wo_hbm, square.at[4]), (group_hbm, group_ref),
+         (cot_hbm, cot_ref)], sems,
+    )
+    y = lax.axis_index("y")
+    gain, shift = gain_ref[...], shift_ref[...]
     gate_bias = jnp.broadcast_to(gb_ref[...], (BLOCK, BLOCK)).T
+    for copy in copies:
+        copy.wait()
+    turned = [square[n].astype(f32).T.astype(bf16) for n in range(4)]
     rows = group_ref.shape[0]
     for i in range(rows):
         x = group_ref[i].astype(f32)
@@ -42,64 +99,46 @@
         low = (centered * reciprocal * gain + shift).astype(bf16)
         dots = [lax.dot_general(w, low, NT, preferred_element_type=f32) for w in turned]
         gating = jax.nn.sigmoid(dots[3] + gate_bias)
-        gated = lax.dot_general(wo_ref[...], cot_ref[i], NT, preferred_element_type=f32)
+        gated = lax.dot_general(square[4], cot_ref[i], NT, preferred_element_type=f32)
         upstream = gated * gating
         coef[i] = upstream * (1.0 - gating)
         for n, value in enumerate((dots[1], dots[2], dots[0] * SCALE, upstream)):
             value = value.astype(bf16).reshape(HEADS, HEAD_DIM, BLOCK)
             for h in range(HEADS):
                 parts[h, n * rows + i] = value[h]
-
-    weight_t = jnp.concatenate(
-        [wb_ref[...].astype(f32), jnp.zeros((BLOCK, BLOCK - HEADS), f32)], axis=1
-    ).T[:16].astype(bf16)
-
-    def norm_rows(step, carry):
-        x = pair_ref[pl.ds(step * 16, 16)].astype(f32).reshape(512, BLOCK)
-        centered = x - jnp.mean(x, axis=-1, keepdims=True)
-        reciprocal = lax.rsqrt(jnp.mean(centered * centered, axis=-1, keepdims=True) + EPS)
-        low = (centered * reciprocal * gain + shift).astype(bf16).astype(f32)
-        normed[pl.ds(pl.multiple_of(step * 512, 512), 512), :] = low
-        return carry
-
-    lax.fori_loop(0, 8, norm_rows, 0)
-
-    for k in range(32):
-        block = normed[pl.ds(k, BLOCK, stride=32), :].astype(bf16)
-        product = lax.dot_general(weight_t, block, NT, preferred_element_type=f32)
-        for h in range(HEADS):
-            heads[h, k : k + 1, :] = product[h : h + 1]
-    for h in range(HEADS):
-        parts[h, 4 * rows] = heads[h].astype(bf16)
     for step, out in enumerate((s0, s1, s2, s3)):
         out[...] = parts[lax.rem(y + step, 4)]
 
 
-def front_call(group, cotangent, pair, *small):
+def project_call(group, cotangent, gain, shift, wq, wk, wv, wg, gate_bias, wo):
     rows = group.shape[0]
-    sent = jax.ShapeDtypeStruct((4 * rows + 1, HEAD_DIM, BLOCK), bf16)
-    return pl.pallas_call(
-        front_kernel,
+    sent = jax.ShapeDtypeStruct((4 * rows, HEAD_DIM, BLOCK), bf16)
+    vmem, hbm = pl.BlockSpec(memory_space=pltpu.VMEM), pl.BlockSpec(memory_space=pltpu.HBM)
+    return pl.pallas_call(
+        project_kernel,
         out_shape=(sent,) * 4 + (jax.ShapeDtypeStruct((rows, BLOCK, BLOCK), f32),),
+        in_specs=[hbm, hbm, vmem, vmem, hbm, hbm, hbm, hbm, vmem, hbm],
         scratch_shapes=[
-            pltpu.VMEM((4096, BLOCK), f32),
-            pltpu.VMEM((HEADS, 32, BLOCK), f32),
-            pltpu.VMEM((HEADS, 4 * rows + 1, HEAD_DIM, BLOCK), bf16),
+            pltpu.VMEM(group.shape, bf16),
+            pltpu.VMEM(group.shape, bf16),
+            pltpu.VMEM((5, BLOCK, BLOCK), bf16),
+            pltpu.VMEM((HEADS, 4 * rows, HEAD_DIM, BLOCK), bf16),
+            pltpu.SemaphoreType.DMA((7,)),
         ],
         compiler_params=pltpu.CompilerParams(vmem_limit_bytes=VMEM_LIMIT),
         cost_estimate=pl.CostEstimate(
-            flops=130_000_000, bytes_accessed=3_000_000, transcendentals=100_000
-        ),
-        name="front",
-    )(group, cotangent, pair, *small)
+            flops=110_000_000, bytes_accessed=2_000_000, transcendentals=100_000
+        ),
+        name="project",
+    )(group, cotangent, gain, shift, wq, wk, wv, wg, gate_bias, wo)
 
 
 def attention_kernel(
     mask_ref, bias_own, bias_other, s0, s1, s2, s3, kv_other,
     out_own, out_other, out_q, keep, send,
-    bias, grad, key_t, value_t, key_s, value_s, query_t, up_t, key_out,
+    bias, grad, key_t, value_t, key_s, value_s, query_t, up_t, key_out, query_out,
 ):
-    x, zh, core, z, y = place()
+    x, core, z, y = (lax.axis_index(name) for name in ("x", "core", "z", "y"))
     keys, queries = bias.shape
     rows = key_t.shape[0]
 
@@ -108,13 +147,13 @@
         bias[blk * BLOCK : (blk + 1) * BLOCK, :] = jnp.concatenate([live] * (queries // BLOCK), 1)
     for source, c in ((bias_own, core), (bias_other, 1 - core)):
         for dx in range(4):
-            for dz in range(4):
-                r = lax.rem(x - dx + 4, 4) * 8 + lax.rem(zh - dz + 4, 4) * 2 + c
+            for zh in range(4):
+                r = lax.rem(x - dx + 4, 4) * 8 + zh * 2 + c
                 at = pl.ds(pl.multiple_of(r * 32, 32), 32)
-                for dy in range(4):
-                    lanes = slice(dy * BLOCK, (dy + 1) * BLOCK)
+                for n in range(4):
+                    lanes = slice(n * BLOCK, (n + 1) * BLOCK)
                     bias[at, lanes] = jnp.where(
-                        bias[at, lanes] > 0.0, source[dx, dz, dy].astype(f32), -jnp.inf
+                        bias[at, lanes] > 0.0, source[dx, zh, n].astype(f32), -jnp.inf
                     )
     grad[...] = jnp.zeros_like(grad)
 
@@ -128,9 +167,10 @@
                 value_t[i, :, at] = v
                 key_s[i, at, :] = k.astype(f32).T.astype(bf16)
                 value_s[i, at, :] = v.astype(f32).T.astype(bf16)
+        at = pl.ds(pl.multiple_of(yy * BLOCK, BLOCK), BLOCK)
         for i in range(rows):
-            query_t[i, :, step * BLOCK : (step + 1) * BLOCK] = own[2 * rows + i]
-            up_t[i, :, step * BLOCK : (step + 1) * BLOCK] = own[3 * rows + i]
+            query_t[i, :, at] = own[2 * rows + i]
+            up_t[i, :, at] = own[3 * rows + i]
 
     width = 256
 
@@ -153,10 +193,8 @@
             grad_query = jnp.dot(key_t[i], scores_low, preferred_element_type=f32) * SCALE
             grad_key += lax.dot_general(scores_low, q, NT, preferred_element_type=f32)
             grad_value += lax.dot_general(low, g, NT, preferred_element_type=f32)
-            for n in range(width // BLOCK):
-                block, at = part * (width // BLOCK) + n, slice(n * BLOCK, (n + 1) * BLOCK)
-                out_q[block, i] = grad_query[:, at].astype(bf16)
-                out_q[block, rows + i] = attended[:, at].astype(bf16)
+            query_out[i, 0, :, lanes] = grad_query.astype(bf16)
+            query_out[i, 1, :, lanes] = attended.astype(bf16)
         both = jnp.concatenate([grad_key, grad_value], axis=1).T.astype(bf16)
         key_out[i, 0] = both[:HEAD_DIM]
         key_out[i, 1] = both[HEAD_DIM:]
@@ -171,13 +209,18 @@
             for i in range(rows):
                 out[step, i] = key_out[i, 0, :, at]
                 out[step, rows + i] = key_out[i, 1, :, at]
+        at = pl.ds(pl.multiple_of(yy * BLOCK, BLOCK), BLOCK)
+        for i in range(rows):
+            out_q[step, i] = query_out[i, 0, :, at]
+            out_q[step, rows + i] = query_out[i, 1, :, at]
     for out, c in ((keep, core), (send, 1 - core)):
         for dx in range(4):
-            for dz in range(4):
-                r = lax.rem(x - dx + 4, 4) * 8 + lax.rem(zh - dz + 4, 4) * 2 + c
+            for zh in range(4):
+                r = lax.rem(x - dx + 4, 4) * 8 + zh * 2 + c
                 at = pl.ds(pl.multiple_of(r * 32, 32), 32)
-                for dy in range(4):
-                    out[dx, dz, dy] = grad[at, dy * BLOCK : (dy + 1) * BLOCK].astype(out.dtype)
+                for n in range(4):
+                    piece = grad[at, n * BLOCK : (n + 1) * BLOCK]
+                    out[dx, zh, n] = piece.astype(out.dtype)
 
 
 def attention_call(mask, bias_own, bias_other, pieces, kv_other):
@@ -202,6 +245,7 @@
             pltpu.VMEM((rows, HEAD_DIM, queries), bf16),
             pltpu.VMEM((rows, HEAD_DIM, queries), bf16),
             pltpu.VMEM((rows, 2, HEAD_DIM, keys), bf16),
+            pltpu.VMEM((rows, 2, HEAD_DIM, queries), bf16),
         ],
         compiler_params=pltpu.CompilerParams(vmem_limit_bytes=VMEM_LIMIT),
         cost_estimate=pl.CostEstimate(
@@ -226,46 +270,42 @@
     )(keep, came)
 
 
-def add_four_kernel(keep, c1, c2, c3, k0, s1, s2, s3):
-    for n, out in enumerate((k0, s1, s2, s3)):
-        total = keep[n] + c1[n].astype(f32) + c2[n].astype(f32) + c3[n].astype(f32)
-        out[...] = total.astype(out.dtype)
+def add_four_kernel(keep, c1, c2, c3, out):
+    total = (keep[...] + c1[...].astype(f32)) + (c2[...].astype(f32) + c3[...].astype(f32))
+    out[...] = total.astype(bf16)
 
 
 def add_four(keep, c1, c2, c3):
-    shape = keep.shape[1:]
     return pl.pallas_call(
         add_four_kernel,
-        out_shape=(jax.ShapeDtypeStruct(shape, f32),) + (jax.ShapeDtypeStruct(shape, bf16),) * 3,
+        out_shape=jax.ShapeDtypeStruct(keep.shape, bf16),
         compiler_params=pltpu.CompilerParams(vmem_limit_bytes=VMEM_LIMIT),
         name="add_four",
     )(keep, c1, c2, c3)
 
 
-def pack_kernel(keep, c1, c2, c3, own, came, query, t0, t1, t2, t3):
+def pack_kernel(own, came, query, t0, t1, t2, t3):
     half = own.shape[1]
     for n, out in enumerate((t0, t1, t2, t3)):
         out[:half] = (own[n].astype(f32) + came[n].astype(f32)).astype(bf16)
-        out[half : 2 * half] = query[n]
-        total = keep[n] + c1[n].astype(f32) + c2[n].astype(f32) + c3[n].astype(f32)
-        out[2 * half] = total.astype(bf16)
-
-
-def pack_call(keep, c1, c2, c3, own, came, query):
+        out[half:] = query[n]
+
+
+def pack_call(own, came, query):
     half, *tile = own.shape[1:]
     return pl.pallas_call(
         pack_kernel,
-        out_shape=(jax.ShapeDtypeStruct((2 * half + 1, *tile), bf16),) * 4,
+        out_shape=(jax.ShapeDtypeStruct((2 * half, *tile), bf16),) * 4,
         compiler_params=pltpu.CompilerParams(vmem_limit_bytes=VMEM_LIMIT),
         name="pack",
-    )(keep, c1, c2, c3, own, came, query)
+    )(own, came, query)
 
 
 def group_kernel(
     group_ref, gain_ref, wq_ref, wk_ref, wv_ref, wg_ref, coef,
     t0, t1, t2, t3, out_ref,
 ):
-    _, _, _, _, y = place()
+    y = lax.axis_index("y")
     gain = gain_ref[...]
     turn = lax.rem(4 - y, 4) * HEAD_DIM
     wq, wk, wv, wg = (
@@ -308,21 +348,19 @@
     )(group, gain, wq, wk, wv, wg, coef, *pieces)
 
 
-def pair_kernel(pair_ref, gain_ref, weight_ref, t0, t1, t2, t3, out_ref, grad, db):
-    _, _, _, _, y = place()
+def pair_kernel(pair_ref, gain_ref, weight_ref, came, out_ref, grad, db):
     weight = jnp.concatenate(
-        [weight_ref[...].astype(f32), jnp.zeros((BLOCK, BLOCK - HEADS), f32)], axis=1
-    ).T[:8] * gain_ref[...]
+        [weight_ref[...].astype(f32), jnp.zeros((8 - HEADS, BLOCK), f32)], axis=0
+    ) * gain_ref[...]
     weight = weight - jnp.mean(weight, axis=-1, keepdims=True)
     high, low = split_high_low(weight)
     weights = jnp.concatenate([high, high, low, jnp.zeros((8, BLOCK), bf16)], axis=0)
     db[...] = jnp.zeros_like(db)
-    last = t0.shape[0] - 1
-    for step, t in enumerate((t0, t1, t2, t3)):
-        h = lax.rem(y + step, 4)
-        value = t[last].astype(f32)
+    for h in range(HEADS):
+        wide = [came[zh, h].astype(f32) for zh in range(4)]
+        value = (wide[0] + wide[1]) + (wide[2] + wide[3])
         for k in range(32):
-            db[k, pl.ds(h, 1), :] = value[k : k + 1]
+            db[k, h : h + 1, :] = value[k : k + 1]
 
     for k in range(32):
         db_high, db_low = split_high_low(db[k])
@@ -345,7 +383,7 @@
     lax.fori_loop(0, 8, rows, 0)
 
 
-def pair_call(pair, gain, weight, pieces):
+def pair_call(pair, gain, weight, came):
     return pl.pallas_call(
         pair_kernel,
         out_shape=jax.ShapeDtypeStruct(pair.shape, bf16),
@@ -355,12 +393,18 @@
             flops=60_000_000, bytes_accessed=2_200_000, transcendentals=4096
         ),
         name="pair_backward",
-    )(pair, gain, weight, *pieces)
+    )(pair, gain, weight, came)
 
 
 def along(value, axis, step):
     size = 2 if axis in ("core", "z") else 4
     return lax.ppermute(value, axis, [(p, (p + step) % size) for p in range(size)])
+
+
+def exchange(value):
+    flat = value.reshape(16, *value.shape[2:])
+    flat = lax.all_to_all(flat, ("zh", "y"), split_axis=0, concat_axis=0, tiled=True)
+    return flat.reshape(value.shape)
 
 
 def per_device(
@@ -369,16 +413,16 @@
 ):
     gain, shift = ln_gain.reshape(1, BLOCK), ln_shift.reshape(1, BLOCK)
     half = 2 * group.shape[0]
-    *sent, coef = front_call(
-        group, cotangent, pair, gain, shift, w_query, w_key, w_value, w_gate,
-        gate_bias.reshape(1, BLOCK), w_out, w_bias,
+    bias = bias_call(pair, gain, shift, w_bias.T)
+    bias, group, cotangent = lax.optimization_barrier((bias, group, cotangent))
+    near = exchange(bias)
+
+    *sent, coef = project_call(
+        group, cotangent, gain, shift, w_query, w_key, w_value, w_gate,
+        gate_bias.reshape(1, BLOCK), w_out,
     )
     pieces = [sent[0]] + [along(sent[d], "y", d) for d in range(1, 4)]
-    own = jnp.stack([p[2 * half] for p in pieces])
-    gathered = [own] + [along(own, "zh", d) for d in range(1, 4)]
     key_value = jnp.stack([p[:half] for p in pieces])
-    gathered, key_value = lax.optimization_barrier((gathered, key_value))
-    near = jnp.stack(gathered)
     line, kv_other = lax.optimization_barrier(
         ([near] + [along(near, "x", d) for d in range(1, 4)], along(key_value, "z", 1))
     )
@@ -392,12 +436,12 @@
     first = add_core(keep, along(send, "core", 1))
     came = along(out_other, "z", 1)
     second = add_four(first[0], *(along(first[d], "x", -d) for d in range(1, 4)))
-    third = [along(second[d], "zh", -d) for d in range(1, 4)]
-    packed = pack_call(second[0], *third, out_own, came, out_q)
+    grad_bias = exchange(second)
+    packed = pack_call(out_own, came, out_q)
     back = [packed[0]] + [along(packed[d], "y", -d) for d in range(1, 4)]
 
     grad_group = group_call(group, gain, w_query, w_key, w_value, w_gate, coef, back)
-    grad_pair = pair_call(pair, gain, w_bias, back)
+    grad_pair = pair_call(pair, gain, w_bias.T, grad_bias)
     return (grad_group, grad_pair)
 
 

time: 111 us -> 108 us (0.973)
  the two profiles are of different devices: /device:TPU:32 before, /device:TPU:1 now
where the time goes in v3:
time: 108 us; the launch traced here: 107 us
  starting transfers between devices  38.9 us (36%)
  waiting for transfers between devices  34.3 us (32%)
  Pallas kernels  30.4 us (28%)
  local copies, waits for them, and re-layouts  2.56 us (2%)
    ppermute x16, waiting for transfers between devices, along(): lax.ppermute(value, axis, [(p, (p + step) % size) for p in range(size)])  34.3 us
    all_to_all x2, starting transfers between devices, exchange(): lax.all_to_all(flat, ('zh', 'y'), split_axis=0, concat_axis=0, tiled=True)  19.5 us
    ppermute x16, starting transfers between devices, along(): lax.ppermute(value, axis, [(p, (p + step) % size) for p in range(size)])  19.4 us
    pallas_call x1, Pallas kernels, attention_call(): pl.pallas_call(attention_kernel, out_shape=(part, part, part, jax.ShapeDt...  15.5 us
    pallas_call x1, Pallas kernels, pair_call(): pl.pallas_call(pair_kernel, out_shape=jax.ShapeDtypeStruct(pair.shape, bf...  5.46 us
    pallas_call x1, Pallas kernels, bias_call(): pl.pallas_call(bias_kernel, out_shape=jax.ShapeDtypeStruct((4, HEADS, 32,...  5.14 us
    unnamed x28, local copies, waits for them, and re-layouts  2.54 us
  transfers between devices with their start and end apart: 18, of which 13 were waited for; matrix products, arithmetic and copies ran while one was open for 0% of the time, Pallas kernels for 4%

profile of v3, /device:TPU:1, one launch (start us, length us, event | category | flops | bytes accessed | tf_op | source)
XLA Modules:
  0.0 107.2 jit_solution(7691306403420866607)
XLA Ops:
  2.6 5.1 %pair_bias.1 = bf16[4,4,32,128]{3,2,1,0:T(8,128)(2,1)} custom-call(bf16[128,32,128]{2,1,0:T(8,128)(2,1)S(1)} %copy-done, f32[1,128]{1,0:T(1,128)S(1)} %bitcast.22, f32[1,128]{1,0:T(1,128)S(1)} %bitcast.28, bf16[4,128]{1,0:T(4,128)(2,1)S(1)} %bitcast.26), custom_call_target="tpu_custom_call" | custom-call | flops 20000000 | bytes 1200000 | tf_op jit(solution)/shard_map/pair_bias/pallas_call | solution.py:61
  7.8 11.9 %all-to-all-start = ((bf16[16,32,128]{2,1,0:T(8,128)(2,1)}), bf16[16,32,128]{2,1,0:T(8,128)(2,1)S(1)}, u32[]{:S(2)}, u32[]{:S(2)}) async-start(bf16[16,32,128]{2,1,0:T(8,128)(2,1)} %bitcast.5), calls=%async_computation | async-start | bytes 262144 | tf_op jit(solution)/shard_map/all_to_all | solution.py:406
  20.3 1.7 %project.1 = (bf16[20,32,128]{2,1,0:T(8,128)(2,1)S(1)}, bf16[20,32,128]{2,1,0:T(8,128)(2,1)S(1)}, bf16[20,32,128]{2,1,0:T(8,128)(2,1)S(1)}, bf16[20,32,128]{2,1,0:T(8,128)(2,1)S(1)}, f32[5,128,128]{2,1,0:T(8,128)S(1)}) custom-call(bf16[5,128,128]{2,1,0:T(8,128)(2,1)S(1)} %copy-done.2, bf16[5,128,128]{2,1,0:T(8,128)(2,1)S(1)} %copy-done.3, ...), custom_call_target="tpu_custom_call" | custom-call | flops 110000000 | bytes 2000000 | tf_op jit(solution)/shard_map/project/pallas_call | solution.py:117
  22.0 1.4 %collective-permute-start.3 = (bf16[20,32,128]{2,1,0:T(8,128)(2,1)S(1)}, bf16[20,32,128]{2,1,0:T(8,128)(2,1)S(1)}, u32[]{:S(2)}, u32[]{:S(2)}) collective-permute-start(bf16[20,32,128]{2,1,0:T(8,128)(2,1)S(1)} %get-tuple-element.33), channel_id=1, source_target_pairs={{0,1},{1,2},{2,3},{3,0},{4,5},{5,6},{6,7},{7,4},{8,9},{9,10},{10,1... | collective-permute-start | bytes 491528 | tf_op jit(solution)/shard_map/ppermute | solution.py:401
  23.5 2.4 %collective-permute-start.4 = (bf16[20,32,128]{2,1,0:T(8,128)(2,1)S(1)}, bf16[20,32,128]{2,1,0:T(8,128)(2,1)S(1)}, u32[]{:S(2)}, u32[]{:S(2)}) collective-permute-start(bf16[20,32,128]{2,1,0:T(8,128)(2,1)S(1)} %get-tuple-element.34), channel_id=1, source_target_pairs={{0,2},{1,3},{2,0},{3,1},{4,6},{5,7},{6,4},{7,5},{8,10},{9,11},{10,... | collective-permute-start | bytes 491528 | tf_op jit(solution)/shard_map/ppermute | solution.py:401
  27.1 1.6 %collective-permute-done.3.s1 = bf16[20,32,128]{2,1,0:T(8,128)(2,1)S(1)} collective-permute-done((bf16[20,32,128]{2,1,0:T(8,128)(2,1)S(1)}, bf16[20,32,128]{2,1,0:T(8,128)(2,1)S(1)}, u32[]{:S(2)}, u32[]{:S(2)}) %collective-permute-start.3) | collective-permute-done | bytes 163872 | tf_op jit(solution)/shard_map/ppermute | solution.py:401
  28.7 4.9 %collective-permute-done.4.s2 = bf16[20,32,128]{2,1,0:T(8,128)(2,1)S(1)} collective-permute-done((bf16[20,32,128]{2,1,0:T(8,128)(2,1)S(1)}, bf16[20,32,128]{2,1,0:T(8,128)(2,1)S(1)}, u32[]{:S(2)}, u32[]{:S(2)}) %collective-permute-start.4) | collective-permute-done | bytes 163872 | tf_op jit(solution)/shard_map/ppermute | solution.py:401
  34.6 2.5 %collective-permute-start.2 = (bf16[4,4,32,128]{3,2,1,0:T(8,128)(2,1)S(1)}, bf16[4,4,32,128]{3,2,1,0:T(8,128)(2,1)S(1)}, u32[]{:S(2)}, u32[]{:S(2)}) collective-permute-start(bf16[4,4,32,128]{3,2,1,0:T(8,128)(2,1)S(1)} %bitcast.32), channel_id=1, source_target_pairs={{0,192},{64,0},{128,64},{192,128},{1,193},{65,1},{129,65},{193,129... | collective-permute-start | bytes 393224 | tf_op jit(solution)/shard_map/ppermute | solution.py:401
  38.2 1.5 %collective-permute-done.2 = bf16[4,4,32,128]{3,2,1,0:T(8,128)(2,1)S(1)} collective-permute-done((bf16[4,4,32,128]{3,2,1,0:T(8,128)(2,1)S(1)}, bf16[4,4,32,128]{3,2,1,0:T(8,128)(2,1)S(1)}, u32[]{:S(2)}, u32[]{:S(2)}) %collective-permute-start.2) | collective-permute-done | bytes 131104 | tf_op jit(solution)/shard_map/ppermute | solution.py:401
  39.7 2.8 %collective-permute-done.1 = bf16[4,4,32,128]{3,2,1,0:T(8,128)(2,1)S(1)} collective-permute-done((bf16[4,4,32,128]{3,2,1,0:T(8,128)(2,1)S(1)}, bf16[4,4,32,128]{3,2,1,0:T(8,128)(2,1)S(1)}, u32[]{:S(2)}, u32[]{:S(2)}) %collective-permute-start.1) | collective-permute-done | bytes 131104 | tf_op jit(solution)/shard_map/ppermute | solution.py:401
  42.5 1.6 %collective-permute-done = bf16[4,4,32,128]{3,2,1,0:T(8,128)(2,1)S(1)} collective-permute-done((bf16[4,4,32,128]{3,2,1,0:T(8,128)(2,1)S(1)}, bf16[4,4,32,128]{3,2,1,0:T(8,128)(2,1)S(1)}, u32[]{:S(2)}, u32[]{:S(2)}) %collective-permute-start) | collective-permute-done | bytes 131104 | tf_op jit(solution)/shard_map/ppermute | solution.py:401
  44.2 3.4 %collective-permute-start.7 = (bf16[4,4,4,32,128]{4,3,2,1,0:T(8,128)(2,1)S(1)}, bf16[4,4,4,32,128]{4,3,2,1,0:T(8,128)(2,1)S(1)}, u32[]{:S(2)}, u32[]{:S(2)}) collective-permute-start(bf16[4,4,4,32,128]{4,3,2,1,0:T(8,128)(2,1)S(1)} %pad_maximum_fusion.bias_own), channel_id=1, source_target_pairs={{0,8},{8,0},{1,9},{9,1},{2,10},{10,2},{3,11},{11,3},{4,12},{12,4},... | collective-permute-start | bytes 1572872 | tf_op jit(solution)/shard_map/ppermute | solution.py:401
  47.7 1.5 %collective-permute-done.7.bias_other = bf16[4,4,4,32,128]{4,3,2,1,0:T(8,128)(2,1)S(1)} collective-permute-done((bf16[4,4,4,32,128]{4,3,2,1,0:T(8,128)(2,1)S(1)}, bf16[4,4,4,32,128]{4,3,2,1,0:T(8,128)(2,1)S(1)}, u32[]{:S(2)}, u32[]{:S(2)}) %collective-permute-start.7) | collective-permute-done | bytes 524320 | tf_op jit(solution)/shard_map/ppermute | solution.py:401
  49.2 15.5 %attention.1 = (bf16[4,10,32,128]{3,2,1,0:T(8,128)(2,1)S(1)}, bf16[4,10,32,128]{3,2,1,0:T(8,128)(2,1)S(1)}, bf16[4,10,32,128]{3,2,1,0:T(8,128)(2,1)S(1)}, f32[4,...) custom-call(s32[8,128]{1,0:T(8,128)S(1)} %bitcast.31, ...), custom_call_target="tpu_custom_call" | custom-call | flops 8000000000 | bytes 6000000 | tf_op jit(solution)/shard_map/attention/pallas_call | solution.py:231
  68.4 3.2 %collective-permute-done.13.c1 = bf16[4,4,32,128]{3,2,1,0:T(8,128)(2,1)S(1)} collective-permute-done((bf16[4,4,32,128]{3,2,1,0:T(8,128)(2,1)S(1)}, bf16[4,4,32,128]{3,2,1,0:T(8,128)(2,1)S(1)}, u32[]{:S(2)}, u32[]{:S(2)}) %collective-permute-start.13) | collective-permute-done | bytes 131104 | tf_op jit(solution)/shard_map/ppermute | solution.py:401
  71.6 1.5 %collective-permute-done.14.c2 = bf16[4,4,32,128]{3,2,1,0:T(8,128)(2,1)S(1)} collective-permute-done((bf16[4,4,32,128]{3,2,1,0:T(8,128)(2,1)S(1)}, bf16[4,4,32,128]{3,2,1,0:T(8,128)(2,1)S(1)}, u32[]{:S(2)}, u32[]{:S(2)}) %collective-permute-start.14) | collective-permute-done | bytes 131104 | tf_op jit(solution)/shard_map/ppermute | solution.py:401
  73.1 3.8 %collective-permute-done.15.c3 = bf16[4,4,32,128]{3,2,1,0:T(8,128)(2,1)S(1)} collective-permute-done((bf16[4,4,32,128]{3,2,1,0:T(8,128)(2,1)S(1)}, bf16[4,4,32,128]{3,2,1,0:T(8,128)(2,1)S(1)}, u32[]{:S(2)}, u32[]{:S(2)}) %collective-permute-start.15) | collective-permute-done | bytes 131104 | tf_op jit(solution)/shard_map/ppermute | solution.py:401
  77.7 7.6 %all-to-all-start.1 = ((bf16[16,32,128]{2,1,0:T(8,128)(2,1)}), bf16[16,32,128]{2,1,0:T(8,128)(2,1)S(1)}, u32[]{:S(2)}, u32[]{:S(2)}) async-start(bf16[16,32,128]{2,1,0:T(8,128)(2,1)} %bitcast.15), calls=%async_computation.1 | async-start | bytes 262144 | tf_op jit(solution)/shard_map/all_to_all | solution.py:406
  85.4 2.6 %collective-permute-start.9 = (bf16[20,32,128]{2,1,0:T(8,128)(2,1)S(1)}, bf16[20,32,128]{2,1,0:T(8,128)(2,1)S(1)}, u32[]{:S(2)}, u32[]{:S(2)}) collective-permute-start(bf16[20,32,128]{2,1,0:T(8,128)(2,1)S(1)} %get-tuple-element.45), channel_id=1, source_target_pairs={{0,3},{1,0},{2,1},{3,2},{4,7},{5,4},{6,5},{7,6},{8,11},{9,8},{10,9... | collective-permute-start | bytes 491528 | tf_op jit(solution)/shard_map/ppermute | solution.py:401
  89.2 3.4 %collective-permute-done.9.t1 = bf16[20,32,128]{2,1,0:T(8,128)(2,1)S(1)} collective-permute-done((bf16[20,32,128]{2,1,0:T(8,128)(2,1)S(1)}, bf16[20,32,128]{2,1,0:T(8,128)(2,1)S(1)}, u32[]{:S(2)}, u32[]{:S(2)}) %collective-permute-start.9) | collective-permute-done | bytes 163872 | tf_op jit(solution)/shard_map/ppermute | solution.py:401
  92.6 2.2 %collective-permute-done.10.t2 = bf16[20,32,128]{2,1,0:T(8,128)(2,1)S(1)} collective-permute-done((bf16[20,32,128]{2,1,0:T(8,128)(2,1)S(1)}, bf16[20,32,128]{2,1,0:T(8,128)(2,1)S(1)}, u32[]{:S(2)}, u32[]{:S(2)}) %collective-permute-start.10) | collective-permute-done | bytes 163872 | tf_op jit(solution)/shard_map/ppermute | solution.py:401
  94.8 5.2 %collective-permute-done.11.t3 = bf16[20,32,128]{2,1,0:T(8,128)(2,1)S(1)} collective-permute-done((bf16[20,32,128]{2,1,0:T(8,128)(2,1)S(1)}, bf16[20,32,128]{2,1,0:T(8,128)(2,1)S(1)}, u32[]{:S(2)}, u32[]{:S(2)}) %collective-permute-start.11) | collective-permute-done | bytes 163872 | tf_op jit(solution)/shard_map/ppermute | solution.py:401
  100.0 1.7 %group_backward.1 = bf16[5,128,128]{2,1,0:T(8,128)(2,1)} custom-call(bf16[5,128,128]{2,1,0:T(8,128)(2,1)S(1)} %copy-done.2, f32[1,128]{1,0:T(1,128)S(1)} %bitcast.24, bf16[128,128]{1,0:T(8,128)(2,1)S(1)} %copy-done.4, bf16[128,128]{1,0:T(8,128)(2,1)S(1)} %copy-done.5, bf16[128,128]{1,0:T(8,128)(2,1)S(1)} %copy-done.6, bf16[128,128]{1,0:T(8,128)(2,1)S(1)} %copy-done.7, ...), custom_call_target="tpu_custom_call" | custom-call | flops 160000000 | bytes 2000000 | tf_op jit(solution)/shard_map/group_backward/pallas_call | solution.py:340
  101.8 5.5 %pair_backward.1 = bf16[128,32,128]{2,1,0:T(8,128)(2,1)} custom-call(bf16[128,32,128]{2,1,0:T(8,128)(2,1)S(1)} %copy-done.1, f32[1,128]{1,0:T(1,128)S(1)} %bitcast.25, bf16[4,128]{1,0:T(4,128)(2,1)S(1)} %bitcast.27, bf16[4,4,32,128]{3,2,1,0:T(8,128)(2,1)S(1)} %bitcast.21), custom_call_target="tpu_custom_call" | custom-call | flops 60000000 | bytes 2200000 | tf_op jit(solution)/shard_map/pair_backward/pallas_call | solution.py:387
  (54 shorter events, 11.6 us)
Async XLA Ops:
  2.6 17.1 %copy-start.3 = (bf16[5,128,128]{2,1,0:T(8,128)(2,1)S(1)}, bf16[5,128,128]{2,1,0:T(8,128)(2,1)}, u32[]{:S(2)}) copy-start(bf16[5,128,128]{2,1,0:T(8,128)(2,1)} %cot_hbm) | copy-start | bytes 491524
  2.6 17.1 %copy-start.7 = (bf16[128,128]{1,0:T(8,128)(2,1)S(1)}, bf16[128,128]{1,0:T(8,128)(2,1)}, u32[]{:S(2)}) copy-start(bf16[128,128]{1,0:T(8,128)(2,1)} %wg_ref.1) | copy-start | bytes 98308
  2.6 17.1 %copy-start.8 = (bf16[128,128]{1,0:T(8,128)(2,1)S(1)}, bf16[128,128]{1,0:T(8,128)(2,1)}, u32[]{:S(2)}) copy-start(bf16[128,128]{1,0:T(8,128)(2,1)} %wo_hbm.1) | copy-start | bytes 98308
  7.7 12.0 %copy-start.2 = (bf16[5,128,128]{2,1,0:T(8,128)(2,1)S(1)}, bf16[5,128,128]{2,1,0:T(8,128)(2,1)}, u32[]{:S(2)}) copy-start(bf16[5,128,128]{2,1,0:T(8,128)(2,1)} %group_ref) | copy-start | bytes 491524
  7.7 12.0 %copy-start.4 = (bf16[128,128]{1,0:T(8,128)(2,1)S(1)}, bf16[128,128]{1,0:T(8,128)(2,1)}, u32[]{:S(2)}) copy-start(bf16[128,128]{1,0:T(8,128)(2,1)} %wq_ref.1) | copy-start | bytes 98308
  7.8 26.9 %all-to-all-start = ((bf16[16,32,128]{2,1,0:T(8,128)(2,1)}), bf16[16,32,128]{2,1,0:T(8,128)(2,1)S(1)}, u32[]{:S(2)}, u32[]{:S(2)}) async-start(bf16[16,32,128]{2,1,0:T(8,128)(2,1)} %bitcast.5), calls=%async_computation | async-start | bytes 262144 | tf_op jit(solution)/shard_map/all_to_all | solution.py:406
  22.0 6.7 %collective-permute-start.3 = (bf16[20,32,128]{2,1,0:T(8,128)(2,1)S(1)}, bf16[20,32,128]{2,1,0:T(8,128)(2,1)S(1)}, u32[]{:S(2)}, u32[]{:S(2)}) collective-permute-start(bf16[20,32,128]{2,1,0:T(8,128)(2,1)S(1)} %get-tuple-element.33), channel_id=1, source_target_pairs={{0,1},{1,2},{2,3},{3,0},{4,5},{5,6},{6,7},{7,4},{8,9},{9,10},{10,1... | collective-permute-start | bytes 491528 | tf_op jit(solution)/shard_map/ppermute | solution.py:401
  23.5 10.1 %collective-permute-start.4 = (bf16[20,32,128]{2,1,0:T(8,128)(2,1)S(1)}, bf16[20,32,128]{2,1,0:T(8,128)(2,1)S(1)}, u32[]{:S(2)}, u32[]{:S(2)}) collective-permute-start(bf16[20,32,128]{2,1,0:T(8,128)(2,1)S(1)} %get-tuple-element.34), channel_id=1, source_target_pairs={{0,2},{1,3},{2,0},{3,1},{4,6},{5,7},{6,4},{7,5},{8,10},{9,11},{10,... | collective-permute-start | bytes 491528 | tf_op jit(solution)/shard_map/ppermute | solution.py:401
  25.9 7.7 %collective-permute-start.5 = (bf16[20,32,128]{2,1,0:T(8,128)(2,1)S(1)}, bf16[20,32,128]{2,1,0:T(8,128)(2,1)S(1)}, u32[]{:S(2)}, u32[]{:S(2)}) collective-permute-start(bf16[20,32,128]{2,1,0:T(8,128)(2,1)S(1)} %get-tuple-element.35), channel_id=1, source_target_pairs={{0,3},{1,0},{2,1},{3,2},{4,7},{5,4},{6,5},{7,6},{8,11},{9,8},{10,9... | collective-permute-start | bytes 491528 | tf_op jit(solution)/shard_map/ppermute | solution.py:401
  33.7 10.5 %collective-permute-start.6 = (bf16[4,10,32,128]{3,2,1,0:T(8,128)(2,1)S(1)}, bf16[4,10,32,128]{3,2,1,0:T(8,128)(2,1)S(1)}, u32[]{:S(2)}, u32[]{:S(2)}) collective-permute-start(bf16[4,10,32,128]{3,2,1,0:T(8,128)(2,1)S(1)} %pad_maximum_fusion.1), channel_id=1, source_target_pairs={{0,4},{4,0},{1,5},{5,1},{2,6},{6,2},{3,7},{7,3},{8,12},{12,8},{9,1... | collective-permute-start | bytes 983048 | tf_op jit(solution)/shard_map/ppermute | solution.py:401
  34.6 5.1 %collective-permute-start.2 = (bf16[4,4,32,128]{3,2,1,0:T(8,128)(2,1)S(1)}, bf16[4,4,32,128]{3,2,1,0:T(8,128)(2,1)S(1)}, u32[]{:S(2)}, u32[]{:S(2)}) collective-permute-start(bf16[4,4,32,128]{3,2,1,0:T(8,128)(2,1)S(1)} %bitcast.32), channel_id=1, source_target_pairs={{0,192},{64,0},{128,64},{192,128},{1,193},{65,1},{129,65},{193,129... | collective-permute-start | bytes 393224 | tf_op jit(solution)/shard_map/ppermute | solution.py:401
  37.1 5.4 %collective-permute-start.1 = (bf16[4,4,32,128]{3,2,1,0:T(8,128)(2,1)S(1)}, bf16[4,4,32,128]{3,2,1,0:T(8,128)(2,1)S(1)}, u32[]{:S(2)}, u32[]{:S(2)}) collective-permute-start(bf16[4,4,32,128]{3,2,1,0:T(8,128)(2,1)S(1)} %bitcast.33), channel_id=1, source_target_pairs={{0,128},{64,192},{128,0},{192,64},{1,129},{65,193},{129,1},{193,65... | collective-permute-start | bytes 393224 | tf_op jit(solution)/shard_map/ppermute | solution.py:401
  37.6 6.5 %collective-permute-start = (bf16[4,4,32,128]{3,2,1,0:T(8,128)(2,1)S(1)}, bf16[4,4,32,128]{3,2,1,0:T(8,128)(2,1)S(1)}, u32[]{:S(2)}, u32[]{:S(2)}) collective-permute-start(bf16[4,4,32,128]{3,2,1,0:T(8,128)(2,1)S(1)} %bitcast.34), channel_id=1, source_target_pairs={{0,64},{64,128},{128,192},{192,0},{1,65},{65,129},{129,193},{193,1... | collective-permute-start | bytes 393224 | tf_op jit(solution)/shard_map/ppermute | solution.py:401
  44.2 5.0 %collective-permute-start.7 = (bf16[4,4,4,32,128]{4,3,2,1,0:T(8,128)(2,1)S(1)}, bf16[4,4,4,32,128]{4,3,2,1,0:T(8,128)(2,1)S(1)}, u32[]{:S(2)}, u32[]{:S(2)}) collective-permute-start(bf16[4,4,4,32,128]{4,3,2,1,0:T(8,128)(2,1)S(1)} %pad_maximum_fusion.bias_own), channel_id=1, source_target_pairs={{0,8},{8,0},{1,9},{9,1},{2,10},{10,2},{3,11},{11,3},{4,12},{12,4},... | collective-permute-start | bytes 1572872 | tf_op jit(solution)/shard_map/ppermute | solution.py:401
  64.7 2.0 %collective-permute-start.12 = (bf16[4,4,4,32,128]{4,3,2,1,0:T(8,128)(2,1)S(1)}, bf16[4,4,4,32,128]{4,3,2,1,0:T(8,128)(2,1)S(1)}, u32[]{:S(2)}, u32[]{:S(2)}) collective-permute-start(bf16[4,4,4,32,128]{4,3,2,1,0:T(8,128)(2,1)S(1)} %get-tuple-element.49), channel_id=1, source_target_pairs={{0,8},{8,0},{1,9},{9,1},{2,10},{10,2},{3,11},{11,3},{4,12},{12,4},... | collective-permute-start | bytes 1572872 | tf_op jit(solution)/shard_map/ppermute | solution.py:401
  65.2 20.1 %collective-permute-start.8 = (bf16[4,10,32,128]{3,2,1,0:T(8,128)(2,1)S(1)}, bf16[4,10,32,128]{3,2,1,0:T(8,128)(2,1)S(1)}, u32[]{:S(2)}, u32[]{:S(2)}) collective-permute-start(bf16[4,10,32,128]{3,2,1,0:T(8,128)(2,1)S(1)} %get-tuple-element.42), channel_id=1, source_target_pairs={{0,4},{4,0},{1,5},{5,1},{2,6},{6,2},{3,7},{7,3},{8,12},{12,8},{9,1... | collective-permute-start | bytes 983048 | tf_op jit(solution)/shard_map/ppermute | solution.py:401
  66.8 4.8 %collective-permute-start.13 = (bf16[4,4,32,128]{3,2,1,0:T(8,128)(2,1)S(1)}, bf16[4,4,32,128]{3,2,1,0:T(8,128)(2,1)S(1)}, u32[]{:S(2)}, u32[]{:S(2)}) collective-permute-start(bf16[4,4,32,128]{3,2,1,0:T(8,128)(2,1)S(1)} %get-tuple-element.51), channel_id=1, source_target_pairs={{0,192},{64,0},{128,64},{192,128},{1,193},{65,1},{129,65},{193,129... | collective-permute-start | bytes 393224 | tf_op jit(solution)/shard_map/ppermute | solution.py:401
  67.2 5.9 %collective-permute-start.14 = (bf16[4,4,32,128]{3,2,1,0:T(8,128)(2,1)S(1)}, bf16[4,4,32,128]{3,2,1,0:T(8,128)(2,1)S(1)}, u32[]{:S(2)}, u32[]{:S(2)}) collective-permute-start(bf16[4,4,32,128]{3,2,1,0:T(8,128)(2,1)S(1)} %get-tuple-element.52), channel_id=1, source_target_pairs={{0,128},{64,192},{128,0},{192,64},{1,129},{65,193},{129,1},{193,65... | collective-permute-start | bytes 393224 | tf_op jit(solution)/shard_map/ppermute | solution.py:401
  67.7 9.2 %collective-permute-start.15 = (bf16[4,4,32,128]{3,2,1,0:T(8,128)(2,1)S(1)}, bf16[4,4,32,128]{3,2,1,0:T(8,128)(2,1)S(1)}, u32[]{:S(2)}, u32[]{:S(2)}) collective-permute-start(bf16[4,4,32,128]{3,2,1,0:T(8,128)(2,1)S(1)} %get-tuple-element.53), channel_id=1, source_target_pairs={{0,64},{64,128},{128,192},{192,0},{1,65},{65,129},{129,193},{193,1... | collective-permute-start | bytes 393224 | tf_op jit(solution)/shard_map/ppermute | solution.py:401
  77.7 24.1 %all-to-all-start.1 = ((bf16[16,32,128]{2,1,0:T(8,128)(2,1)}), bf16[16,32,128]{2,1,0:T(8,128)(2,1)S(1)}, u32[]{:S(2)}, u32[]{:S(2)}) async-start(bf16[16,32,128]{2,1,0:T(8,128)(2,1)} %bitcast.15), calls=%async_computation.1 | async-start | bytes 262144 | tf_op jit(solution)/shard_map/all_to_all | solution.py:406
  85.3 16.5 %copy-start.1 = (bf16[128,32,128]{2,1,0:T(8,128)(2,1)S(1)}, bf16[128,32,128]{2,1,0:T(8,128)(2,1)}, u32[]{:S(2)}) copy-start(bf16[128,32,128]{2,1,0:T(8,128)(2,1)} %pair_ref.1) | copy-start | bytes 3145732
  85.4 7.2 %collective-permute-start.9 = (bf16[20,32,128]{2,1,0:T(8,128)(2,1)S(1)}, bf16[20,32,128]{2,1,0:T(8,128)(2,1)S(1)}, u32[]{:S(2)}, u32[]{:S(2)}) collective-permute-start(bf16[20,32,128]{2,1,0:T(8,128)(2,1)S(1)} %get-tuple-element.45), channel_id=1, source_target_pairs={{0,3},{1,0},{2,1},{3,2},{4,7},{5,4},{6,5},{7,6},{8,11},{9,8},{10,9... | collective-permute-start | bytes 491528 | tf_op jit(solution)/shard_map/ppermute | solution.py:401
  88.0 6.8 %collective-permute-start.10 = (bf16[20,32,128]{2,1,0:T(8,128)(2,1)S(1)}, bf16[20,32,128]{2,1,0:T(8,128)(2,1)S(1)}, u32[]{:S(2)}, u32[]{:S(2)}) collective-permute-start(bf16[20,32,128]{2,1,0:T(8,128)(2,1)S(1)} %get-tuple-element.46), channel_id=1, source_target_pairs={{0,2},{1,3},{2,0},{3,1},{4,6},{5,7},{6,4},{7,5},{8,10},{9,11},{10,... | collective-permute-start | bytes 491528 | tf_op jit(solution)/shard_map/ppermute | solution.py:401
  88.6 11.4 %collective-permute-start.11 = (bf16[20,32,128]{2,1,0:T(8,128)(2,1)S(1)}, bf16[20,32,128]{2,1,0:T(8,128)(2,1)S(1)}, u32[]{:S(2)}, u32[]{:S(2)}) collective-permute-start(bf16[20,32,128]{2,1,0:T(8,128)(2,1)S(1)} %get-tuple-element.47), channel_id=1, source_target_pairs={{0,1},{1,2},{2,3},{3,0},{4,5},{5,6},{6,7},{7,4},{8,9},{9,10},{10,1... | collective-permute-start | bytes 491528 | tf_op jit(solution)/shard_map/ppermute | solution.py:401
  (8 other events, 32.9 us)

commit v4 on v3

--- a/solution.py
+++ b/solution.py
@@ -22,30 +22,21 @@
     return high, (value - high.astype(f32)).astype(bf16)
 
 
-def fetch(pairs, sems):
-    copies = [pltpu.make_async_copy(src, dst, sems.at[n]) for n, (src, dst) in enumerate(pairs)]
-    for copy in copies:
-        copy.start()
-    return copies
-
-
-def bias_kernel(
-    pair_hbm, gain_ref, shift_ref, weight_ref, out_ref, pair_ref, normed, heads, sems
-):
-    chunks = [pl.ds(16 * n, 16) for n in range(8)]
-    copies = fetch([(pair_hbm.at[at], pair_ref.at[at]) for at in chunks], sems)
+def bias_kernel(pair_ref, gain_ref, shift_ref, weight_ref, out_ref, normed, heads):
     gain, shift = gain_ref[...], shift_ref[...]
     weight_t = jnp.concatenate(
         [weight_ref[...].astype(f32), jnp.zeros((16 - HEADS, BLOCK), f32)], axis=0
     ).astype(bf16)
 
-    for n, copy in enumerate(copies):
-        copy.wait()
-        x = pair_ref[16 * n : 16 * (n + 1)].astype(f32).reshape(512, BLOCK)
+    def rows(step, carry):
+        x = pair_ref[pl.ds(step * 16, 16)].astype(f32).reshape(512, BLOCK)
         centered = x - jnp.mean(x, axis=-1, keepdims=True)
         reciprocal = lax.rsqrt(jnp.mean(centered * centered, axis=-1, keepdims=True) + EPS)
         low = (centered * reciprocal * gain + shift).astype(bf16).astype(f32)
-        normed[512 * n : 512 * (n + 1), :] = low
+        normed[pl.ds(pl.multiple_of(step * 512, 512), 512), :] = low
+        return carry
+
+    lax.fori_loop(0, 8, rows, 0)
 
     for k in range(32):
         block = normed[pl.ds(k, BLOCK, stride=32), :].astype(bf16)
@@ -57,17 +48,10 @@
 
 
 def bias_call(pair, gain, shift, weight):
-    vmem, hbm = pl.BlockSpec(memory_space=pltpu.VMEM), pl.BlockSpec(memory_space=pltpu.HBM)
     return pl.pallas_call(
         bias_kernel,
         out_shape=jax.ShapeDtypeStruct((4, HEADS, 32, BLOCK), bf16),
-        in_specs=[hbm, vmem, vmem, vmem],
-        scratch_shapes=[
-            pltpu.VMEM(pair.shape, bf16),
-            pltpu.VMEM((4096, BLOCK), f32),
-            pltpu.VMEM((HEADS, 32, BLOCK), f32),
-            pltpu.SemaphoreType.DMA((8,)),
-        ],
+        scratch_shapes=[pltpu.VMEM((4096, BLOCK), f32), pltpu.VMEM((HEADS, 32, BLOCK), f32)],
         compiler_params=pltpu.CompilerParams(vmem_limit_bytes=VMEM_LIMIT),
         cost_estimate=pl.CostEstimate(
             flops=20_000_000, bytes_accessed=1_200_000, transcendentals=4096
@@ -77,20 +61,13 @@
 
 
 def project_kernel(
-    group_hbm, cot_hbm, gain_ref, shift_ref, wq_hbm, wk_hbm, wv_hbm, wg_hbm, gb_ref, wo_hbm,
-    s0, s1, s2, s3, coef, group_ref, cot_ref, square, parts, sems,
+    group_ref, cot_ref, gain_ref, shift_ref, wq_ref, wk_ref, wv_ref, wg_ref, gb_ref, wo_ref,
+    s0, s1, s2, s3, coef, parts,
 ):
-    copies = fetch(
-        [(wq_hbm, square.at[0]), (wk_hbm, square.at[1]), (wv_hbm, square.at[2]),
-         (wg_hbm, square.at[3]), (wo_hbm, square.at[4]), (group_hbm, group_ref),
-         (cot_hbm, cot_ref)], sems,
-    )
     y = lax.axis_index("y")
     gain, shift = gain_ref[...], shift_ref[...]
     gate_bias = jnp.broadcast_to(gb_ref[...], (BLOCK, BLOCK)).T
-    for copy in copies:
-        copy.wait()
-    turned = [square[n].astype(f32).T.astype(bf16) for n in range(4)]
+    turned = [w[...].astype(f32).T.astype(bf16) for w in (wq_ref, wk_ref, wv_ref, wg_ref)]
     rows = group_ref.shape[0]
     for i in range(rows):
         x = group_ref[i].astype(f32)
@@ -99,7 +76,7 @@
         low = (centered * reciprocal * gain + shift).astype(bf16)
         dots = [lax.dot_general(w, low, NT, preferred_element_type=f32) for w in turned]
         gating = jax.nn.sigmoid(dots[3] + gate_bias)
-        gated = lax.dot_general(square[4], cot_ref[i], NT, preferred_element_type=f32)
+        gated = lax.dot_general(wo_ref[...], cot_ref[i], NT, preferred_element_type=f32)
         upstream = gated * gating
         coef[i] = upstream * (1.0 - gating)
         for n, value in enumerate((dots[1], dots[2], dots[0] * SCALE, upstream)):
@@ -113,18 +90,10 @@
 def project_call(group, cotangent, gain, shift, wq, wk, wv, wg, gate_bias, wo):
     rows = group.shape[0]
     sent = jax.ShapeDtypeStruct((4 * rows, HEAD_DIM, BLOCK), bf16)
-    vmem, hbm = pl.BlockSpec(memory_space=pltpu.VMEM), pl.BlockSpec(memory_space=pltpu.HBM)
     return pl.pallas_call(
         project_kernel,
         out_shape=(sent,) * 4 + (jax.ShapeDtypeStruct((rows, BLOCK, BLOCK), f32),),
-        in_specs=[hbm, hbm, vmem, vmem, hbm, hbm, hbm, hbm, vmem, hbm],
-        scratch_shapes=[
-            pltpu.VMEM(group.shape, bf16),
-            pltpu.VMEM(group.shape, bf16),
-            pltpu.VMEM((5, BLOCK, BLOCK), bf16),
-            pltpu.VMEM((HEADS, 4 * rows, HEAD_DIM, BLOCK), bf16),
-            pltpu.SemaphoreType.DMA((7,)),
-        ],
+        scratch_shapes=[pltpu.VMEM((HEADS, 4 * rows, HEAD_DIM, BLOCK), bf16)],
         compiler_params=pltpu.CompilerParams(vmem_limit_bytes=VMEM_LIMIT),
         cost_estimate=pl.CostEstimate(
             flops=110_000_000, bytes_accessed=2_000_000, transcendentals=100_000
@@ -415,13 +384,13 @@
     half = 2 * group.shape[0]
     bias = bias_call(pair, gain, shift, w_bias.T)
     bias, group, cotangent = lax.optimization_barrier((bias, group, cotangent))
-    near = exchange(bias)
-
     *sent, coef = project_call(
         group, cotangent, gain, shift, w_query, w_key, w_value, w_gate,
         gate_bias.reshape(1, BLOCK), w_out,
     )
     pieces = [sent[0]] + [along(sent[d], "y", d) for d in range(1, 4)]
+    bias, pieces[1] = lax.optimization_barrier((bias, pieces[1]))
+    near = exchange(bias)
     key_value = jnp.stack([p[:half] for p in pieces])
     line, kv_other = lax.optimization_barrier(
         ([near] + [along(near, "x", d) for d in range(1, 4)], along(key_value, "z", 1))
@@ -435,11 +404,12 @@
 
     first = add_core(keep, along(send, "core", 1))
     came = along(out_other, "z", 1)
-    second = add_four(first[0], *(along(first[d], "x", -d) for d in range(1, 4)))
-    grad_bias = exchange(second)
+    first, out_own, out_q = lax.optimization_barrier((first, out_own, out_q))
     packed = pack_call(out_own, came, out_q)
     back = [packed[0]] + [along(packed[d], "y", -d) for d in range(1, 4)]
-
+    sums = [along(first[d], "x", -d) for d in range(1, 4)]
+    back, sums = lax.optimization_barrier((back, sums))
+    grad_bias = exchange(add_four(first[0], *sums))
     grad_group = group_call(group, gain, w_query, w_key, w_value, w_gate, coef, back)
     grad_pair = pair_call(pair, gain, w_bias.T, grad_bias)
     return (grad_group, grad_pair)

time: 108 us -> 110 us (1.019)
  the two profiles are of different devices: /device:TPU:1 before, /device:TPU:32 now
where the time goes in v4:
time: 110 us
  waiting for transfers between devices  42.5 us (39%)
  starting transfers between devices  35.7 us (32%)
  Pallas kernels  28.3 us (26%)
  local copies, waits for them, and re-layouts  2.58 us (2%)
    ppermute x16, waiting for transfers between devices, along(): lax.ppermute(value, axis, [(p, (p + step) % size) for p in range(size)])  24.7 us
    ppermute x16, starting transfers between devices, along(): lax.ppermute(value, axis, [(p, (p + step) % size) for p in range(size)])  18.2 us
    all_to_all x2, waiting for transfers between devices, exchange(): lax.all_to_all(flat, ('zh', 'y'), split_axis=0, concat_axis=0, tiled=True)  17.8 us
    all_to_all x2, starting transfers between devices, exchange(): lax.all_to_all(flat, ('zh', 'y'), split_axis=0, concat_axis=0, tiled=True)  17.5 us
    pallas_call x1, Pallas kernels, attention_call(): pl.pallas_call(attention_kernel, out_shape=(part, part, part, jax.ShapeDt...  15.5 us
    pallas_call x1, Pallas kernels, pair_call(): pl.pallas_call(pair_kernel, out_shape=jax.ShapeDtypeStruct(pair.shape, bf...  5.47 us
    pallas_call x1, Pallas kernels, bias_call(): pl.pallas_call(bias_kernel, out_shape=jax.ShapeDtypeStruct((4, HEADS, 32,...  3.8 us
    unnamed x28, local copies, waits for them, and re-layouts  2.55 us
  transfers between devices with their start and end apart: 18, of which 12 were waited for; matrix products, arithmetic and copies ran while one was open for 0% of the time, Pallas kernels for 2%

profile of v4, /device:TPU:32, one launch (start us, length us, event | category | flops | bytes accessed | tf_op | source)
XLA Modules:
  0.0 110.1 jit_solution(10324981725562390545)
XLA Ops:
  1.3 1.2 %copy-done = bf16[128,32,128]{2,1,0:T(8,128)(2,1)S(1)} copy-done((bf16[128,32,128]{2,1,0:T(8,128)(2,1)S(1)}, bf16[128,32,128]{2,1,0:T(8,128)(2,1)}, u32[]{:S(2)}) %copy-start) | copy-done | bytes 1048600
  2.6 3.8 %pair_bias.1 = bf16[4,4,32,128]{3,2,1,0:T(8,128)(2,1)} custom-call(bf16[128,32,128]{2,1,0:T(8,128)(2,1)S(1)} %copy-done, f32[1,128]{1,0:T(1,128)S(1)} %bitcast.22, f32[1,128]{1,0:T(1,128)S(1)} %bitcast.28, bf16[4,128]{1,0:T(4,128)(2,1)S(1)} %bitcast.26), custom_call_target="tpu_custom_call" | custom-call | flops 20000000 | bytes 1200000 | tf_op jit(solution)/shard_map/pair_bias/pallas_call | solution.py:51
  8.0 1.6 %collective-permute-start = (bf16[20,32,128]{2,1,0:T(8,128)(2,1)S(1)}, bf16[20,32,128]{2,1,0:T(8,128)(2,1)S(1)}, u32[]{:S(2)}, u32[]{:S(2)}) collective-permute-start(bf16[20,32,128]{2,1,0:T(8,128)(2,1)S(1)} %get-tuple-element.47), channel_id=1, source_target_pairs={{0,1},{1,2},{2,3},{3,0},{4,5},{5,6},{6,7},{7,4},{8,9},{9,10},{10,1... | collective-permute-start | bytes 491528 | tf_op jit(solution)/shard_map/ppermute | solution.py:370
  9.6 2.9 %collective-permute-start.4 = (bf16[20,32,128]{2,1,0:T(8,128)(2,1)S(1)}, bf16[20,32,128]{2,1,0:T(8,128)(2,1)S(1)}, u32[]{:S(2)}, u32[]{:S(2)}) collective-permute-start(bf16[20,32,128]{2,1,0:T(8,128)(2,1)S(1)} %get-tuple-element.51), channel_id=1, source_target_pairs={{0,2},{1,3},{2,0},{3,1},{4,6},{5,7},{6,4},{7,5},{8,10},{9,11},{10,... | collective-permute-start | bytes 491528 | tf_op jit(solution)/shard_map/ppermute | solution.py:370
  12.5 1.3 %collective-permute-start.5 = (bf16[20,32,128]{2,1,0:T(8,128)(2,1)S(1)}, bf16[20,32,128]{2,1,0:T(8,128)(2,1)S(1)}, u32[]{:S(2)}, u32[]{:S(2)}) collective-permute-start(bf16[20,32,128]{2,1,0:T(8,128)(2,1)S(1)} %get-tuple-element.52), channel_id=1, source_target_pairs={{0,3},{1,0},{2,1},{3,2},{4,7},{5,4},{6,5},{7,6},{8,11},{9,8},{10,9... | collective-permute-start | bytes 491528 | tf_op jit(solution)/shard_map/ppermute | solution.py:370
  13.9 1.4 %collective-permute-done.s1 = bf16[20,32,128]{2,1,0:T(8,128)(2,1)S(1)} collective-permute-done((bf16[20,32,128]{2,1,0:T(8,128)(2,1)S(1)}, bf16[20,32,128]{2,1,0:T(8,128)(2,1)S(1)}, u32[]{:S(2)}, u32[]{:S(2)}) %collective-permute-start) | collective-permute-done | bytes 163872 | tf_op jit(solution)/shard_map/ppermute | solution.py:370
  15.3 12.5 %all-to-all-start = ((bf16[16,32,128]{2,1,0:T(8,128)(2,1)}), bf16[16,32,128]{2,1,0:T(8,128)(2,1)S(1)}, u32[]{:S(2)}, u32[]{:S(2)}) async-start(bf16[16,32,128]{2,1,0:T(8,128)(2,1)} %bitcast.5), calls=%async_computation | async-start | bytes 262144 | tf_op jit(solution)/shard_map/all_to_all | solution.py:375
  29.0 9.1 %all-to-all-done = bf16[16,32,128]{2,1,0:T(8,128)(2,1)S(1)} async-done(((bf16[16,32,128]{2,1,0:T(8,128)(2,1)}), bf16[16,32,128]{2,1,0:T(8,128)(2,1)S(1)}, u32[]{:S(2)}, u32[]{:S(2)}) %all-to-all-start) | async-done | bytes 131104 | tf_op jit(solution)/shard_map/all_to_all | solution.py:375
  38.1 2.8 %collective-permute-start.3 = (bf16[4,4,32,128]{3,2,1,0:T(8,128)(2,1)S(1)}, bf16[4,4,32,128]{3,2,1,0:T(8,128)(2,1)S(1)}, u32[]{:S(2)}, u32[]{:S(2)}) collective-permute-start(bf16[4,4,32,128]{3,2,1,0:T(8,128)(2,1)S(1)} %bitcast.32), channel_id=1, source_target_pairs={{0,192},{64,0},{128,64},{192,128},{1,193},{65,1},{129,65},{193,129... | collective-permute-start | bytes 393224 | tf_op jit(solution)/shard_map/ppermute | solution.py:370
  42.6 2.2 %collective-permute-done.3 = bf16[4,4,32,128]{3,2,1,0:T(8,128)(2,1)S(1)} collective-permute-done((bf16[4,4,32,128]{3,2,1,0:T(8,128)(2,1)S(1)}, bf16[4,4,32,128]{3,2,1,0:T(8,128)(2,1)S(1)}, u32[]{:S(2)}, u32[]{:S(2)}) %collective-permute-start.3) | collective-permute-done | bytes 131104 | tf_op jit(solution)/shard_map/ppermute | solution.py:370
  44.8 2.6 %collective-permute-done.2 = bf16[4,4,32,128]{3,2,1,0:T(8,128)(2,1)S(1)} collective-permute-done((bf16[4,4,32,128]{3,2,1,0:T(8,128)(2,1)S(1)}, bf16[4,4,32,128]{3,2,1,0:T(8,128)(2,1)S(1)}, u32[]{:S(2)}, u32[]{:S(2)}) %collective-permute-start.2) | collective-permute-done | bytes 131104 | tf_op jit(solution)/shard_map/ppermute | solution.py:370
  47.5 1.3 %collective-permute-done.1 = bf16[4,4,32,128]{3,2,1,0:T(8,128)(2,1)S(1)} collective-permute-done((bf16[4,4,32,128]{3,2,1,0:T(8,128)(2,1)S(1)}, bf16[4,4,32,128]{3,2,1,0:T(8,128)(2,1)S(1)}, u32[]{:S(2)}, u32[]{:S(2)}) %collective-permute-start.1) | collective-permute-done | bytes 131104 | tf_op jit(solution)/shard_map/ppermute | solution.py:370
  48.9 1.9 %collective-permute-done.7.bias_other = bf16[4,4,4,32,128]{4,3,2,1,0:T(8,128)(2,1)S(1)} collective-permute-done((bf16[4,4,4,32,128]{4,3,2,1,0:T(8,128)(2,1)S(1)}, bf16[4,4,4,32,128]{4,3,2,1,0:T(8,128)(2,1)S(1)}, u32[]{:S(2)}, u32[]{:S(2)}) %collective-permute-start.7) | collective-permute-done | bytes 524320 | tf_op jit(solution)/shard_map/ppermute | solution.py:370
  50.8 15.5 %attention.1 = (bf16[4,10,32,128]{3,2,1,0:T(8,128)(2,1)S(1)}, bf16[4,10,32,128]{3,2,1,0:T(8,128)(2,1)S(1)}, bf16[4,10,32,128]{3,2,1,0:T(8,128)(2,1)S(1)}, f32[4,...) custom-call(s32[8,128]{1,0:T(8,128)S(1)} %bitcast.31, ...), custom_call_target="tpu_custom_call" | custom-call | flops 8000000000 | bytes 6000000 | tf_op jit(solution)/shard_map/attention/pallas_call | solution.py:200
  66.8 1.1 %collective-permute-start.9 = (bf16[4,10,32,128]{3,2,1,0:T(8,128)(2,1)S(1)}, bf16[4,10,32,128]{3,2,1,0:T(8,128)(2,1)S(1)}, u32[]{:S(2)}, u32[]{:S(2)}) collective-permute-start(bf16[4,10,32,128]{3,2,1,0:T(8,128)(2,1)S(1)} %get-tuple-element.67), channel_id=1, source_target_pairs={{0,4},{4,0},{1,5},{5,1},{2,6},{6,2},{3,7},{7,3},{8,12},{12,8},{9,1... | collective-permute-start | bytes 983048 | tf_op jit(solution)/shard_map/ppermute | solution.py:370
  69.3 7.5 %collective-permute-done.9.came = bf16[4,10,32,128]{3,2,1,0:T(8,128)(2,1)S(1)} collective-permute-done((bf16[4,10,32,128]{3,2,1,0:T(8,128)(2,1)S(1)}, bf16[4,10,32,128]{3,2,1,0:T(8,128)(2,1)S(1)}, u32[]{:S(2)}, u32[]{:S(2)}) %collective-permute-start.9) | collective-permute-done | bytes 327712 | tf_op jit(solution)/shard_map/ppermute | solution.py:370
  76.8 1.2 %collective-permute-start.10 = (bf16[20,32,128]{2,1,0:T(8,128)(2,1)S(1)}, bf16[20,32,128]{2,1,0:T(8,128)(2,1)S(1)}, u32[]{:S(2)}, u32[]{:S(2)}) collective-permute-start(bf16[20,32,128]{2,1,0:T(8,128)(2,1)S(1)} %get-tuple-element.70), channel_id=1, source_target_pairs={{0,3},{1,0},{2,1},{3,2},{4,7},{5,4},{6,5},{7,6},{8,11},{9,8},{10,9... | collective-permute-start | bytes 491528 | tf_op jit(solution)/shard_map/ppermute | solution.py:370
  78.0 1.3 %collective-permute-start.11 = (bf16[20,32,128]{2,1,0:T(8,128)(2,1)S(1)}, bf16[20,32,128]{2,1,0:T(8,128)(2,1)S(1)}, u32[]{:S(2)}, u32[]{:S(2)}) collective-permute-start(bf16[20,32,128]{2,1,0:T(8,128)(2,1)S(1)} %get-tuple-element.71), channel_id=1, source_target_pairs={{0,2},{1,3},{2,0},{3,1},{4,6},{5,7},{6,4},{7,5},{8,10},{9,11},{10,... | collective-permute-start | bytes 491528 | tf_op jit(solution)/shard_map/ppermute | solution.py:370
  81.3 5.7 %collective-permute-done.14.c2 = bf16[4,4,32,128]{3,2,1,0:T(8,128)(2,1)S(1)} collective-permute-done((bf16[4,4,32,128]{3,2,1,0:T(8,128)(2,1)S(1)}, bf16[4,4,32,128]{3,2,1,0:T(8,128)(2,1)S(1)}, u32[]{:S(2)}, u32[]{:S(2)}) %collective-permute-start.14) | collective-permute-done | bytes 131104 | tf_op jit(solution)/shard_map/ppermute | solution.py:370
  87.0 1.3 %collective-permute-done.15.c3 = bf16[4,4,32,128]{3,2,1,0:T(8,128)(2,1)S(1)} collective-permute-done((bf16[4,4,32,128]{3,2,1,0:T(8,128)(2,1)S(1)}, bf16[4,4,32,128]{3,2,1,0:T(8,128)(2,1)S(1)}, u32[]{:S(2)}, u32[]{:S(2)}) %collective-permute-start.15) | collective-permute-done | bytes 131104 | tf_op jit(solution)/shard_map/ppermute | solution.py:370
  89.1 5.0 %all-to-all-start.1 = ((bf16[16,32,128]{2,1,0:T(8,128)(2,1)}), bf16[16,32,128]{2,1,0:T(8,128)(2,1)S(1)}, u32[]{:S(2)}, u32[]{:S(2)}) async-start(bf16[16,32,128]{2,1,0:T(8,128)(2,1)} %bitcast.15), calls=%async_computation.1 | async-start | bytes 262144 | tf_op jit(solution)/shard_map/all_to_all | solution.py:375
  94.1 1.7 %group_backward.1 = bf16[5,128,128]{2,1,0:T(8,128)(2,1)} custom-call(bf16[5,128,128]{2,1,0:T(8,128)(2,1)S(1)} %copy-done.2, f32[1,128]{1,0:T(1,128)S(1)} %bitcast.24, bf16[128,128]{1,0:T(8,128)(2,1)S(1)} %copy-done.4, bf16[128,128]{1,0:T(8,128)(2,1)S(1)} %copy-done.5, bf16[128,128]{1,0:T(8,128)(2,1)S(1)} %copy-done.6, bf16[128,128]{1,0:T(8,128)(2,1)S(1)} %copy-done.7, ...), custom_call_target="tpu_custom_call" | custom-call | flops 160000000 | bytes 2000000 | tf_op jit(solution)/shard_map/group_backward/pallas_call | solution.py:309
  95.9 8.7 %all-to-all-done.1 = bf16[16,32,128]{2,1,0:T(8,128)(2,1)S(1)} async-done(((bf16[16,32,128]{2,1,0:T(8,128)(2,1)}), bf16[16,32,128]{2,1,0:T(8,128)(2,1)S(1)}, u32[]{:S(2)}, u32[]{:S(2)}) %all-to-all-start.1) | async-done | bytes 131104 | tf_op jit(solution)/shard_map/all_to_all | solution.py:375
  104.6 5.5 %pair_backward.1 = bf16[128,32,128]{2,1,0:T(8,128)(2,1)} custom-call(bf16[128,32,128]{2,1,0:T(8,128)(2,1)S(1)} %copy-done.1, f32[1,128]{1,0:T(1,128)S(1)} %bitcast.25, bf16[4,128]{1,0:T(4,128)(2,1)S(1)} %bitcast.27, bf16[4,4,32,128]{3,2,1,0:T(8,128)(2,1)S(1)} %bitcast.21), custom_call_target="tpu_custom_call" | custom-call | flops 60000000 | bytes 2200000 | tf_op jit(solution)/shard_map/pair_backward/pallas_call | solution.py:356
  (54 shorter events, 10.0 us)
Async XLA Ops:
  2.6 3.8 %copy-start.4 = (bf16[128,128]{1,0:T(8,128)(2,1)S(1)}, bf16[128,128]{1,0:T(8,128)(2,1)}, u32[]{:S(2)}) copy-start(bf16[128,128]{1,0:T(8,128)(2,1)} %wq_ref.3) | copy-start | bytes 98308
  2.6 3.8 %copy-start.5 = (bf16[128,128]{1,0:T(8,128)(2,1)S(1)}, bf16[128,128]{1,0:T(8,128)(2,1)}, u32[]{:S(2)}) copy-start(bf16[128,128]{1,0:T(8,128)(2,1)} %wk_ref.3) | copy-start | bytes 98308
  2.6 3.9 %copy-start.6 = (bf16[128,128]{1,0:T(8,128)(2,1)S(1)}, bf16[128,128]{1,0:T(8,128)(2,1)}, u32[]{:S(2)}) copy-start(bf16[128,128]{1,0:T(8,128)(2,1)} %wv_ref.3) | copy-start | bytes 98308
  2.6 3.9 %copy-start.7 = (bf16[128,128]{1,0:T(8,128)(2,1)S(1)}, bf16[128,128]{1,0:T(8,128)(2,1)}, u32[]{:S(2)}) copy-start(bf16[128,128]{1,0:T(8,128)(2,1)} %wg_ref.3) | copy-start | bytes 98308
  2.6 3.9 %copy-start.8 = (bf16[128,128]{1,0:T(8,128)(2,1)S(1)}, bf16[128,128]{1,0:T(8,128)(2,1)}, u32[]{:S(2)}) copy-start(bf16[128,128]{1,0:T(8,128)(2,1)} %wo_ref.1) | copy-start | bytes 98308
  8.0 7.3 %collective-permute-start = (bf16[20,32,128]{2,1,0:T(8,128)(2,1)S(1)}, bf16[20,32,128]{2,1,0:T(8,128)(2,1)S(1)}, u32[]{:S(2)}, u32[]{:S(2)}) collective-permute-start(bf16[20,32,128]{2,1,0:T(8,128)(2,1)S(1)} %get-tuple-element.47), channel_id=1, source_target_pairs={{0,1},{1,2},{2,3},{3,0},{4,5},{5,6},{6,7},{7,4},{8,9},{9,10},{10,1... | collective-permute-start | bytes 491528 | tf_op jit(solution)/shard_map/ppermute | solution.py:370
  9.6 18.2 %collective-permute-start.4 = (bf16[20,32,128]{2,1,0:T(8,128)(2,1)S(1)}, bf16[20,32,128]{2,1,0:T(8,128)(2,1)S(1)}, u32[]{:S(2)}, u32[]{:S(2)}) collective-permute-start(bf16[20,32,128]{2,1,0:T(8,128)(2,1)S(1)} %get-tuple-element.51), channel_id=1, source_target_pairs={{0,2},{1,3},{2,0},{3,1},{4,6},{5,7},{6,4},{7,5},{8,10},{9,11},{10,... | collective-permute-start | bytes 491528 | tf_op jit(solution)/shard_map/ppermute | solution.py:370
  12.5 15.3 %collective-permute-start.5 = (bf16[20,32,128]{2,1,0:T(8,128)(2,1)S(1)}, bf16[20,32,128]{2,1,0:T(8,128)(2,1)S(1)}, u32[]{:S(2)}, u32[]{:S(2)}) collective-permute-start(bf16[20,32,128]{2,1,0:T(8,128)(2,1)S(1)} %get-tuple-element.52), channel_id=1, source_target_pairs={{0,3},{1,0},{2,1},{3,2},{4,7},{5,4},{6,5},{7,6},{8,11},{9,8},{10,9... | collective-permute-start | bytes 491528 | tf_op jit(solution)/shard_map/ppermute | solution.py:370
  15.3 22.9 %all-to-all-start = ((bf16[16,32,128]{2,1,0:T(8,128)(2,1)}), bf16[16,32,128]{2,1,0:T(8,128)(2,1)S(1)}, u32[]{:S(2)}, u32[]{:S(2)}) async-start(bf16[16,32,128]{2,1,0:T(8,128)(2,1)} %bitcast.5), calls=%async_computation | async-start | bytes 262144 | tf_op jit(solution)/shard_map/all_to_all | solution.py:375
  27.9 14.6 %collective-permute-start.6 = (bf16[4,10,32,128]{3,2,1,0:T(8,128)(2,1)S(1)}, bf16[4,10,32,128]{3,2,1,0:T(8,128)(2,1)S(1)}, u32[]{:S(2)}, u32[]{:S(2)}) collective-permute-start(bf16[4,10,32,128]{3,2,1,0:T(8,128)(2,1)S(1)} %pad_maximum_fusion.1), channel_id=1, source_target_pairs={{0,4},{4,0},{1,5},{5,1},{2,6},{6,2},{3,7},{7,3},{8,12},{12,8},{9,1... | collective-permute-start | bytes 983048 | tf_op jit(solution)/shard_map/ppermute | solution.py:370
  38.1 6.7 %collective-permute-start.3 = (bf16[4,4,32,128]{3,2,1,0:T(8,128)(2,1)S(1)}, bf16[4,4,32,128]{3,2,1,0:T(8,128)(2,1)S(1)}, u32[]{:S(2)}, u32[]{:S(2)}) collective-permute-start(bf16[4,4,32,128]{3,2,1,0:T(8,128)(2,1)S(1)} %bitcast.32), channel_id=1, source_target_pairs={{0,192},{64,0},{128,64},{192,128},{1,193},{65,1},{129,65},{193,129... | collective-permute-start | bytes 393224 | tf_op jit(solution)/shard_map/ppermute | solution.py:370
  40.9 6.6 %collective-permute-start.2 = (bf16[4,4,32,128]{3,2,1,0:T(8,128)(2,1)S(1)}, bf16[4,4,32,128]{3,2,1,0:T(8,128)(2,1)S(1)}, u32[]{:S(2)}, u32[]{:S(2)}) collective-permute-start(bf16[4,4,32,128]{3,2,1,0:T(8,128)(2,1)S(1)} %bitcast.33), channel_id=1, source_target_pairs={{0,128},{64,192},{128,0},{192,64},{1,129},{65,193},{129,1},{193,65... | collective-permute-start | bytes 393224 | tf_op jit(solution)/shard_map/ppermute | solution.py:370
  41.7 7.1 %collective-permute-start.1 = (bf16[4,4,32,128]{3,2,1,0:T(8,128)(2,1)S(1)}, bf16[4,4,32,128]{3,2,1,0:T(8,128)(2,1)S(1)}, u32[]{:S(2)}, u32[]{:S(2)}) collective-permute-start(bf16[4,4,32,128]{3,2,1,0:T(8,128)(2,1)S(1)} %bitcast.34), channel_id=1, source_target_pairs={{0,64},{64,128},{128,192},{192,0},{1,65},{65,129},{129,193},{193,1... | collective-permute-start | bytes 393224 | tf_op jit(solution)/shard_map/ppermute | solution.py:370
  48.8 2.0 %collective-permute-start.7 = (bf16[4,4,4,32,128]{4,3,2,1,0:T(8,128)(2,1)S(1)}, bf16[4,4,4,32,128]{4,3,2,1,0:T(8,128)(2,1)S(1)}, u32[]{:S(2)}, u32[]{:S(2)}) collective-permute-start(bf16[4,4,4,32,128]{4,3,2,1,0:T(8,128)(2,1)S(1)} %pad_maximum_fusion.bias_own), channel_id=1, source_target_pairs={{0,8},{8,0},{1,9},{9,1},{2,10},{10,2},{3,11},{11,3},{4,12},{12,4},... | collective-permute-start | bytes 1572872 | tf_op jit(solution)/shard_map/ppermute | solution.py:370
  66.4 2.2 %collective-permute-start.8 = (bf16[4,4,4,32,128]{4,3,2,1,0:T(8,128)(2,1)S(1)}, bf16[4,4,4,32,128]{4,3,2,1,0:T(8,128)(2,1)S(1)}, u32[]{:S(2)}, u32[]{:S(2)}) collective-permute-start(bf16[4,4,4,32,128]{4,3,2,1,0:T(8,128)(2,1)S(1)} %get-tuple-element.59), channel_id=1, source_target_pairs={{0,8},{8,0},{1,9},{9,1},{2,10},{10,2},{3,11},{11,3},{4,12},{12,4},... | collective-permute-start | bytes 1572872 | tf_op jit(solution)/shard_map/ppermute | solution.py:370
  66.8 10.0 %collective-permute-start.9 = (bf16[4,10,32,128]{3,2,1,0:T(8,128)(2,1)S(1)}, bf16[4,10,32,128]{3,2,1,0:T(8,128)(2,1)S(1)}, u32[]{:S(2)}, u32[]{:S(2)}) collective-permute-start(bf16[4,10,32,128]{3,2,1,0:T(8,128)(2,1)S(1)} %get-tuple-element.67), channel_id=1, source_target_pairs={{0,4},{4,0},{1,5},{5,1},{2,6},{6,2},{3,7},{7,3},{8,12},{12,8},{9,1... | collective-permute-start | bytes 983048 | tf_op jit(solution)/shard_map/ppermute | solution.py:370
  68.6 12.0 %collective-permute-start.13 = (bf16[4,4,32,128]{3,2,1,0:T(8,128)(2,1)S(1)}, bf16[4,4,32,128]{3,2,1,0:T(8,128)(2,1)S(1)}, u32[]{:S(2)}, u32[]{:S(2)}) collective-permute-start(bf16[4,4,32,128]{3,2,1,0:T(8,128)(2,1)S(1)} %get-tuple-element.73), channel_id=1, source_target_pairs={{0,192},{64,0},{128,64},{192,128},{1,193},{65,1},{129,65},{193,129... | collective-permute-start | bytes 393224 | tf_op jit(solution)/shard_map/ppermute | solution.py:370
  76.8 11.5 %collective-permute-start.10 = (bf16[20,32,128]{2,1,0:T(8,128)(2,1)S(1)}, bf16[20,32,128]{2,1,0:T(8,128)(2,1)S(1)}, u32[]{:S(2)}, u32[]{:S(2)}) collective-permute-start(bf16[20,32,128]{2,1,0:T(8,128)(2,1)S(1)} %get-tuple-element.70), channel_id=1, source_target_pairs={{0,3},{1,0},{2,1},{3,2},{4,7},{5,4},{6,5},{7,6},{8,11},{9,8},{10,9... | collective-permute-start | bytes 491528 | tf_op jit(solution)/shard_map/ppermute | solution.py:370
  78.0 10.3 %collective-permute-start.11 = (bf16[20,32,128]{2,1,0:T(8,128)(2,1)S(1)}, bf16[20,32,128]{2,1,0:T(8,128)(2,1)S(1)}, u32[]{:S(2)}, u32[]{:S(2)}) collective-permute-start(bf16[20,32,128]{2,1,0:T(8,128)(2,1)S(1)} %get-tuple-element.71), channel_id=1, source_target_pairs={{0,2},{1,3},{2,0},{3,1},{4,6},{5,7},{6,4},{7,5},{8,10},{9,11},{10,... | collective-permute-start | bytes 491528 | tf_op jit(solution)/shard_map/ppermute | solution.py:370
  79.3 9.1 %collective-permute-start.12 = (bf16[20,32,128]{2,1,0:T(8,128)(2,1)S(1)}, bf16[20,32,128]{2,1,0:T(8,128)(2,1)S(1)}, u32[]{:S(2)}, u32[]{:S(2)}) collective-permute-start(bf16[20,32,128]{2,1,0:T(8,128)(2,1)S(1)} %get-tuple-element.72), channel_id=1, source_target_pairs={{0,1},{1,2},{2,3},{3,0},{4,5},{5,6},{6,7},{7,4},{8,9},{9,10},{10,1... | collective-permute-start | bytes 491528 | tf_op jit(solution)/shard_map/ppermute | solution.py:370
  79.9 7.1 %collective-permute-start.14 = (bf16[4,4,32,128]{3,2,1,0:T(8,128)(2,1)S(1)}, bf16[4,4,32,128]{3,2,1,0:T(8,128)(2,1)S(1)}, u32[]{:S(2)}, u32[]{:S(2)}) collective-permute-start(bf16[4,4,32,128]{3,2,1,0:T(8,128)(2,1)S(1)} %get-tuple-element.74), channel_id=1, source_target_pairs={{0,128},{64,192},{128,0},{192,64},{1,129},{65,193},{129,1},{193,65... | collective-permute-start | bytes 393224 | tf_op jit(solution)/shard_map/ppermute | solution.py:370
  80.7 7.6 %collective-permute-start.15 = (bf16[4,4,32,128]{3,2,1,0:T(8,128)(2,1)S(1)}, bf16[4,4,32,128]{3,2,1,0:T(8,128)(2,1)S(1)}, u32[]{:S(2)}, u32[]{:S(2)}) collective-permute-start(bf16[4,4,32,128]{3,2,1,0:T(8,128)(2,1)S(1)} %get-tuple-element.75), channel_id=1, source_target_pairs={{0,64},{64,128},{128,192},{192,0},{1,65},{65,129},{129,193},{193,1... | collective-permute-start | bytes 393224 | tf_op jit(solution)/shard_map/ppermute | solution.py:370
  89.1 15.5 %copy-start.1 = (bf16[128,32,128]{2,1,0:T(8,128)(2,1)S(1)}, bf16[128,32,128]{2,1,0:T(8,128)(2,1)}, u32[]{:S(2)}) copy-start(bf16[128,32,128]{2,1,0:T(8,128)(2,1)} %pair_ref.3) | copy-start | bytes 3145732
  89.1 15.4 %all-to-all-start.1 = ((bf16[16,32,128]{2,1,0:T(8,128)(2,1)}), bf16[16,32,128]{2,1,0:T(8,128)(2,1)S(1)}, u32[]{:S(2)}, u32[]{:S(2)}) async-start(bf16[16,32,128]{2,1,0:T(8,128)(2,1)} %bitcast.15), calls=%async_computation.1 | async-start | bytes 262144 | tf_op jit(solution)/shard_map/all_to_all | solution.py:375
  (8 other events, 13.7 us)

commit v5 on v2

--- a/solution.py
+++ b/solution.py
@@ -26,14 +26,68 @@
     return high, (value - high.astype(f32)).astype(bf16)
 
 
-def front_kernel(
-    group_ref, cot_ref, pair_ref, gain_ref, shift_ref, wq_ref, wk_ref, wv_ref, wg_ref, gb_ref,
-    wo_ref, wb_ref, s0, s1, s2, s3, coef, normed, heads, parts,
+def bias_kernel(pair_ref, gain_ref, shift_ref, weight_ref, out_ref, normed, heads):
+    gain, shift = gain_ref[...], shift_ref[...]
+    weight_t = jnp.concatenate(
+        [weight_ref[...].astype(f32), jnp.zeros((16 - HEADS, BLOCK), f32)], axis=0
+    ).astype(bf16)
+
+    def rows(step, carry):
+        x = pair_ref[pl.ds(step * 16, 16)].astype(f32).reshape(512, BLOCK)
+        centered = x - jnp.mean(x, axis=-1, keepdims=True)
+        reciprocal = lax.rsqrt(jnp.mean(centered * centered, axis=-1, keepdims=True) + EPS)
+        low = (centered * reciprocal * gain + shift).astype(bf16).astype(f32)
+        normed[pl.ds(pl.multiple_of(step * 512, 512), 512), :] = low
+        return carry
+
+    lax.fori_loop(0, 8, rows, 0)
+
+    for k in range(32):
+        block = normed[pl.ds(k, BLOCK, stride=32), :].astype(bf16)
+        product = lax.dot_general(weight_t, block, NT, preferred_element_type=f32)
+        for h in range(HEADS):
+            heads[h, k : k + 1, :] = product[h : h + 1]
+    y = lax.axis_index("y")
+    for step in range(HEADS):
+        out_ref[step] = heads[lax.rem(y + step, 4)].astype(bf16)
+
+
+def bias_call(pair, gain, shift, weight):
+    return pl.pallas_call(
+        bias_kernel,
+        out_shape=jax.ShapeDtypeStruct((HEADS, 32, BLOCK), bf16),
+        scratch_shapes=[pltpu.VMEM((4096, BLOCK), f32), pltpu.VMEM((HEADS, 32, BLOCK), f32)],
+        compiler_params=pltpu.CompilerParams(vmem_limit_bytes=VMEM_LIMIT),
+        cost_estimate=pl.CostEstimate(
+            flops=20_000_000, bytes_accessed=1_200_000, transcendentals=4096
+        ),
+        name="pair_bias",
+    )(pair, gain, shift, weight)
+
+
+def turn_kernel(g0, g1, g2, g3, s0, s1, s2, s3):
+    for n, source in enumerate((g0, g1, g2, g3)):
+        for step, out in enumerate((s0, s1, s2, s3)):
+            out[n] = source[step]
+
+
+def turn_call(gathered):
+    return pl.pallas_call(
+        turn_kernel,
+        out_shape=(jax.ShapeDtypeStruct(gathered[0].shape, bf16),) * 4,
+        compiler_params=pltpu.CompilerParams(vmem_limit_bytes=VMEM_LIMIT),
+        name="turn",
+    )(*gathered)
+
+
+def project_kernel(
+    group_ref, cot_ref, gain_ref, shift_ref, wq_ref, wk_ref, wv_ref, wg_ref, gb_ref, wo_ref,
+    s0, s1, s2, s3, coef, parts,
 ):
-    _, _, _, _, y = place()
+    y = lax.axis_index("y")
     gain, shift = gain_ref[...], shift_ref[...]
+    gate_bias = jnp.broadcast_to(gb_ref[...], (BLOCK, BLOCK)).T
     turned = [w[...].astype(f32).T.astype(bf16) for w in (wq_ref, wk_ref, wv_ref, wg_ref)]
-    gate_bias = jnp.broadcast_to(gb_ref[...], (BLOCK, BLOCK)).T
     rows = group_ref.shape[0]
     for i in range(rows):
         x = group_ref[i].astype(f32)
@@ -49,49 +103,23 @@
             value = value.astype(bf16).reshape(HEADS, HEAD_DIM, BLOCK)
             for h in range(HEADS):
                 parts[h, n * rows + i] = value[h]
-
-    weight_t = jnp.concatenate(
-        [wb_ref[...].astype(f32), jnp.zeros((BLOCK, BLOCK - HEADS), f32)], axis=1
-    ).T[:16].astype(bf16)
-
-    def norm_rows(step, carry):
-        x = pair_ref[pl.ds(step * 16, 16)].astype(f32).reshape(512, BLOCK)
-        centered = x - jnp.mean(x, axis=-1, keepdims=True)
-        reciprocal = lax.rsqrt(jnp.mean(centered * centered, axis=-1, keepdims=True) + EPS)
-        low = (centered * reciprocal * gain + shift).astype(bf16).astype(f32)
-        normed[pl.ds(pl.multiple_of(step * 512, 512), 512), :] = low
-        return carry
-
-    lax.fori_loop(0, 8, norm_rows, 0)
-
-    for k in range(32):
-        block = normed[pl.ds(k, BLOCK, stride=32), :].astype(bf16)
-        product = lax.dot_general(weight_t, block, NT, preferred_element_type=f32)
-        for h in range(HEADS):
-            heads[h, k : k + 1, :] = product[h : h + 1]
-    for h in range(HEADS):
-        parts[h, 4 * rows] = heads[h].astype(bf16)
     for step, out in enumerate((s0, s1, s2, s3)):
         out[...] = parts[lax.rem(y + step, 4)]
 
 
-def front_call(group, cotangent, pair, *small):
+def project_call(group, cotangent, gain, shift, wq, wk, wv, wg, gate_bias, wo):
     rows = group.shape[0]
-    sent = jax.ShapeDtypeStruct((4 * rows + 1, HEAD_DIM, BLOCK), bf16)
-    return pl.pallas_call(
-        front_kernel,
+    sent = jax.ShapeDtypeStruct((4 * rows, HEAD_DIM, BLOCK), bf16)
+    return pl.pallas_call(
+        project_kernel,
         out_shape=(sent,) * 4 + (jax.ShapeDtypeStruct((rows, BLOCK, BLOCK), f32),),
-        scratch_shapes=[
-            pltpu.VMEM((4096, BLOCK), f32),
-            pltpu.VMEM((HEADS, 32, BLOCK), f32),
-            pltpu.VMEM((HEADS, 4 * rows + 1, HEAD_DIM, BLOCK), bf16),
-        ],
+        scratch_shapes=[pltpu.VMEM((HEADS, 4 * rows, HEAD_DIM, BLOCK), bf16)],
         compiler_params=pltpu.CompilerParams(vmem_limit_bytes=VMEM_LIMIT),
         cost_estimate=pl.CostEstimate(
-            flops=130_000_000, bytes_accessed=3_000_000, transcendentals=100_000
-        ),
-        name="front",
-    )(group, cotangent, pair, *small)
+            flops=110_000_000, bytes_accessed=2_000_000, transcendentals=100_000
+        ),
+        name="project",
+    )(group, cotangent, gain, shift, wq, wk, wv, wg, gate_bias, wo)
 
 
 def attention_kernel(
@@ -114,7 +142,7 @@
                 for dy in range(4):
                     lanes = slice(dy * BLOCK, (dy + 1) * BLOCK)
                     bias[at, lanes] = jnp.where(
-                        bias[at, lanes] > 0.0, source[dx, dz, dy].astype(f32), -jnp.inf
+                        bias[at, lanes] > 0.0, source[dx, dy, dz].astype(f32), -jnp.inf
                     )
     grad[...] = jnp.zeros_like(grad)
 
@@ -311,8 +339,8 @@
 def pair_kernel(pair_ref, gain_ref, weight_ref, t0, t1, t2, t3, out_ref, grad, db):
     _, _, _, _, y = place()
     weight = jnp.concatenate(
-        [weight_ref[...].astype(f32), jnp.zeros((BLOCK, BLOCK - HEADS), f32)], axis=1
-    ).T[:8] * gain_ref[...]
+        [weight_ref[...].astype(f32), jnp.zeros((8 - HEADS, BLOCK), f32)], axis=0
+    ) * gain_ref[...]
     weight = weight - jnp.mean(weight, axis=-1, keepdims=True)
     high, low = split_high_low(weight)
     weights = jnp.concatenate([high, high, low, jnp.zeros((8, BLOCK), bf16)], axis=0)
@@ -369,16 +397,18 @@
 ):
     gain, shift = ln_gain.reshape(1, BLOCK), ln_shift.reshape(1, BLOCK)
     half = 2 * group.shape[0]
-    *sent, coef = front_call(
-        group, cotangent, pair, gain, shift, w_query, w_key, w_value, w_gate,
-        gate_bias.reshape(1, BLOCK), w_out, w_bias,
-    )
+    bias = bias_call(pair, gain, shift, w_bias.T)
+    bias, group, cotangent = lax.optimization_barrier((bias, group, cotangent))
+    *sent, coef = project_call(
+        group, cotangent, gain, shift, w_query, w_key, w_value, w_gate,
+        gate_bias.reshape(1, BLOCK), w_out,
+    )
+    turned = turn_call([bias] + [along(bias, "zh", d) for d in range(1, 4)])
     pieces = [sent[0]] + [along(sent[d], "y", d) for d in range(1, 4)]
-    own = jnp.stack([p[2 * half] for p in pieces])
-    gathered = [own] + [along(own, "zh", d) for d in range(1, 4)]
+    turned, pieces = lax.optimization_barrier((turned, pieces))
+    blocks = [turned[0]] + [along(turned[d], "y", d) for d in range(1, 4)]
     key_value = jnp.stack([p[:half] for p in pieces])
-    gathered, key_value = lax.optimization_barrier((gathered, key_value))
-    near = jnp.stack(gathered)
+    near = jnp.stack(blocks)
     line, kv_other = lax.optimization_barrier(
         ([near] + [along(near, "x", d) for d in range(1, 4)], along(key_value, "z", 1))
     )
@@ -397,7 +427,7 @@
     back = [packed[0]] + [along(packed[d], "y", -d) for d in range(1, 4)]
 
     grad_group = group_call(group, gain, w_query, w_key, w_value, w_gate, coef, back)
-    grad_pair = pair_call(pair, gain, w_bias, back)
+    grad_pair = pair_call(pair, gain, w_bias.T, back)
     return (grad_group, grad_pair)
 
 

time: 111 us -> 106 us (0.955)
  local copies, waits for them, and re-layouts: 7.62 us -> 2.56 us
  starting transfers between devices: 35.7 us -> 39 us
  waiting for transfers between devices: 38.7 us -> 36.1 us
    unnamed x35 -> x28, local copies, waits for them, and re-layouts: 7.59 us -> 2.54 us
    ppermute x22 -> x25, starting transfers between devices: 35.7 us -> 39 us  [along(): lax.ppermute(value, axis, [(p, (p + step) % size) for p in range(size)])]
    ppermute x22 -> x25, waiting for transfers between devices: 38.7 us -> 36.1 us  [along(): lax.ppermute(value, axis, [(p, (p + step) % size) for p in range(size)])]
    pallas_call x1 -> x3, Pallas kernels: 4.08 us -> 4.06 us  [the longest x1 3.13 us: bias_call(): pl.pallas_call(bias_kernel, out_shape=jax.ShapeDtypeStruct((HEADS, 32, BL...]
  transfers between devices with their start and end apart: 22 -> 25, of which waited for: 16 -> 18; matrix products, arithmetic and copies ran while one was open for 0% -> 0% of each run, Pallas kernels for 0% -> 0%
where the time goes in v5:
time: 106 us
  starting transfers between devices  39 us (37%)
  waiting for transfers between devices  36.1 us (34%)
  Pallas kernels  26.9 us (25%)
  local copies, waits for them, and re-layouts  2.56 us (2%)
    ppermute x25, starting transfers between devices, along(): lax.ppermute(value, axis, [(p, (p + step) % size) for p in range(size)])  39 us
    ppermute x25, waiting for transfers between devices, along(): lax.ppermute(value, axis, [(p, (p + step) % size) for p in range(size)])  36.1 us
    pallas_call x1, Pallas kernels, attention_call(): pl.pallas_call(attention_kernel, out_shape=(part, part, part, jax.ShapeDt...  15.4 us
    pallas_call x1, Pallas kernels, pair_call(): pl.pallas_call(pair_kernel, out_shape=jax.ShapeDtypeStruct(pair.shape, bf...  5.44 us
    pallas_call x1, Pallas kernels, bias_call(): pl.pallas_call(bias_kernel, out_shape=jax.ShapeDtypeStruct((HEADS, 32, BL...  3.13 us
    unnamed x28, local copies, waits for them, and re-layouts  2.54 us
  transfers between devices with their start and end apart: 25, of which 18 were waited for; matrix products, arithmetic and copies ran while one was open for 0% of the time, Pallas kernels for 0%

profile of v5, /device:TPU:32, one launch (start us, length us, event | category | flops | bytes accessed | tf_op | source)
XLA Modules:
  0.0 105.6 jit_solution(7946088106625890986)
XLA Ops:
  2.6 3.1 %pair_bias.1.g0 = bf16[4,32,128]{2,1,0:T(8,128)(2,1)S(1)} custom-call(bf16[128,32,128]{2,1,0:T(8,128)(2,1)S(1)} %copy-done, f32[1,128]{1,0:T(1,128)S(1)} %bitcast.22, f32[1,128]{1,0:T(1,128)S(1)} %bitcast.28, bf16[4,128]{1,0:T(4,128)(2,1)S(1)} %bitcast.26), custom_call_target="tpu_custom_call" | custom-call | flops 20000000 | bytes 1200000 | tf_op jit(solution)/shard_map/pair_bias/pallas_call | solution.py:56
  7.3 1.7 %collective-permute-start.3 = (bf16[20,32,128]{2,1,0:T(8,128)(2,1)S(1)}, bf16[20,32,128]{2,1,0:T(8,128)(2,1)S(1)}, u32[]{:S(2)}, u32[]{:S(2)}) collective-permute-start(bf16[20,32,128]{2,1,0:T(8,128)(2,1)S(1)} %get-tuple-element.53), channel_id=1, source_target_pairs={{0,1},{1,2},{2,3},{3,0},{4,5},{5,6},{6,7},{7,4},{8,9},{9,10},{10,1... | collective-permute-start | bytes 491528 | tf_op jit(solution)/shard_map/ppermute | solution.py:391
  9.0 2.9 %collective-permute-start.4 = (bf16[20,32,128]{2,1,0:T(8,128)(2,1)S(1)}, bf16[20,32,128]{2,1,0:T(8,128)(2,1)S(1)}, u32[]{:S(2)}, u32[]{:S(2)}) collective-permute-start(bf16[20,32,128]{2,1,0:T(8,128)(2,1)S(1)} %get-tuple-element.54), channel_id=1, source_target_pairs={{0,2},{1,3},{2,0},{3,1},{4,6},{5,7},{6,4},{7,5},{8,10},{9,11},{10,... | collective-permute-start | bytes 491528 | tf_op jit(solution)/shard_map/ppermute | solution.py:391
  13.2 5.4 %collective-permute-start.2 = (bf16[4,32,128]{2,1,0:T(8,128)(2,1)S(1)}, bf16[4,32,128]{2,1,0:T(8,128)(2,1)S(1)}, u32[]{:S(2)}, u32[]{:S(2)}) collective-permute-start(bf16[4,32,128]{2,1,0:T(8,128)(2,1)S(1)} %pair_bias.1.g0), channel_id=1, source_target_pairs={{0,48},{16,0},{32,16},{48,32},{1,49},{17,1},{33,17},{49,33},{2,50}... | collective-permute-start | bytes 98312 | tf_op jit(solution)/shard_map/ppermute | solution.py:391
  20.2 2.6 %collective-permute-start = (bf16[4,32,128]{2,1,0:T(8,128)(2,1)S(1)}, bf16[4,32,128]{2,1,0:T(8,128)(2,1)S(1)}, u32[]{:S(2)}, u32[]{:S(2)}) collective-permute-start(bf16[4,32,128]{2,1,0:T(8,128)(2,1)S(1)} %pair_bias.1.g0), channel_id=1, source_target_pairs={{0,16},{16,32},{32,48},{48,0},{1,17},{17,33},{33,49},{49,1},{2,18}... | collective-permute-start | bytes 98312 | tf_op jit(solution)/shard_map/ppermute | solution.py:391
  22.9 3.6 %collective-permute-done.1.g2 = bf16[4,32,128]{2,1,0:T(8,128)(2,1)S(1)} collective-permute-done((bf16[4,32,128]{2,1,0:T(8,128)(2,1)S(1)}, bf16[4,32,128]{2,1,0:T(8,128)(2,1)S(1)}, u32[]{:S(2)}, u32[]{:S(2)}) %collective-permute-start.1) | collective-permute-done | bytes 32800 | tf_op jit(solution)/shard_map/ppermute | solution.py:391
  31.4 1.8 %collective-permute-done.6 = bf16[4,32,128]{2,1,0:T(8,128)(2,1)S(1)} collective-permute-done((bf16[4,32,128]{2,1,0:T(8,128)(2,1)S(1)}, bf16[4,32,128]{2,1,0:T(8,128)(2,1)S(1)}, u32[]{:S(2)}, u32[]{:S(2)}) %collective-permute-start.6) | collective-permute-done | bytes 32800 | tf_op jit(solution)/shard_map/ppermute | solution.py:391
  34.4 2.8 %collective-permute-start.11 = (bf16[4,4,32,128]{3,2,1,0:T(8,128)(2,1)S(1)}, bf16[4,4,32,128]{3,2,1,0:T(8,128)(2,1)S(1)}, u32[]{:S(2)}, u32[]{:S(2)}) collective-permute-start(bf16[4,4,32,128]{3,2,1,0:T(8,128)(2,1)S(1)} %pad_maximum_fusion.2), channel_id=1, source_target_pairs={{0,192},{64,0},{128,64},{192,128},{1,193},{65,1},{129,65},{193,129... | collective-permute-start | bytes 393224 | tf_op jit(solution)/shard_map/ppermute | solution.py:391
  38.9 2.2 %collective-permute-done.11 = bf16[4,4,32,128]{3,2,1,0:T(8,128)(2,1)S(1)} collective-permute-done((bf16[4,4,32,128]{3,2,1,0:T(8,128)(2,1)S(1)}, bf16[4,4,32,128]{3,2,1,0:T(8,128)(2,1)S(1)}, u32[]{:S(2)}, u32[]{:S(2)}) %collective-permute-start.11) | collective-permute-done | bytes 131104 | tf_op jit(solution)/shard_map/ppermute | solution.py:391
  41.2 2.6 %collective-permute-done.10 = bf16[4,4,32,128]{3,2,1,0:T(8,128)(2,1)S(1)} collective-permute-done((bf16[4,4,32,128]{3,2,1,0:T(8,128)(2,1)S(1)}, bf16[4,4,32,128]{3,2,1,0:T(8,128)(2,1)S(1)}, u32[]{:S(2)}, u32[]{:S(2)}) %collective-permute-start.10) | collective-permute-done | bytes 131104 | tf_op jit(solution)/shard_map/ppermute | solution.py:391
  45.5 1.9 %collective-permute-done.13.bias_other = bf16[4,4,4,32,128]{4,3,2,1,0:T(8,128)(2,1)S(1)} collective-permute-done((bf16[4,4,4,32,128]{4,3,2,1,0:T(8,128)(2,1)S(1)}, bf16[4,4,4,32,128]{4,3,2,1,0:T(8,128)(2,1)S(1)}, u32[]{:S(2)}, u32[]{:S(2)}) %collective-permute-start.13) | collective-permute-done | bytes 524320 | tf_op jit(solution)/shard_map/ppermute | solution.py:391
  47.4 15.4 %attention.1 = (bf16[4,10,32,128]{3,2,1,0:T(8,128)(2,1)S(1)}, bf16[4,10,32,128]{3,2,1,0:T(8,128)(2,1)S(1)}, bf16[4,10,32,128]{3,2,1,0:T(8,128)(2,1)S(1)}, f32[4,...) custom-call(s32[8,128]{1,0:T(8,128)S(1)} %bitcast.31, ...), custom_call_target="tpu_custom_call" | custom-call | flops 8000000000 | bytes 6000000 | tf_op jit(solution)/shard_map/attention/pallas_call | solution.py:216
  67.2 4.1 %collective-permute-done.15.c1 = bf16[4,4,32,128]{3,2,1,0:T(8,128)(2,1)S(1)} collective-permute-done((bf16[4,4,32,128]{3,2,1,0:T(8,128)(2,1)S(1)}, bf16[4,4,32,128]{3,2,1,0:T(8,128)(2,1)S(1)}, u32[]{:S(2)}, u32[]{:S(2)}) %collective-permute-start.15) | collective-permute-done | bytes 131104 | tf_op jit(solution)/shard_map/ppermute | solution.py:391
  71.3 2.0 %collective-permute-done.16.c2 = bf16[4,4,32,128]{3,2,1,0:T(8,128)(2,1)S(1)} collective-permute-done((bf16[4,4,32,128]{3,2,1,0:T(8,128)(2,1)S(1)}, bf16[4,4,32,128]{3,2,1,0:T(8,128)(2,1)S(1)}, u32[]{:S(2)}, u32[]{:S(2)}) %collective-permute-start.16) | collective-permute-done | bytes 131104 | tf_op jit(solution)/shard_map/ppermute | solution.py:391
  73.4 1.7 %collective-permute-done.17.c3 = bf16[4,4,32,128]{3,2,1,0:T(8,128)(2,1)S(1)} collective-permute-done((bf16[4,4,32,128]{3,2,1,0:T(8,128)(2,1)S(1)}, bf16[4,4,32,128]{3,2,1,0:T(8,128)(2,1)S(1)}, u32[]{:S(2)}, u32[]{:S(2)}) %collective-permute-start.17) | collective-permute-done | bytes 131104 | tf_op jit(solution)/shard_map/ppermute | solution.py:391
  75.2 2.7 %collective-permute-start.18 = (bf16[4,32,128]{2,1,0:T(8,128)(2,1)S(1)}, bf16[4,32,128]{2,1,0:T(8,128)(2,1)S(1)}, u32[]{:S(2)}, u32[]{:S(2)}) collective-permute-start(bf16[4,32,128]{2,1,0:T(8,128)(2,1)S(1)} %get-tuple-element.76), channel_id=1, source_target_pairs={{0,48},{16,0},{32,16},{48,32},{1,49},{17,1},{33,17},{49,33},{2,50}... | collective-permute-start | bytes 98312 | tf_op jit(solution)/shard_map/ppermute | solution.py:391
  79.4 2.8 %collective-permute-start.20 = (bf16[4,32,128]{2,1,0:T(8,128)(2,1)S(1)}, bf16[4,32,128]{2,1,0:T(8,128)(2,1)S(1)}, u32[]{:S(2)}, u32[]{:S(2)}) collective-permute-start(bf16[4,32,128]{2,1,0:T(8,128)(2,1)S(1)} %get-tuple-element.78), channel_id=1, source_target_pairs={{0,16},{16,32},{32,48},{48,0},{1,17},{17,33},{33,49},{49,1},{2,18}... | collective-permute-start | bytes 98312 | tf_op jit(solution)/shard_map/ppermute | solution.py:391
  82.2 3.6 %collective-permute-done.19.c2 = bf16[4,32,128]{2,1,0:T(8,128)(2,1)S(1)} collective-permute-done((bf16[4,32,128]{2,1,0:T(8,128)(2,1)S(1)}, bf16[4,32,128]{2,1,0:T(8,128)(2,1)S(1)}, u32[]{:S(2)}, u32[]{:S(2)}) %collective-permute-start.19) | collective-permute-done | bytes 32800 | tf_op jit(solution)/shard_map/ppermute | solution.py:391
  85.9 2.7 %collective-permute-start.22 = (bf16[21,32,128]{2,1,0:T(8,128)(2,1)S(1)}, bf16[21,32,128]{2,1,0:T(8,128)(2,1)S(1)}, u32[]{:S(2)}, u32[]{:S(2)}) collective-permute-start(bf16[21,32,128]{2,1,0:T(8,128)(2,1)S(1)} %get-tuple-element.83), channel_id=1, source_target_pairs={{0,3},{1,0},{2,1},{3,2},{4,7},{5,4},{6,5},{7,6},{8,11},{9,8},{10,9... | collective-permute-start | bytes 516104 | tf_op jit(solution)/shard_map/ppermute | solution.py:391
  89.7 5.0 %collective-permute-done.22.t1 = bf16[21,32,128]{2,1,0:T(8,128)(2,1)S(1)} collective-permute-done((bf16[21,32,128]{2,1,0:T(8,128)(2,1)S(1)}, bf16[21,32,128]{2,1,0:T(8,128)(2,1)S(1)}, u32[]{:S(2)}, u32[]{:S(2)}) %collective-permute-start.22) | collective-permute-done | bytes 172064 | tf_op jit(solution)/shard_map/ppermute | solution.py:391
  94.7 1.9 %collective-permute-done.23.t2 = bf16[21,32,128]{2,1,0:T(8,128)(2,1)S(1)} collective-permute-done((bf16[21,32,128]{2,1,0:T(8,128)(2,1)S(1)}, bf16[21,32,128]{2,1,0:T(8,128)(2,1)S(1)}, u32[]{:S(2)}, u32[]{:S(2)}) %collective-permute-start.23) | collective-permute-done | bytes 172064 | tf_op jit(solution)/shard_map/ppermute | solution.py:391
  96.6 1.8 %collective-permute-done.24.t3 = bf16[21,32,128]{2,1,0:T(8,128)(2,1)S(1)} collective-permute-done((bf16[21,32,128]{2,1,0:T(8,128)(2,1)S(1)}, bf16[21,32,128]{2,1,0:T(8,128)(2,1)S(1)}, u32[]{:S(2)}, u32[]{:S(2)}) %collective-permute-start.24) | collective-permute-done | bytes 172064 | tf_op jit(solution)/shard_map/ppermute | solution.py:391
  98.4 5.4 %pair_backward.1 = bf16[128,32,128]{2,1,0:T(8,128)(2,1)} custom-call(bf16[128,32,128]{2,1,0:T(8,128)(2,1)S(1)} %copy-done.1, f32[1,128]{1,0:T(1,128)S(1)} %bitcast.24, bf16[4,128]{1,0:T(4,128)(2,1)S(1)} %bitcast.27, bf16[21,32,128]{2,1,0:T(8,128)(2,1)S(1)} %get-tuple-element.82.t0, bf16[21,32,128]{2,1,0:T(8,128)(2,1)S(1)} %collective-permute-done.22.t1, ...), custom_call_target="tpu_custom_call" | custom-call | flops 60000000 | bytes 2200000 | tf_op jit(solution)/shard_map/pair_backward/pallas_call | solution.py:377
  103.8 1.7 %group_backward.1 = bf16[5,128,128]{2,1,0:T(8,128)(2,1)} custom-call(bf16[5,128,128]{2,1,0:T(8,128)(2,1)S(1)} %copy-done.2, f32[1,128]{1,0:T(1,128)S(1)} %bitcast.25, bf16[128,128]{1,0:T(8,128)(2,1)S(1)} %copy-done.4, bf16[128,128]{1,0:T(8,128)(2,1)S(1)} %copy-done.5, bf16[128,128]{1,0:T(8,128)(2,1)S(1)} %copy-done.6, bf16[128,128]{1,0:T(8,128)(2,1)S(1)} %copy-done.7, ...), custom_call_target="tpu_custom_call" | custom-call | flops 160000000 | bytes 2000000 | tf_op jit(solution)/shard_map/group_backward/pallas_call | solution.py:328
  (68 shorter events, 22.9 us)
Async XLA Ops:
  7.3 19.2 %collective-permute-start.3 = (bf16[20,32,128]{2,1,0:T(8,128)(2,1)S(1)}, bf16[20,32,128]{2,1,0:T(8,128)(2,1)S(1)}, u32[]{:S(2)}, u32[]{:S(2)}) collective-permute-start(bf16[20,32,128]{2,1,0:T(8,128)(2,1)S(1)} %get-tuple-element.53), channel_id=1, source_target_pairs={{0,1},{1,2},{2,3},{3,0},{4,5},{5,6},{6,7},{7,4},{8,9},{9,10},{10,1... | collective-permute-start | bytes 491528 | tf_op jit(solution)/shard_map/ppermute | solution.py:391
  9.0 17.6 %collective-permute-start.4 = (bf16[20,32,128]{2,1,0:T(8,128)(2,1)S(1)}, bf16[20,32,128]{2,1,0:T(8,128)(2,1)S(1)}, u32[]{:S(2)}, u32[]{:S(2)}) collective-permute-start(bf16[20,32,128]{2,1,0:T(8,128)(2,1)S(1)} %get-tuple-element.54), channel_id=1, source_target_pairs={{0,2},{1,3},{2,0},{3,1},{4,6},{5,7},{6,4},{7,5},{8,10},{9,11},{10,... | collective-permute-start | bytes 491528 | tf_op jit(solution)/shard_map/ppermute | solution.py:391
  11.9 14.7 %collective-permute-start.5 = (bf16[20,32,128]{2,1,0:T(8,128)(2,1)S(1)}, bf16[20,32,128]{2,1,0:T(8,128)(2,1)S(1)}, u32[]{:S(2)}, u32[]{:S(2)}) collective-permute-start(bf16[20,32,128]{2,1,0:T(8,128)(2,1)S(1)} %get-tuple-element.55), channel_id=1, source_target_pairs={{0,3},{1,0},{2,1},{3,2},{4,7},{5,4},{6,5},{7,6},{8,11},{9,8},{10,9... | collective-permute-start | bytes 491528 | tf_op jit(solution)/shard_map/ppermute | solution.py:391
  13.2 7.0 %collective-permute-start.2 = (bf16[4,32,128]{2,1,0:T(8,128)(2,1)S(1)}, bf16[4,32,128]{2,1,0:T(8,128)(2,1)S(1)}, u32[]{:S(2)}, u32[]{:S(2)}) collective-permute-start(bf16[4,32,128]{2,1,0:T(8,128)(2,1)S(1)} %pair_bias.1.g0), channel_id=1, source_target_pairs={{0,48},{16,0},{32,16},{48,32},{1,49},{17,1},{33,17},{49,33},{2,50}... | collective-permute-start | bytes 98312 | tf_op jit(solution)/shard_map/ppermute | solution.py:391
  18.6 7.8 %collective-permute-start.1 = (bf16[4,32,128]{2,1,0:T(8,128)(2,1)S(1)}, bf16[4,32,128]{2,1,0:T(8,128)(2,1)S(1)}, u32[]{:S(2)}, u32[]{:S(2)}) collective-permute-start(bf16[4,32,128]{2,1,0:T(8,128)(2,1)S(1)} %pair_bias.1.g0), channel_id=1, source_target_pairs={{0,32},{16,48},{32,0},{48,16},{1,33},{17,49},{33,1},{49,17},{2,34}... | collective-permute-start | bytes 98312 | tf_op jit(solution)/shard_map/ppermute | solution.py:391
  20.2 6.3 %collective-permute-start = (bf16[4,32,128]{2,1,0:T(8,128)(2,1)S(1)}, bf16[4,32,128]{2,1,0:T(8,128)(2,1)S(1)}, u32[]{:S(2)}, u32[]{:S(2)}) collective-permute-start(bf16[4,32,128]{2,1,0:T(8,128)(2,1)S(1)} %pair_bias.1.g0), channel_id=1, source_target_pairs={{0,16},{16,32},{32,48},{48,0},{1,17},{17,33},{33,49},{49,1},{2,18}... | collective-permute-start | bytes 98312 | tf_op jit(solution)/shard_map/ppermute | solution.py:391
  26.7 18.4 %collective-permute-start.12 = (bf16[4,10,32,128]{3,2,1,0:T(8,128)(2,1)S(1)}, bf16[4,10,32,128]{3,2,1,0:T(8,128)(2,1)S(1)}, u32[]{:S(2)}, u32[]{:S(2)}) collective-permute-start(bf16[4,10,32,128]{3,2,1,0:T(8,128)(2,1)S(1)} %pad_maximum_fusion.1), channel_id=1, source_target_pairs={{0,4},{4,0},{1,5},{5,1},{2,6},{6,2},{3,7},{7,3},{8,12},{12,8},{9,1... | collective-permute-start | bytes 983048 | tf_op jit(solution)/shard_map/ppermute | solution.py:391
  28.1 5.1 %collective-permute-start.6 = (bf16[4,32,128]{2,1,0:T(8,128)(2,1)S(1)}, bf16[4,32,128]{2,1,0:T(8,128)(2,1)S(1)}, u32[]{:S(2)}, u32[]{:S(2)}) collective-permute-start(bf16[4,32,128]{2,1,0:T(8,128)(2,1)S(1)} %get-tuple-element.57), channel_id=1, source_target_pairs={{0,1},{1,2},{2,3},{3,0},{4,5},{5,6},{6,7},{7,4},{8,9},{9,10},{10,1... | collective-permute-start | bytes 98312 | tf_op jit(solution)/shard_map/ppermute | solution.py:391
  28.7 5.4 %collective-permute-start.7 = (bf16[4,32,128]{2,1,0:T(8,128)(2,1)S(1)}, bf16[4,32,128]{2,1,0:T(8,128)(2,1)S(1)}, u32[]{:S(2)}, u32[]{:S(2)}) collective-permute-start(bf16[4,32,128]{2,1,0:T(8,128)(2,1)S(1)} %get-tuple-element.58), channel_id=1, source_target_pairs={{0,2},{1,3},{2,0},{3,1},{4,6},{5,7},{6,4},{7,5},{8,10},{9,11},{10,... | collective-permute-start | bytes 98312 | tf_op jit(solution)/shard_map/ppermute | solution.py:391
  29.9 4.5 %collective-permute-start.8 = (bf16[4,32,128]{2,1,0:T(8,128)(2,1)S(1)}, bf16[4,32,128]{2,1,0:T(8,128)(2,1)S(1)}, u32[]{:S(2)}, u32[]{:S(2)}) collective-permute-start(bf16[4,32,128]{2,1,0:T(8,128)(2,1)S(1)} %get-tuple-element.59), channel_id=1, source_target_pairs={{0,3},{1,0},{2,1},{3,2},{4,7},{5,4},{6,5},{7,6},{8,11},{9,8},{10,9... | collective-permute-start | bytes 98312 | tf_op jit(solution)/shard_map/ppermute | solution.py:391
  34.4 6.8 %collective-permute-start.11 = (bf16[4,4,32,128]{3,2,1,0:T(8,128)(2,1)S(1)}, bf16[4,4,32,128]{3,2,1,0:T(8,128)(2,1)S(1)}, u32[]{:S(2)}, u32[]{:S(2)}) collective-permute-start(bf16[4,4,32,128]{3,2,1,0:T(8,128)(2,1)S(1)} %pad_maximum_fusion.2), channel_id=1, source_target_pairs={{0,192},{64,0},{128,64},{192,128},{1,193},{65,1},{129,65},{193,129... | collective-permute-start | bytes 393224 | tf_op jit(solution)/shard_map/ppermute | solution.py:391
  37.3 6.6 %collective-permute-start.10 = (bf16[4,4,32,128]{3,2,1,0:T(8,128)(2,1)S(1)}, bf16[4,4,32,128]{3,2,1,0:T(8,128)(2,1)S(1)}, u32[]{:S(2)}, u32[]{:S(2)}) collective-permute-start(bf16[4,4,32,128]{3,2,1,0:T(8,128)(2,1)S(1)} %pad_maximum_fusion.2), channel_id=1, source_target_pairs={{0,128},{64,192},{128,0},{192,64},{1,129},{65,193},{129,1},{193,65... | collective-permute-start | bytes 393224 | tf_op jit(solution)/shard_map/ppermute | solution.py:391
  38.1 7.1 %collective-permute-start.9 = (bf16[4,4,32,128]{3,2,1,0:T(8,128)(2,1)S(1)}, bf16[4,4,32,128]{3,2,1,0:T(8,128)(2,1)S(1)}, u32[]{:S(2)}, u32[]{:S(2)}) collective-permute-start(bf16[4,4,32,128]{3,2,1,0:T(8,128)(2,1)S(1)} %pad_maximum_fusion.2), channel_id=1, source_target_pairs={{0,64},{64,128},{128,192},{192,0},{1,65},{65,129},{129,193},{193,1... | collective-permute-start | bytes 393224 | tf_op jit(solution)/shard_map/ppermute | solution.py:391
  45.2 2.2 %collective-permute-start.13 = (bf16[4,4,4,32,128]{4,3,2,1,0:T(8,128)(2,1)S(1)}, bf16[4,4,4,32,128]{4,3,2,1,0:T(8,128)(2,1)S(1)}, u32[]{:S(2)}, u32[]{:S(2)}) collective-permute-start(bf16[4,4,4,32,128]{4,3,2,1,0:T(8,128)(2,1)S(1)} %pad_maximum_fusion.bias_own), channel_id=1, source_target_pairs={{0,8},{8,0},{1,9},{9,1},{2,10},{10,2},{3,11},{11,3},{4,12},{12,4},... | collective-permute-start | bytes 1572872 | tf_op jit(solution)/shard_map/ppermute | solution.py:391
  63.0 19.2 %collective-permute-start.21 = (bf16[4,10,32,128]{3,2,1,0:T(8,128)(2,1)S(1)}, bf16[4,10,32,128]{3,2,1,0:T(8,128)(2,1)S(1)}, u32[]{:S(2)}, u32[]{:S(2)}) collective-permute-start(bf16[4,10,32,128]{3,2,1,0:T(8,128)(2,1)S(1)} %get-tuple-element.80), channel_id=1, source_target_pairs={{0,4},{4,0},{1,5},{5,1},{2,6},{6,2},{3,7},{7,3},{8,12},{12,8},{9,1... | collective-permute-start | bytes 983048 | tf_op jit(solution)/shard_map/ppermute | solution.py:391
  64.9 6.4 %collective-permute-start.15 = (bf16[4,4,32,128]{3,2,1,0:T(8,128)(2,1)S(1)}, bf16[4,4,32,128]{3,2,1,0:T(8,128)(2,1)S(1)}, u32[]{:S(2)}, u32[]{:S(2)}) collective-permute-start(bf16[4,4,32,128]{3,2,1,0:T(8,128)(2,1)S(1)} %get-tuple-element.72), channel_id=1, source_target_pairs={{0,192},{64,0},{128,64},{192,128},{1,193},{65,1},{129,65},{193,129... | collective-permute-start | bytes 393224 | tf_op jit(solution)/shard_map/ppermute | solution.py:391
  65.6 7.8 %collective-permute-start.16 = (bf16[4,4,32,128]{3,2,1,0:T(8,128)(2,1)S(1)}, bf16[4,4,32,128]{3,2,1,0:T(8,128)(2,1)S(1)}, u32[]{:S(2)}, u32[]{:S(2)}) collective-permute-start(bf16[4,4,32,128]{3,2,1,0:T(8,128)(2,1)S(1)} %get-tuple-element.73), channel_id=1, source_target_pairs={{0,128},{64,192},{128,0},{192,64},{1,129},{65,193},{129,1},{193,65... | collective-permute-start | bytes 393224 | tf_op jit(solution)/shard_map/ppermute | solution.py:391
  66.4 8.8 %collective-permute-start.17 = (bf16[4,4,32,128]{3,2,1,0:T(8,128)(2,1)S(1)}, bf16[4,4,32,128]{3,2,1,0:T(8,128)(2,1)S(1)}, u32[]{:S(2)}, u32[]{:S(2)}) collective-permute-start(bf16[4,4,32,128]{3,2,1,0:T(8,128)(2,1)S(1)} %get-tuple-element.74), channel_id=1, source_target_pairs={{0,64},{64,128},{128,192},{192,0},{1,65},{65,129},{129,193},{193,1... | collective-permute-start | bytes 393224 | tf_op jit(solution)/shard_map/ppermute | solution.py:391
  75.2 7.0 %collective-permute-start.18 = (bf16[4,32,128]{2,1,0:T(8,128)(2,1)S(1)}, bf16[4,32,128]{2,1,0:T(8,128)(2,1)S(1)}, u32[]{:S(2)}, u32[]{:S(2)}) collective-permute-start(bf16[4,32,128]{2,1,0:T(8,128)(2,1)S(1)} %get-tuple-element.76), channel_id=1, source_target_pairs={{0,48},{16,0},{32,16},{48,32},{1,49},{17,1},{33,17},{49,33},{2,50}... | collective-permute-start | bytes 98312 | tf_op jit(solution)/shard_map/ppermute | solution.py:391
  78.0 7.8 %collective-permute-start.19 = (bf16[4,32,128]{2,1,0:T(8,128)(2,1)S(1)}, bf16[4,32,128]{2,1,0:T(8,128)(2,1)S(1)}, u32[]{:S(2)}, u32[]{:S(2)}) collective-permute-start(bf16[4,32,128]{2,1,0:T(8,128)(2,1)S(1)} %get-tuple-element.77), channel_id=1, source_target_pairs={{0,32},{16,48},{32,0},{48,16},{1,33},{17,49},{33,1},{49,17},{2,34}... | collective-permute-start | bytes 98312 | tf_op jit(solution)/shard_map/ppermute | solution.py:391
  79.4 6.4 %collective-permute-start.20 = (bf16[4,32,128]{2,1,0:T(8,128)(2,1)S(1)}, bf16[4,32,128]{2,1,0:T(8,128)(2,1)S(1)}, u32[]{:S(2)}, u32[]{:S(2)}) collective-permute-start(bf16[4,32,128]{2,1,0:T(8,128)(2,1)S(1)} %get-tuple-element.78), channel_id=1, source_target_pairs={{0,16},{16,32},{32,48},{48,0},{1,17},{17,33},{33,49},{49,1},{2,18}... | collective-permute-start | bytes 98312 | tf_op jit(solution)/shard_map/ppermute | solution.py:391
  85.9 8.8 %collective-permute-start.22 = (bf16[21,32,128]{2,1,0:T(8,128)(2,1)S(1)}, bf16[21,32,128]{2,1,0:T(8,128)(2,1)S(1)}, u32[]{:S(2)}, u32[]{:S(2)}) collective-permute-start(bf16[21,32,128]{2,1,0:T(8,128)(2,1)S(1)} %get-tuple-element.83), channel_id=1, source_target_pairs={{0,3},{1,0},{2,1},{3,2},{4,7},{5,4},{6,5},{7,6},{8,11},{9,8},{10,9... | collective-permute-start | bytes 516104 | tf_op jit(solution)/shard_map/ppermute | solution.py:391
  88.6 8.0 %collective-permute-start.23 = (bf16[21,32,128]{2,1,0:T(8,128)(2,1)S(1)}, bf16[21,32,128]{2,1,0:T(8,128)(2,1)S(1)}, u32[]{:S(2)}, u32[]{:S(2)}) collective-permute-start(bf16[21,32,128]{2,1,0:T(8,128)(2,1)S(1)} %get-tuple-element.84), channel_id=1, source_target_pairs={{0,2},{1,3},{2,0},{3,1},{4,6},{5,7},{6,4},{7,5},{8,10},{9,11},{10,... | collective-permute-start | bytes 516104 | tf_op jit(solution)/shard_map/ppermute | solution.py:391
  89.7 8.7 %collective-permute-start.24 = (bf16[21,32,128]{2,1,0:T(8,128)(2,1)S(1)}, bf16[21,32,128]{2,1,0:T(8,128)(2,1)S(1)}, u32[]{:S(2)}, u32[]{:S(2)}) collective-permute-start(bf16[21,32,128]{2,1,0:T(8,128)(2,1)S(1)} %get-tuple-element.85), channel_id=1, source_target_pairs={{0,1},{1,2},{2,3},{3,0},{4,5},{5,6},{6,7},{7,4},{8,9},{9,10},{10,1... | collective-permute-start | bytes 516104 | tf_op jit(solution)/shard_map/ppermute | solution.py:391
  (15 other events, 64.0 us)

commit v6 on v5

--- a/solution.py
+++ b/solution.py
@@ -59,7 +59,7 @@
         scratch_shapes=[pltpu.VMEM((4096, BLOCK), f32), pltpu.VMEM((HEADS, 32, BLOCK), f32)],
         compiler_params=pltpu.CompilerParams(vmem_limit_bytes=VMEM_LIMIT),
         cost_estimate=pl.CostEstimate(
-            flops=20_000_000, bytes_accessed=1_200_000, transcendentals=4096
+            flops=3_500_000_000, bytes_accessed=1_200_000, transcendentals=4096
         ),
         name="pair_bias",
     )(pair, gain, shift, weight)
@@ -160,7 +160,7 @@
             query_t[i, :, step * BLOCK : (step + 1) * BLOCK] = own[2 * rows + i]
             up_t[i, :, step * BLOCK : (step + 1) * BLOCK] = own[3 * rows + i]
 
-    width = 256
+    width = 512
 
     def row(i, carry):
         grad_key = jnp.zeros((keys, HEAD_DIM), f32)
@@ -270,23 +270,36 @@
     )(keep, c1, c2, c3)
 
 
-def pack_kernel(keep, c1, c2, c3, own, came, query, t0, t1, t2, t3):
+def add_last_kernel(keep, c1, c2, c3, s0, s1, s2, s3):
+    for n, out in enumerate((s0, s1, s2, s3)):
+        total = keep[n] + c1[n].astype(f32) + c2[n].astype(f32) + c3[n].astype(f32)
+        out[...] = total.astype(bf16)
+
+
+def add_last(keep, c1, c2, c3):
+    return pl.pallas_call(
+        add_last_kernel,
+        out_shape=(jax.ShapeDtypeStruct(keep.shape[1:], bf16),) * 4,
+        compiler_params=pltpu.CompilerParams(vmem_limit_bytes=VMEM_LIMIT),
+        name="add_last",
+    )(keep, c1, c2, c3)
+
+
+def pack_kernel(own, came, query, t0, t1, t2, t3):
     half = own.shape[1]
     for n, out in enumerate((t0, t1, t2, t3)):
         out[:half] = (own[n].astype(f32) + came[n].astype(f32)).astype(bf16)
-        out[half : 2 * half] = query[n]
-        total = keep[n] + c1[n].astype(f32) + c2[n].astype(f32) + c3[n].astype(f32)
-        out[2 * half] = total.astype(bf16)
-
-
-def pack_call(keep, c1, c2, c3, own, came, query):
+        out[half:] = query[n]
+
+
+def pack_call(own, came, query):
     half, *tile = own.shape[1:]
     return pl.pallas_call(
         pack_kernel,
-        out_shape=(jax.ShapeDtypeStruct((2 * half + 1, *tile), bf16),) * 4,
+        out_shape=(jax.ShapeDtypeStruct((2 * half, *tile), bf16),) * 4,
         compiler_params=pltpu.CompilerParams(vmem_limit_bytes=VMEM_LIMIT),
         name="pack",
-    )(keep, c1, c2, c3, own, came, query)
+    )(own, came, query)
 
 
 def group_kernel(
@@ -336,8 +349,33 @@
     )(group, gain, wq, wk, wv, wg, coef, *pieces)
 
 
-def pair_kernel(pair_ref, gain_ref, weight_ref, t0, t1, t2, t3, out_ref, grad, db):
-    _, _, _, _, y = place()
+def stats_kernel(pair_ref, xhat, recip):
+    def rows(step, carry):
+        x = pair_ref[pl.ds(step * 16, 16)].astype(f32).reshape(512, BLOCK)
+        centered = x - jnp.mean(x, axis=-1, keepdims=True)
+        reciprocal = lax.rsqrt(jnp.mean(centered * centered, axis=-1, keepdims=True) + EPS)
+        at = pl.ds(pl.multiple_of(step * 512, 512), 512)
+        xhat[at, :] = centered * reciprocal
+        recip[at, :] = jnp.broadcast_to(reciprocal, (512, BLOCK))
+        return carry
+
+    lax.fori_loop(0, 8, rows, 0)
+
+
+def stats_call(pair):
+    return pl.pallas_call(
+        stats_kernel,
+        out_shape=(jax.ShapeDtypeStruct((4096, BLOCK), f32),) * 2,
+        compiler_params=pltpu.CompilerParams(vmem_limit_bytes=VMEM_LIMIT),
+        cost_estimate=pl.CostEstimate(
+            flops=10_000_000, bytes_accessed=5_000_000, transcendentals=4096
+        ),
+        name="pair_stats",
+    )(pair)
+
+
+def pair_kernel(xhat, recip, gain_ref, weight_ref, t0, t1, t2, t3, out_ref, grad, db):
+    y = lax.axis_index("y")
     weight = jnp.concatenate(
         [weight_ref[...].astype(f32), jnp.zeros((8 - HEADS, BLOCK), f32)], axis=0
     ) * gain_ref[...]
@@ -345,10 +383,9 @@
     high, low = split_high_low(weight)
     weights = jnp.concatenate([high, high, low, jnp.zeros((8, BLOCK), bf16)], axis=0)
     db[...] = jnp.zeros_like(db)
-    last = t0.shape[0] - 1
     for step, t in enumerate((t0, t1, t2, t3)):
         h = lax.rem(y + step, 4)
-        value = t[last].astype(f32)
+        value = t[...].astype(f32)
         for k in range(32):
             db[k, pl.ds(h, 1), :] = value[k : k + 1]
 
@@ -360,30 +397,27 @@
         )
 
     def rows(step, carry):
-        x = pair_ref[pl.ds(step * 16, 16)].astype(f32).reshape(512, BLOCK)
-        centered = x - jnp.mean(x, axis=-1, keepdims=True)
-        reciprocal = lax.rsqrt(jnp.mean(centered * centered, axis=-1, keepdims=True) + EPS)
-        normalized = centered * reciprocal
-        scaled = grad[pl.ds(pl.multiple_of(step * 512, 512), 512), :]
+        at = pl.ds(pl.multiple_of(step * 512, 512), 512)
+        scaled, normalized = grad[at, :], xhat[at, :]
         second = jnp.mean(scaled * normalized, axis=-1, keepdims=True)
-        result = reciprocal * (scaled - normalized * second)
+        result = recip[at, :] * (scaled - normalized * second)
         out_ref[pl.ds(step * 16, 16)] = result.astype(bf16).reshape(16, 32, BLOCK)
         return carry
 
     lax.fori_loop(0, 8, rows, 0)
 
 
-def pair_call(pair, gain, weight, pieces):
+def pair_call(shape, stats, gain, weight, pieces):
     return pl.pallas_call(
         pair_kernel,
-        out_shape=jax.ShapeDtypeStruct(pair.shape, bf16),
+        out_shape=jax.ShapeDtypeStruct(shape, bf16),
         scratch_shapes=[pltpu.VMEM((4096, BLOCK), f32), pltpu.VMEM((32, 8, BLOCK), f32)],
         compiler_params=pltpu.CompilerParams(vmem_limit_bytes=VMEM_LIMIT),
         cost_estimate=pl.CostEstimate(
-            flops=60_000_000, bytes_accessed=2_200_000, transcendentals=4096
+            flops=60_000_000, bytes_accessed=5_200_000, transcendentals=0
         ),
         name="pair_backward",
-    )(pair, gain, weight, *pieces)
+    )(*stats, gain, weight, *pieces)
 
 
 def along(value, axis, step):
@@ -421,13 +455,18 @@
 
     first = add_core(keep, along(send, "core", 1))
     came = along(out_other, "z", 1)
-    second = add_four(first[0], *(along(first[d], "x", -d) for d in range(1, 4)))
+    sums = [along(first[d], "x", -d) for d in range(1, 4)]
+    packed = pack_call(out_own, came, out_q)
+    sums, packed = lax.optimization_barrier((sums, packed))
+    second = add_four(first[0], *sums)
+    back = [packed[0]] + [along(packed[d], "y", -d) for d in range(1, 4)]
     third = [along(second[d], "zh", -d) for d in range(1, 4)]
-    packed = pack_call(second[0], *third, out_own, came, out_q)
-    back = [packed[0]] + [along(packed[d], "y", -d) for d in range(1, 4)]
+    third, back = lax.optimization_barrier((third, back))
+    last = add_last(second[0], *third)
+    last = [last[0]] + [along(last[d], "y", -d) for d in range(1, 4)]
 
     grad_group = group_call(group, gain, w_query, w_key, w_value, w_gate, coef, back)
-    grad_pair = pair_call(pair, gain, w_bias.T, back)
+    grad_pair = pair_call(pair.shape, stats_call(pair), gain, w_bias.T, last)
     return (grad_group, grad_pair)
 
 

time: 106 us -> 101 us (0.953)
  waiting for transfers between devices: 36.1 us -> 30.8 us
  Pallas kernels: 26.9 us -> 23.7 us
  starting transfers between devices: 39 us -> 42 us
    ppermute x25 -> x28, waiting for transfers between devices: 36.1 us -> 30.8 us  [along(): lax.ppermute(value, axis, [(p, (p + step) % size) for p in range(size)])]
    pallas_call x1, Pallas kernels: 15.4 us -> 11.6 us  [attention_call(): pl.pallas_call(attention_kernel, out_shape=(part, part, part, jax.ShapeDt...]
    ppermute x25 -> x28, starting transfers between devices: 39 us -> 42 us  [along(): lax.ppermute(value, axis, [(p, (p + step) % size) for p in range(size)])]
    unnamed x28 -> x32, local copies, waits for them, and re-layouts: 2.54 us -> 3.26 us
    pallas_call x2 -> x4, Pallas kernels: 5.54 us -> 6.16 us  [the longest x1 4.21 us: pair_call(): pl.pallas_call(pair_kernel, out_shape=jax.ShapeDtypeStruct(shape, bf16),...]
  transfers between devices with their start and end apart: 25 -> 28, of which waited for: 18 -> 19; matrix products, arithmetic and copies ran while one was open for 0% -> 0% of each run, Pallas kernels for 0% -> 4%
where the time goes in v6:
time: 101 us
  starting transfers between devices  42 us (42%)
  waiting for transfers between devices  30.8 us (30%)
  Pallas kernels  23.7 us (23%)
  local copies, waits for them, and re-layouts  3.29 us (3%)
    ppermute x28, starting transfers between devices, along(): lax.ppermute(value, axis, [(p, (p + step) % size) for p in range(size)])  42 us
    ppermute x28, waiting for transfers between devices, along(): lax.ppermute(value, axis, [(p, (p + step) % size) for p in range(size)])  30.8 us
    pallas_call x1, Pallas kernels, attention_call(): pl.pallas_call(attention_kernel, out_shape=(part, part, part, jax.ShapeDt...  11.6 us
    pallas_call x1, Pallas kernels, pair_call(): pl.pallas_call(pair_kernel, out_shape=jax.ShapeDtypeStruct(shape, bf16),...  4.21 us
    unnamed x32, local copies, waits for them, and re-layouts  3.26 us
    pallas_call x1, Pallas kernels, bias_call(): pl.pallas_call(bias_kernel, out_shape=jax.ShapeDtypeStruct((HEADS, 32, BL...  3.13 us
  transfers between devices with their start and end apart: 28, of which 19 were waited for; matrix products, arithmetic and copies ran while one was open for 0% of the time, Pallas kernels for 4%

profile of v6, /device:TPU:32, one launch (start us, length us, event | category | flops | bytes accessed | tf_op | source)
XLA Modules:
  0.0 100.8 jit_solution(17740273620526601643)
XLA Ops:
  3.9 3.1 %pair_bias.1.g0 = bf16[4,32,128]{2,1,0:T(8,128)(2,1)S(1)} custom-call(bf16[128,32,128]{2,1,0:T(8,128)(2,1)S(1)} %copy-done, f32[1,128]{1,0:T(1,128)S(1)} %bitcast.22, f32[1,128]{1,0:T(1,128)S(1)} %bitcast.28, bf16[4,128]{1,0:T(4,128)(2,1)S(1)} %bitcast.26), custom_call_target="tpu_custom_call" | custom-call | flops 3500000000 | bytes 1200000 | tf_op jit(solution)/shard_map/pair_bias/pallas_call | solution.py:56
  8.1 1.7 %collective-permute-start.3 = (bf16[20,32,128]{2,1,0:T(8,128)(2,1)S(1)}, bf16[20,32,128]{2,1,0:T(8,128)(2,1)S(1)}, u32[]{:S(2)}, u32[]{:S(2)}) collective-permute-start(bf16[20,32,128]{2,1,0:T(8,128)(2,1)S(1)} %get-tuple-element.73), channel_id=1, source_target_pairs={{0,1},{1,2},{2,3},{3,0},{4,5},{5,6},{6,7},{7,4},{8,9},{9,10},{10,1... | collective-permute-start | bytes 491528 | tf_op jit(solution)/shard_map/ppermute | solution.py:425
  9.7 2.9 %collective-permute-start.4 = (bf16[20,32,128]{2,1,0:T(8,128)(2,1)S(1)}, bf16[20,32,128]{2,1,0:T(8,128)(2,1)S(1)}, u32[]{:S(2)}, u32[]{:S(2)}) collective-permute-start(bf16[20,32,128]{2,1,0:T(8,128)(2,1)S(1)} %get-tuple-element.74), channel_id=1, source_target_pairs={{0,2},{1,3},{2,0},{3,1},{4,6},{5,7},{6,4},{7,5},{8,10},{9,11},{10,... | collective-permute-start | bytes 491528 | tf_op jit(solution)/shard_map/ppermute | solution.py:425
  14.0 5.4 %collective-permute-start.2 = (bf16[4,32,128]{2,1,0:T(8,128)(2,1)S(1)}, bf16[4,32,128]{2,1,0:T(8,128)(2,1)S(1)}, u32[]{:S(2)}, u32[]{:S(2)}) collective-permute-start(bf16[4,32,128]{2,1,0:T(8,128)(2,1)S(1)} %pair_bias.1.g0), channel_id=1, source_target_pairs={{0,48},{16,0},{32,16},{48,32},{1,49},{17,1},{33,17},{49,33},{2,50}... | collective-permute-start | bytes 98312 | tf_op jit(solution)/shard_map/ppermute | solution.py:425
  21.0 2.6 %collective-permute-start = (bf16[4,32,128]{2,1,0:T(8,128)(2,1)S(1)}, bf16[4,32,128]{2,1,0:T(8,128)(2,1)S(1)}, u32[]{:S(2)}, u32[]{:S(2)}) collective-permute-start(bf16[4,32,128]{2,1,0:T(8,128)(2,1)S(1)} %pair_bias.1.g0), channel_id=1, source_target_pairs={{0,16},{16,32},{32,48},{48,0},{1,17},{17,33},{33,49},{49,1},{2,18}... | collective-permute-start | bytes 98312 | tf_op jit(solution)/shard_map/ppermute | solution.py:425
  23.6 3.6 %collective-permute-done.1.g2 = bf16[4,32,128]{2,1,0:T(8,128)(2,1)S(1)} collective-permute-done((bf16[4,32,128]{2,1,0:T(8,128)(2,1)S(1)}, bf16[4,32,128]{2,1,0:T(8,128)(2,1)S(1)}, u32[]{:S(2)}, u32[]{:S(2)}) %collective-permute-start.1) | collective-permute-done | bytes 32800 | tf_op jit(solution)/shard_map/ppermute | solution.py:425
  30.6 1.5 %collective-permute-start.8 = (bf16[4,32,128]{2,1,0:T(8,128)(2,1)S(1)}, bf16[4,32,128]{2,1,0:T(8,128)(2,1)S(1)}, u32[]{:S(2)}, u32[]{:S(2)}) collective-permute-start(bf16[4,32,128]{2,1,0:T(8,128)(2,1)S(1)} %get-tuple-element.79), channel_id=1, source_target_pairs={{0,3},{1,0},{2,1},{3,2},{4,7},{5,4},{6,5},{7,6},{8,11},{9,8},{10,9... | collective-permute-start | bytes 98312 | tf_op jit(solution)/shard_map/ppermute | solution.py:425
  32.1 1.8 %collective-permute-done.6 = bf16[4,32,128]{2,1,0:T(8,128)(2,1)S(1)} collective-permute-done((bf16[4,32,128]{2,1,0:T(8,128)(2,1)S(1)}, bf16[4,32,128]{2,1,0:T(8,128)(2,1)S(1)}, u32[]{:S(2)}, u32[]{:S(2)}) %collective-permute-start.6) | collective-permute-done | bytes 32800 | tf_op jit(solution)/shard_map/ppermute | solution.py:425
  35.1 2.8 %collective-permute-start.11 = (bf16[4,4,32,128]{3,2,1,0:T(8,128)(2,1)S(1)}, bf16[4,4,32,128]{3,2,1,0:T(8,128)(2,1)S(1)}, u32[]{:S(2)}, u32[]{:S(2)}) collective-permute-start(bf16[4,4,32,128]{3,2,1,0:T(8,128)(2,1)S(1)} %pad_maximum_fusion.2), channel_id=1, source_target_pairs={{0,192},{64,0},{128,64},{192,128},{1,193},{65,1},{129,65},{193,129... | collective-permute-start | bytes 393224 | tf_op jit(solution)/shard_map/ppermute | solution.py:425
  39.7 2.2 %collective-permute-done.11 = bf16[4,4,32,128]{3,2,1,0:T(8,128)(2,1)S(1)} collective-permute-done((bf16[4,4,32,128]{3,2,1,0:T(8,128)(2,1)S(1)}, bf16[4,4,32,128]{3,2,1,0:T(8,128)(2,1)S(1)}, u32[]{:S(2)}, u32[]{:S(2)}) %collective-permute-start.11) | collective-permute-done | bytes 131104 | tf_op jit(solution)/shard_map/ppermute | solution.py:425
  41.9 2.6 %collective-permute-done.10 = bf16[4,4,32,128]{3,2,1,0:T(8,128)(2,1)S(1)} collective-permute-done((bf16[4,4,32,128]{3,2,1,0:T(8,128)(2,1)S(1)}, bf16[4,4,32,128]{3,2,1,0:T(8,128)(2,1)S(1)}, u32[]{:S(2)}, u32[]{:S(2)}) %collective-permute-start.10) | collective-permute-done | bytes 131104 | tf_op jit(solution)/shard_map/ppermute | solution.py:425
  46.2 1.9 %collective-permute-done.13.bias_other = bf16[4,4,4,32,128]{4,3,2,1,0:T(8,128)(2,1)S(1)} collective-permute-done((bf16[4,4,4,32,128]{4,3,2,1,0:T(8,128)(2,1)S(1)}, bf16[4,4,4,32,128]{4,3,2,1,0:T(8,128)(2,1)S(1)}, u32[]{:S(2)}, u32[]{:S(2)}) %collective-permute-start.13) | collective-permute-done | bytes 524320 | tf_op jit(solution)/shard_map/ppermute | solution.py:425
  48.1 11.6 %attention.1 = (bf16[4,10,32,128]{3,2,1,0:T(8,128)(2,1)S(1)}, bf16[4,10,32,128]{3,2,1,0:T(8,128)(2,1)S(1)}, bf16[4,10,32,128]{3,2,1,0:T(8,128)(2,1)S(1)}, f32[4,...) custom-call(s32[8,128]{1,0:T(8,128)S(1)} %bitcast.31, ...), custom_call_target="tpu_custom_call" | custom-call | flops 8000000000 | bytes 6000000 | tf_op jit(solution)/shard_map/attention/pallas_call | solution.py:216
  64.1 5.8 %collective-permute-done.18.came = bf16[4,10,32,128]{3,2,1,0:T(8,128)(2,1)S(1)} collective-permute-done((bf16[4,10,32,128]{3,2,1,0:T(8,128)(2,1)S(1)}, bf16[4,10,32,128]{3,2,1,0:T(8,128)(2,1)S(1)}, u32[]{:S(2)}, u32[]{:S(2)}) %collective-permute-start.18) | collective-permute-done | bytes 327712 | tf_op jit(solution)/shard_map/ppermute | solution.py:425
  70.3 1.7 %collective-permute-done.17.c3 = bf16[4,4,32,128]{3,2,1,0:T(8,128)(2,1)S(1)} collective-permute-done((bf16[4,4,32,128]{3,2,1,0:T(8,128)(2,1)S(1)}, bf16[4,4,32,128]{3,2,1,0:T(8,128)(2,1)S(1)}, u32[]{:S(2)}, u32[]{:S(2)}) %collective-permute-start.17) | collective-permute-done | bytes 131104 | tf_op jit(solution)/shard_map/ppermute | solution.py:425
  72.0 2.5 %collective-permute-start.22 = (bf16[20,32,128]{2,1,0:T(8,128)(2,1)S(1)}, bf16[20,32,128]{2,1,0:T(8,128)(2,1)S(1)}, u32[]{:S(2)}, u32[]{:S(2)}) collective-permute-start(bf16[20,32,128]{2,1,0:T(8,128)(2,1)S(1)} %get-tuple-element.109), channel_id=1, source_target_pairs={{0,3},{1,0},{2,1},{3,2},{4,7},{5,4},{6,5},{7,6},{8,11},{9,8},{10,9... | collective-permute-start | bytes 491528 | tf_op jit(solution)/shard_map/ppermute | solution.py:425
  75.8 2.7 %collective-permute-start.19 = (bf16[4,32,128]{2,1,0:T(8,128)(2,1)S(1)}, bf16[4,32,128]{2,1,0:T(8,128)(2,1)S(1)}, u32[]{:S(2)}, u32[]{:S(2)}) collective-permute-start(bf16[4,32,128]{2,1,0:T(8,128)(2,1)S(1)} %get-tuple-element.105), channel_id=1, source_target_pairs={{0,48},{16,0},{32,16},{48,32},{1,49},{17,1},{33,17},{49,33},{2,50}... | collective-permute-start | bytes 98312 | tf_op jit(solution)/shard_map/ppermute | solution.py:425
  81.1 1.8 %collective-permute-start.21 = (bf16[4,32,128]{2,1,0:T(8,128)(2,1)S(1)}, bf16[4,32,128]{2,1,0:T(8,128)(2,1)S(1)}, u32[]{:S(2)}, u32[]{:S(2)}) collective-permute-start(bf16[4,32,128]{2,1,0:T(8,128)(2,1)S(1)} %get-tuple-element.107), channel_id=1, source_target_pairs={{0,16},{16,32},{32,48},{48,0},{1,17},{17,33},{33,49},{49,1},{2,18}... | collective-permute-start | bytes 98312 | tf_op jit(solution)/shard_map/ppermute | solution.py:425
  82.8 1.8 %pair_stats.1 = (f32[4096,128]{1,0:T(8,128)S(1)}, f32[4096,128]{1,0:T(8,128)S(1)}) custom-call(bf16[128,32,128]{2,1,0:T(8,128)(2,1)S(1)} %copy-done.1), custom_call_target="tpu_custom_call" | custom-call | flops 10000000 | bytes 5000000 | tf_op jit(solution)/shard_map/pair_stats/pallas_call | solution.py:366
  84.7 1.9 %collective-permute-done.20.c2 = bf16[4,32,128]{2,1,0:T(8,128)(2,1)S(1)} collective-permute-done((bf16[4,32,128]{2,1,0:T(8,128)(2,1)S(1)}, bf16[4,32,128]{2,1,0:T(8,128)(2,1)S(1)}, u32[]{:S(2)}, u32[]{:S(2)}) %collective-permute-start.20) | collective-permute-done | bytes 32800 | tf_op jit(solution)/shard_map/ppermute | solution.py:425
  87.7 3.0 %collective-permute-start.25 = (bf16[32,128]{1,0:T(8,128)(2,1)S(1)}, bf16[32,128]{1,0:T(8,128)(2,1)S(1)}, u32[]{:S(2)}, u32[]{:S(2)}) collective-permute-start(bf16[32,128]{1,0:T(8,128)(2,1)S(1)} %get-tuple-element.123), channel_id=1, source_target_pairs={{0,3},{1,0},{2,1},{3,2},{4,7},{5,4},{6,5},{7,6},{8,11},{9,8},{10,9... | collective-permute-start | bytes 24584 | tf_op jit(solution)/shard_map/ppermute | solution.py:425
  91.8 1.7 %group_backward.1 = bf16[5,128,128]{2,1,0:T(8,128)(2,1)} custom-call(bf16[5,128,128]{2,1,0:T(8,128)(2,1)S(1)} %copy-done.2, f32[1,128]{1,0:T(1,128)S(1)} %bitcast.24, bf16[128,128]{1,0:T(8,128)(2,1)S(1)} %copy-done.4, bf16[128,128]{1,0:T(8,128)(2,1)S(1)} %copy-done.5, bf16[128,128]{1,0:T(8,128)(2,1)S(1)} %copy-done.6, bf16[128,128]{1,0:T(8,128)(2,1)S(1)} %copy-done.7, ...), custom_call_target="tpu_custom_call" | custom-call | flops 160000000 | bytes 2000000 | tf_op jit(solution)/shard_map/group_backward/pallas_call | solution.py:341
  93.5 2.2 %collective-permute-done.26.t2 = bf16[32,128]{1,0:T(8,128)(2,1)S(1)} collective-permute-done((bf16[32,128]{1,0:T(8,128)(2,1)S(1)}, bf16[32,128]{1,0:T(8,128)(2,1)S(1)}, u32[]{:S(2)}, u32[]{:S(2)}) %collective-permute-start.26) | collective-permute-done | bytes 8224 | tf_op jit(solution)/shard_map/ppermute | solution.py:425
  96.6 4.2 %pair_backward.1 = bf16[128,32,128]{2,1,0:T(8,128)(2,1)} custom-call(f32[4096,128]{1,0:T(8,128)S(1)} %get-tuple-element.116.xhat, f32[4096,128]{1,0:T(8,128)S(1)} %get-tuple-element.117.recip, f32[1,128]{1,0:T(1,128)S(1)} %bitcast.25, bf16[4,128]{1,0:T(4,128)(2,1)S(1)} %bitcast.27, bf16[32,128]{1,0:T(8,128)(2,1)S(1)} %get-tuple-element.122.t0, ...), custom_call_target="tpu_custom_call" | custom-call | flops 60000000 | bytes 5200000 | tf_op jit(solution)/shard_map/pair_backward/pallas_call | solution.py:411
  (80 shorter events, 26.7 us)
Async XLA Ops:
  8.1 19.2 %collective-permute-start.3 = (bf16[20,32,128]{2,1,0:T(8,128)(2,1)S(1)}, bf16[20,32,128]{2,1,0:T(8,128)(2,1)S(1)}, u32[]{:S(2)}, u32[]{:S(2)}) collective-permute-start(bf16[20,32,128]{2,1,0:T(8,128)(2,1)S(1)} %get-tuple-element.73), channel_id=1, source_target_pairs={{0,1},{1,2},{2,3},{3,0},{4,5},{5,6},{6,7},{7,4},{8,9},{9,10},{10,1... | collective-permute-start | bytes 491528 | tf_op jit(solution)/shard_map/ppermute | solution.py:425
  9.7 17.6 %collective-permute-start.4 = (bf16[20,32,128]{2,1,0:T(8,128)(2,1)S(1)}, bf16[20,32,128]{2,1,0:T(8,128)(2,1)S(1)}, u32[]{:S(2)}, u32[]{:S(2)}) collective-permute-start(bf16[20,32,128]{2,1,0:T(8,128)(2,1)S(1)} %get-tuple-element.74), channel_id=1, source_target_pairs={{0,2},{1,3},{2,0},{3,1},{4,6},{5,7},{6,4},{7,5},{8,10},{9,11},{10,... | collective-permute-start | bytes 491528 | tf_op jit(solution)/shard_map/ppermute | solution.py:425
  12.6 14.7 %collective-permute-start.5 = (bf16[20,32,128]{2,1,0:T(8,128)(2,1)S(1)}, bf16[20,32,128]{2,1,0:T(8,128)(2,1)S(1)}, u32[]{:S(2)}, u32[]{:S(2)}) collective-permute-start(bf16[20,32,128]{2,1,0:T(8,128)(2,1)S(1)} %get-tuple-element.75), channel_id=1, source_target_pairs={{0,3},{1,0},{2,1},{3,2},{4,7},{5,4},{6,5},{7,6},{8,11},{9,8},{10,9... | collective-permute-start | bytes 491528 | tf_op jit(solution)/shard_map/ppermute | solution.py:425
  14.0 7.0 %collective-permute-start.2 = (bf16[4,32,128]{2,1,0:T(8,128)(2,1)S(1)}, bf16[4,32,128]{2,1,0:T(8,128)(2,1)S(1)}, u32[]{:S(2)}, u32[]{:S(2)}) collective-permute-start(bf16[4,32,128]{2,1,0:T(8,128)(2,1)S(1)} %pair_bias.1.g0), channel_id=1, source_target_pairs={{0,48},{16,0},{32,16},{48,32},{1,49},{17,1},{33,17},{49,33},{2,50}... | collective-permute-start | bytes 98312 | tf_op jit(solution)/shard_map/ppermute | solution.py:425
  19.4 7.8 %collective-permute-start.1 = (bf16[4,32,128]{2,1,0:T(8,128)(2,1)S(1)}, bf16[4,32,128]{2,1,0:T(8,128)(2,1)S(1)}, u32[]{:S(2)}, u32[]{:S(2)}) collective-permute-start(bf16[4,32,128]{2,1,0:T(8,128)(2,1)S(1)} %pair_bias.1.g0), channel_id=1, source_target_pairs={{0,32},{16,48},{32,0},{48,16},{1,33},{17,49},{33,1},{49,17},{2,34}... | collective-permute-start | bytes 98312 | tf_op jit(solution)/shard_map/ppermute | solution.py:425
  21.0 6.3 %collective-permute-start = (bf16[4,32,128]{2,1,0:T(8,128)(2,1)S(1)}, bf16[4,32,128]{2,1,0:T(8,128)(2,1)S(1)}, u32[]{:S(2)}, u32[]{:S(2)}) collective-permute-start(bf16[4,32,128]{2,1,0:T(8,128)(2,1)S(1)} %pair_bias.1.g0), channel_id=1, source_target_pairs={{0,16},{16,32},{32,48},{48,0},{1,17},{17,33},{33,49},{49,1},{2,18}... | collective-permute-start | bytes 98312 | tf_op jit(solution)/shard_map/ppermute | solution.py:425
  27.4 18.4 %collective-permute-start.12 = (bf16[4,10,32,128]{3,2,1,0:T(8,128)(2,1)S(1)}, bf16[4,10,32,128]{3,2,1,0:T(8,128)(2,1)S(1)}, u32[]{:S(2)}, u32[]{:S(2)}) collective-permute-start(bf16[4,10,32,128]{3,2,1,0:T(8,128)(2,1)S(1)} %pad_maximum_fusion.1), channel_id=1, source_target_pairs={{0,4},{4,0},{1,5},{5,1},{2,6},{6,2},{3,7},{7,3},{8,12},{12,8},{9,1... | collective-permute-start | bytes 983048 | tf_op jit(solution)/shard_map/ppermute | solution.py:425
  28.8 5.1 %collective-permute-start.6 = (bf16[4,32,128]{2,1,0:T(8,128)(2,1)S(1)}, bf16[4,32,128]{2,1,0:T(8,128)(2,1)S(1)}, u32[]{:S(2)}, u32[]{:S(2)}) collective-permute-start(bf16[4,32,128]{2,1,0:T(8,128)(2,1)S(1)} %get-tuple-element.77), channel_id=1, source_target_pairs={{0,1},{1,2},{2,3},{3,0},{4,5},{5,6},{6,7},{7,4},{8,9},{9,10},{10,1... | collective-permute-start | bytes 98312 | tf_op jit(solution)/shard_map/ppermute | solution.py:425
  29.4 5.4 %collective-permute-start.7 = (bf16[4,32,128]{2,1,0:T(8,128)(2,1)S(1)}, bf16[4,32,128]{2,1,0:T(8,128)(2,1)S(1)}, u32[]{:S(2)}, u32[]{:S(2)}) collective-permute-start(bf16[4,32,128]{2,1,0:T(8,128)(2,1)S(1)} %get-tuple-element.78), channel_id=1, source_target_pairs={{0,2},{1,3},{2,0},{3,1},{4,6},{5,7},{6,4},{7,5},{8,10},{9,11},{10,... | collective-permute-start | bytes 98312 | tf_op jit(solution)/shard_map/ppermute | solution.py:425
  35.1 6.8 %collective-permute-start.11 = (bf16[4,4,32,128]{3,2,1,0:T(8,128)(2,1)S(1)}, bf16[4,4,32,128]{3,2,1,0:T(8,128)(2,1)S(1)}, u32[]{:S(2)}, u32[]{:S(2)}) collective-permute-start(bf16[4,4,32,128]{3,2,1,0:T(8,128)(2,1)S(1)} %pad_maximum_fusion.2), channel_id=1, source_target_pairs={{0,192},{64,0},{128,64},{192,128},{1,193},{65,1},{129,65},{193,129... | collective-permute-start | bytes 393224 | tf_op jit(solution)/shard_map/ppermute | solution.py:425
  38.0 6.6 %collective-permute-start.10 = (bf16[4,4,32,128]{3,2,1,0:T(8,128)(2,1)S(1)}, bf16[4,4,32,128]{3,2,1,0:T(8,128)(2,1)S(1)}, u32[]{:S(2)}, u32[]{:S(2)}) collective-permute-start(bf16[4,4,32,128]{3,2,1,0:T(8,128)(2,1)S(1)} %pad_maximum_fusion.2), channel_id=1, source_target_pairs={{0,128},{64,192},{128,0},{192,64},{1,129},{65,193},{129,1},{193,65... | collective-permute-start | bytes 393224 | tf_op jit(solution)/shard_map/ppermute | solution.py:425
  38.8 7.1 %collective-permute-start.9 = (bf16[4,4,32,128]{3,2,1,0:T(8,128)(2,1)S(1)}, bf16[4,4,32,128]{3,2,1,0:T(8,128)(2,1)S(1)}, u32[]{:S(2)}, u32[]{:S(2)}) collective-permute-start(bf16[4,4,32,128]{3,2,1,0:T(8,128)(2,1)S(1)} %pad_maximum_fusion.2), channel_id=1, source_target_pairs={{0,64},{64,128},{128,192},{192,0},{1,65},{65,129},{129,193},{193,1... | collective-permute-start | bytes 393224 | tf_op jit(solution)/shard_map/ppermute | solution.py:425
  59.9 10.0 %collective-permute-start.18 = (bf16[4,10,32,128]{3,2,1,0:T(8,128)(2,1)S(1)}, bf16[4,10,32,128]{3,2,1,0:T(8,128)(2,1)S(1)}, u32[]{:S(2)}, u32[]{:S(2)}) collective-permute-start(bf16[4,10,32,128]{3,2,1,0:T(8,128)(2,1)S(1)} %get-tuple-element.96), channel_id=1, source_target_pairs={{0,4},{4,0},{1,5},{5,1},{2,6},{6,2},{3,7},{7,3},{8,12},{12,8},{9,1... | collective-permute-start | bytes 983048 | tf_op jit(solution)/shard_map/ppermute | solution.py:425
  61.8 8.2 %collective-permute-start.15 = (bf16[4,4,32,128]{3,2,1,0:T(8,128)(2,1)S(1)}, bf16[4,4,32,128]{3,2,1,0:T(8,128)(2,1)S(1)}, u32[]{:S(2)}, u32[]{:S(2)}) collective-permute-start(bf16[4,4,32,128]{3,2,1,0:T(8,128)(2,1)S(1)} %get-tuple-element.92), channel_id=1, source_target_pairs={{0,192},{64,0},{128,64},{192,128},{1,193},{65,1},{129,65},{193,129... | collective-permute-start | bytes 393224 | tf_op jit(solution)/shard_map/ppermute | solution.py:425
  62.5 7.8 %collective-permute-start.16 = (bf16[4,4,32,128]{3,2,1,0:T(8,128)(2,1)S(1)}, bf16[4,4,32,128]{3,2,1,0:T(8,128)(2,1)S(1)}, u32[]{:S(2)}, u32[]{:S(2)}) collective-permute-start(bf16[4,4,32,128]{3,2,1,0:T(8,128)(2,1)S(1)} %get-tuple-element.93), channel_id=1, source_target_pairs={{0,128},{64,192},{128,0},{192,64},{1,129},{65,193},{129,1},{193,65... | collective-permute-start | bytes 393224 | tf_op jit(solution)/shard_map/ppermute | solution.py:425
  63.2 8.8 %collective-permute-start.17 = (bf16[4,4,32,128]{3,2,1,0:T(8,128)(2,1)S(1)}, bf16[4,4,32,128]{3,2,1,0:T(8,128)(2,1)S(1)}, u32[]{:S(2)}, u32[]{:S(2)}) collective-permute-start(bf16[4,4,32,128]{3,2,1,0:T(8,128)(2,1)S(1)} %get-tuple-element.94), channel_id=1, source_target_pairs={{0,64},{64,128},{128,192},{192,0},{1,65},{65,129},{129,193},{193,1... | collective-permute-start | bytes 393224 | tf_op jit(solution)/shard_map/ppermute | solution.py:425
  72.0 15.6 %collective-permute-start.22 = (bf16[20,32,128]{2,1,0:T(8,128)(2,1)S(1)}, bf16[20,32,128]{2,1,0:T(8,128)(2,1)S(1)}, u32[]{:S(2)}, u32[]{:S(2)}) collective-permute-start(bf16[20,32,128]{2,1,0:T(8,128)(2,1)S(1)} %get-tuple-element.109), channel_id=1, source_target_pairs={{0,3},{1,0},{2,1},{3,2},{4,7},{5,4},{6,5},{7,6},{8,11},{9,8},{10,9... | collective-permute-start | bytes 491528 | tf_op jit(solution)/shard_map/ppermute | solution.py:425
  74.5 13.1 %collective-permute-start.23 = (bf16[20,32,128]{2,1,0:T(8,128)(2,1)S(1)}, bf16[20,32,128]{2,1,0:T(8,128)(2,1)S(1)}, u32[]{:S(2)}, u32[]{:S(2)}) collective-permute-start(bf16[20,32,128]{2,1,0:T(8,128)(2,1)S(1)} %get-tuple-element.110), channel_id=1, source_target_pairs={{0,2},{1,3},{2,0},{3,1},{4,6},{5,7},{6,4},{7,5},{8,10},{9,11},{10,... | collective-permute-start | bytes 491528 | tf_op jit(solution)/shard_map/ppermute | solution.py:425
  75.8 11.9 %collective-permute-start.24 = (bf16[20,32,128]{2,1,0:T(8,128)(2,1)S(1)}, bf16[20,32,128]{2,1,0:T(8,128)(2,1)S(1)}, u32[]{:S(2)}, u32[]{:S(2)}) collective-permute-start(bf16[20,32,128]{2,1,0:T(8,128)(2,1)S(1)} %get-tuple-element.111), channel_id=1, source_target_pairs={{0,1},{1,2},{2,3},{3,0},{4,5},{5,6},{6,7},{7,4},{8,9},{9,10},{10,1... | collective-permute-start | bytes 491528 | tf_op jit(solution)/shard_map/ppermute | solution.py:425
  75.8 5.2 %collective-permute-start.19 = (bf16[4,32,128]{2,1,0:T(8,128)(2,1)S(1)}, bf16[4,32,128]{2,1,0:T(8,128)(2,1)S(1)}, u32[]{:S(2)}, u32[]{:S(2)}) collective-permute-start(bf16[4,32,128]{2,1,0:T(8,128)(2,1)S(1)} %get-tuple-element.105), channel_id=1, source_target_pairs={{0,48},{16,0},{32,16},{48,32},{1,49},{17,1},{33,17},{49,33},{2,50}... | collective-permute-start | bytes 98312 | tf_op jit(solution)/shard_map/ppermute | solution.py:425
  78.5 8.0 %collective-permute-start.20 = (bf16[4,32,128]{2,1,0:T(8,128)(2,1)S(1)}, bf16[4,32,128]{2,1,0:T(8,128)(2,1)S(1)}, u32[]{:S(2)}, u32[]{:S(2)}) collective-permute-start(bf16[4,32,128]{2,1,0:T(8,128)(2,1)S(1)} %get-tuple-element.106), channel_id=1, source_target_pairs={{0,32},{16,48},{32,0},{48,16},{1,33},{17,49},{33,1},{49,17},{2,34}... | collective-permute-start | bytes 98312 | tf_op jit(solution)/shard_map/ppermute | solution.py:425
  81.1 6.6 %collective-permute-start.21 = (bf16[4,32,128]{2,1,0:T(8,128)(2,1)S(1)}, bf16[4,32,128]{2,1,0:T(8,128)(2,1)S(1)}, u32[]{:S(2)}, u32[]{:S(2)}) collective-permute-start(bf16[4,32,128]{2,1,0:T(8,128)(2,1)S(1)} %get-tuple-element.107), channel_id=1, source_target_pairs={{0,16},{16,32},{32,48},{48,0},{1,17},{17,33},{33,49},{49,1},{2,18}... | collective-permute-start | bytes 98312 | tf_op jit(solution)/shard_map/ppermute | solution.py:425
  87.7 5.9 %collective-permute-start.25 = (bf16[32,128]{1,0:T(8,128)(2,1)S(1)}, bf16[32,128]{1,0:T(8,128)(2,1)S(1)}, u32[]{:S(2)}, u32[]{:S(2)}) collective-permute-start(bf16[32,128]{1,0:T(8,128)(2,1)S(1)} %get-tuple-element.123), channel_id=1, source_target_pairs={{0,3},{1,0},{2,1},{3,2},{4,7},{5,4},{6,5},{7,6},{8,11},{9,8},{10,9... | collective-permute-start | bytes 24584 | tf_op jit(solution)/shard_map/ppermute | solution.py:425
  90.6 5.2 %collective-permute-start.26 = (bf16[32,128]{1,0:T(8,128)(2,1)S(1)}, bf16[32,128]{1,0:T(8,128)(2,1)S(1)}, u32[]{:S(2)}, u32[]{:S(2)}) collective-permute-start(bf16[32,128]{1,0:T(8,128)(2,1)S(1)} %get-tuple-element.124), channel_id=1, source_target_pairs={{0,2},{1,3},{2,0},{3,1},{4,6},{5,7},{6,4},{7,5},{8,10},{9,11},{10,... | collective-permute-start | bytes 24584 | tf_op jit(solution)/shard_map/ppermute | solution.py:425
  (20 other events, 163.5 us)

commit v7 on v6

--- a/solution.py
+++ b/solution.py
@@ -190,7 +190,8 @@
         key_out[i, 1] = both[HEAD_DIM:]
         return carry
 
-    lax.fori_loop(0, rows, row, 0)
+    for i in range(rows):
+        row(i, 0)
 
     for step in range(4):
         yy = lax.rem(y - step + 4, 4)

time: 101 us -> 99.6 us (0.986)
  Pallas kernels: 23.7 us -> 22.3 us
    pallas_call x1, Pallas kernels: 11.6 us -> 10.2 us  [attention_call(): pl.pallas_call(attention_kernel, out_shape=(part, part, part, jax.ShapeDt...]
where the time goes in v7:
time: 99.6 us; the launch traced here: 99.5 us
  starting transfers between devices  42 us (42%)
  waiting for transfers between devices  30.8 us (31%)
  Pallas kernels  22.3 us (22%)
  local copies, waits for them, and re-layouts  3.29 us (3%)
    ppermute x28, starting transfers between devices, along(): lax.ppermute(value, axis, [(p, (p + step) % size) for p in range(size)])  42 us
    ppermute x28, waiting for transfers between devices, along(): lax.ppermute(value, axis, [(p, (p + step) % size) for p in range(size)])  30.8 us
    pallas_call x1, Pallas kernels, attention_call(): pl.pallas_call(attention_kernel, out_shape=(part, part, part, jax.ShapeDt...  10.2 us
    pallas_call x1, Pallas kernels, pair_call(): pl.pallas_call(pair_kernel, out_shape=jax.ShapeDtypeStruct(shape, bf16),...  4.21 us
    unnamed x32, local copies, waits for them, and re-layouts  3.26 us
    pallas_call x1, Pallas kernels, bias_call(): pl.pallas_call(bias_kernel, out_shape=jax.ShapeDtypeStruct((HEADS, 32, BL...  3.13 us
  transfers between devices with their start and end apart: 28, of which 19 were waited for; matrix products, arithmetic and copies ran while one was open for 0% of the time, Pallas kernels for 4%

profile of v7, /device:TPU:32, one launch (start us, length us, event | category | flops | bytes accessed | tf_op | source)
XLA Modules:
  0.0 99.5 jit_solution(16475917844195425472)
XLA Ops:
  3.9 3.1 %pair_bias.1.g0 = bf16[4,32,128]{2,1,0:T(8,128)(2,1)S(1)} custom-call(bf16[128,32,128]{2,1,0:T(8,128)(2,1)S(1)} %copy-done, f32[1,128]{1,0:T(1,128)S(1)} %bitcast.22, f32[1,128]{1,0:T(1,128)S(1)} %bitcast.28, bf16[4,128]{1,0:T(4,128)(2,1)S(1)} %bitcast.26), custom_call_target="tpu_custom_call" | custom-call | flops 3500000000 | bytes 1200000 | tf_op jit(solution)/shard_map/pair_bias/pallas_call | solution.py:56
  8.1 1.7 %collective-permute-start.3 = (bf16[20,32,128]{2,1,0:T(8,128)(2,1)S(1)}, bf16[20,32,128]{2,1,0:T(8,128)(2,1)S(1)}, u32[]{:S(2)}, u32[]{:S(2)}) collective-permute-start(bf16[20,32,128]{2,1,0:T(8,128)(2,1)S(1)} %get-tuple-element.73), channel_id=1, source_target_pairs={{0,1},{1,2},{2,3},{3,0},{4,5},{5,6},{6,7},{7,4},{8,9},{9,10},{10,1... | collective-permute-start | bytes 491528 | tf_op jit(solution)/shard_map/ppermute | solution.py:426
  9.7 2.9 %collective-permute-start.4 = (bf16[20,32,128]{2,1,0:T(8,128)(2,1)S(1)}, bf16[20,32,128]{2,1,0:T(8,128)(2,1)S(1)}, u32[]{:S(2)}, u32[]{:S(2)}) collective-permute-start(bf16[20,32,128]{2,1,0:T(8,128)(2,1)S(1)} %get-tuple-element.74), channel_id=1, source_target_pairs={{0,2},{1,3},{2,0},{3,1},{4,6},{5,7},{6,4},{7,5},{8,10},{9,11},{10,... | collective-permute-start | bytes 491528 | tf_op jit(solution)/shard_map/ppermute | solution.py:426
  14.0 5.4 %collective-permute-start.2 = (bf16[4,32,128]{2,1,0:T(8,128)(2,1)S(1)}, bf16[4,32,128]{2,1,0:T(8,128)(2,1)S(1)}, u32[]{:S(2)}, u32[]{:S(2)}) collective-permute-start(bf16[4,32,128]{2,1,0:T(8,128)(2,1)S(1)} %pair_bias.1.g0), channel_id=1, source_target_pairs={{0,48},{16,0},{32,16},{48,32},{1,49},{17,1},{33,17},{49,33},{2,50}... | collective-permute-start | bytes 98312 | tf_op jit(solution)/shard_map/ppermute | solution.py:426
  21.0 2.6 %collective-permute-start = (bf16[4,32,128]{2,1,0:T(8,128)(2,1)S(1)}, bf16[4,32,128]{2,1,0:T(8,128)(2,1)S(1)}, u32[]{:S(2)}, u32[]{:S(2)}) collective-permute-start(bf16[4,32,128]{2,1,0:T(8,128)(2,1)S(1)} %pair_bias.1.g0), channel_id=1, source_target_pairs={{0,16},{16,32},{32,48},{48,0},{1,17},{17,33},{33,49},{49,1},{2,18}... | collective-permute-start | bytes 98312 | tf_op jit(solution)/shard_map/ppermute | solution.py:426
  23.6 3.6 %collective-permute-done.1.g2 = bf16[4,32,128]{2,1,0:T(8,128)(2,1)S(1)} collective-permute-done((bf16[4,32,128]{2,1,0:T(8,128)(2,1)S(1)}, bf16[4,32,128]{2,1,0:T(8,128)(2,1)S(1)}, u32[]{:S(2)}, u32[]{:S(2)}) %collective-permute-start.1) | collective-permute-done | bytes 32800 | tf_op jit(solution)/shard_map/ppermute | solution.py:426
  30.6 1.5 %collective-permute-start.8 = (bf16[4,32,128]{2,1,0:T(8,128)(2,1)S(1)}, bf16[4,32,128]{2,1,0:T(8,128)(2,1)S(1)}, u32[]{:S(2)}, u32[]{:S(2)}) collective-permute-start(bf16[4,32,128]{2,1,0:T(8,128)(2,1)S(1)} %get-tuple-element.79), channel_id=1, source_target_pairs={{0,3},{1,0},{2,1},{3,2},{4,7},{5,4},{6,5},{7,6},{8,11},{9,8},{10,9... | collective-permute-start | bytes 98312 | tf_op jit(solution)/shard_map/ppermute | solution.py:426
  32.1 1.8 %collective-permute-done.6 = bf16[4,32,128]{2,1,0:T(8,128)(2,1)S(1)} collective-permute-done((bf16[4,32,128]{2,1,0:T(8,128)(2,1)S(1)}, bf16[4,32,128]{2,1,0:T(8,128)(2,1)S(1)}, u32[]{:S(2)}, u32[]{:S(2)}) %collective-permute-start.6) | collective-permute-done | bytes 32800 | tf_op jit(solution)/shard_map/ppermute | solution.py:426
  35.1 2.8 %collective-permute-start.11 = (bf16[4,4,32,128]{3,2,1,0:T(8,128)(2,1)S(1)}, bf16[4,4,32,128]{3,2,1,0:T(8,128)(2,1)S(1)}, u32[]{:S(2)}, u32[]{:S(2)}) collective-permute-start(bf16[4,4,32,128]{3,2,1,0:T(8,128)(2,1)S(1)} %pad_maximum_fusion.2), channel_id=1, source_target_pairs={{0,192},{64,0},{128,64},{192,128},{1,193},{65,1},{129,65},{193,129... | collective-permute-start | bytes 393224 | tf_op jit(solution)/shard_map/ppermute | solution.py:426
  39.7 2.2 %collective-permute-done.11 = bf16[4,4,32,128]{3,2,1,0:T(8,128)(2,1)S(1)} collective-permute-done((bf16[4,4,32,128]{3,2,1,0:T(8,128)(2,1)S(1)}, bf16[4,4,32,128]{3,2,1,0:T(8,128)(2,1)S(1)}, u32[]{:S(2)}, u32[]{:S(2)}) %collective-permute-start.11) | collective-permute-done | bytes 131104 | tf_op jit(solution)/shard_map/ppermute | solution.py:426
  41.9 2.6 %collective-permute-done.10 = bf16[4,4,32,128]{3,2,1,0:T(8,128)(2,1)S(1)} collective-permute-done((bf16[4,4,32,128]{3,2,1,0:T(8,128)(2,1)S(1)}, bf16[4,4,32,128]{3,2,1,0:T(8,128)(2,1)S(1)}, u32[]{:S(2)}, u32[]{:S(2)}) %collective-permute-start.10) | collective-permute-done | bytes 131104 | tf_op jit(solution)/shard_map/ppermute | solution.py:426
  46.2 1.9 %collective-permute-done.13.bias_other = bf16[4,4,4,32,128]{4,3,2,1,0:T(8,128)(2,1)S(1)} collective-permute-done((bf16[4,4,4,32,128]{4,3,2,1,0:T(8,128)(2,1)S(1)}, bf16[4,4,4,32,128]{4,3,2,1,0:T(8,128)(2,1)S(1)}, u32[]{:S(2)}, u32[]{:S(2)}) %collective-permute-start.13) | collective-permute-done | bytes 524320 | tf_op jit(solution)/shard_map/ppermute | solution.py:426
  48.1 10.2 %attention.1 = (bf16[4,10,32,128]{3,2,1,0:T(8,128)(2,1)S(1)}, bf16[4,10,32,128]{3,2,1,0:T(8,128)(2,1)S(1)}, bf16[4,10,32,128]{3,2,1,0:T(8,128)(2,1)S(1)}, f32[4,...) custom-call(s32[8,128]{1,0:T(8,128)S(1)} %bitcast.31, ...), custom_call_target="tpu_custom_call" | custom-call | flops 8000000000 | bytes 6000000 | tf_op jit(solution)/shard_map/attention/pallas_call | solution.py:217
  62.8 5.8 %collective-permute-done.18.came = bf16[4,10,32,128]{3,2,1,0:T(8,128)(2,1)S(1)} collective-permute-done((bf16[4,10,32,128]{3,2,1,0:T(8,128)(2,1)S(1)}, bf16[4,10,32,128]{3,2,1,0:T(8,128)(2,1)S(1)}, u32[]{:S(2)}, u32[]{:S(2)}) %collective-permute-start.18) | collective-permute-done | bytes 327712 | tf_op jit(solution)/shard_map/ppermute | solution.py:426
  68.9 1.7 %collective-permute-done.17.c3 = bf16[4,4,32,128]{3,2,1,0:T(8,128)(2,1)S(1)} collective-permute-done((bf16[4,4,32,128]{3,2,1,0:T(8,128)(2,1)S(1)}, bf16[4,4,32,128]{3,2,1,0:T(8,128)(2,1)S(1)}, u32[]{:S(2)}, u32[]{:S(2)}) %collective-permute-start.17) | collective-permute-done | bytes 131104 | tf_op jit(solution)/shard_map/ppermute | solution.py:426
  70.7 2.5 %collective-permute-start.22 = (bf16[20,32,128]{2,1,0:T(8,128)(2,1)S(1)}, bf16[20,32,128]{2,1,0:T(8,128)(2,1)S(1)}, u32[]{:S(2)}, u32[]{:S(2)}) collective-permute-start(bf16[20,32,128]{2,1,0:T(8,128)(2,1)S(1)} %get-tuple-element.109), channel_id=1, source_target_pairs={{0,3},{1,0},{2,1},{3,2},{4,7},{5,4},{6,5},{7,6},{8,11},{9,8},{10,9... | collective-permute-start | bytes 491528 | tf_op jit(solution)/shard_map/ppermute | solution.py:426
  74.5 2.8 %collective-permute-start.19 = (bf16[4,32,128]{2,1,0:T(8,128)(2,1)S(1)}, bf16[4,32,128]{2,1,0:T(8,128)(2,1)S(1)}, u32[]{:S(2)}, u32[]{:S(2)}) collective-permute-start(bf16[4,32,128]{2,1,0:T(8,128)(2,1)S(1)} %get-tuple-element.105), channel_id=1, source_target_pairs={{0,48},{16,0},{32,16},{48,32},{1,49},{17,1},{33,17},{49,33},{2,50}... | collective-permute-start | bytes 98312 | tf_op jit(solution)/shard_map/ppermute | solution.py:426
  79.7 1.8 %collective-permute-start.21 = (bf16[4,32,128]{2,1,0:T(8,128)(2,1)S(1)}, bf16[4,32,128]{2,1,0:T(8,128)(2,1)S(1)}, u32[]{:S(2)}, u32[]{:S(2)}) collective-permute-start(bf16[4,32,128]{2,1,0:T(8,128)(2,1)S(1)} %get-tuple-element.107), channel_id=1, source_target_pairs={{0,16},{16,32},{32,48},{48,0},{1,17},{17,33},{33,49},{49,1},{2,18}... | collective-permute-start | bytes 98312 | tf_op jit(solution)/shard_map/ppermute | solution.py:426
  81.5 1.8 %pair_stats.1 = (f32[4096,128]{1,0:T(8,128)S(1)}, f32[4096,128]{1,0:T(8,128)S(1)}) custom-call(bf16[128,32,128]{2,1,0:T(8,128)(2,1)S(1)} %copy-done.1), custom_call_target="tpu_custom_call" | custom-call | flops 10000000 | bytes 5000000 | tf_op jit(solution)/shard_map/pair_stats/pallas_call | solution.py:367
  83.3 1.9 %collective-permute-done.20.c2 = bf16[4,32,128]{2,1,0:T(8,128)(2,1)S(1)} collective-permute-done((bf16[4,32,128]{2,1,0:T(8,128)(2,1)S(1)}, bf16[4,32,128]{2,1,0:T(8,128)(2,1)S(1)}, u32[]{:S(2)}, u32[]{:S(2)}) %collective-permute-start.20) | collective-permute-done | bytes 32800 | tf_op jit(solution)/shard_map/ppermute | solution.py:426
  86.3 3.0 %collective-permute-start.25 = (bf16[32,128]{1,0:T(8,128)(2,1)S(1)}, bf16[32,128]{1,0:T(8,128)(2,1)S(1)}, u32[]{:S(2)}, u32[]{:S(2)}) collective-permute-start(bf16[32,128]{1,0:T(8,128)(2,1)S(1)} %get-tuple-element.123), channel_id=1, source_target_pairs={{0,3},{1,0},{2,1},{3,2},{4,7},{5,4},{6,5},{7,6},{8,11},{9,8},{10,9... | collective-permute-start | bytes 24584 | tf_op jit(solution)/shard_map/ppermute | solution.py:426
  90.4 1.7 %group_backward.1 = bf16[5,128,128]{2,1,0:T(8,128)(2,1)} custom-call(bf16[5,128,128]{2,1,0:T(8,128)(2,1)S(1)} %copy-done.2, f32[1,128]{1,0:T(1,128)S(1)} %bitcast.24, bf16[128,128]{1,0:T(8,128)(2,1)S(1)} %copy-done.4, bf16[128,128]{1,0:T(8,128)(2,1)S(1)} %copy-done.5, bf16[128,128]{1,0:T(8,128)(2,1)S(1)} %copy-done.6, bf16[128,128]{1,0:T(8,128)(2,1)S(1)} %copy-done.7, ...), custom_call_target="tpu_custom_call" | custom-call | flops 160000000 | bytes 2000000 | tf_op jit(solution)/shard_map/group_backward/pallas_call | solution.py:342
  92.1 2.3 %collective-permute-done.26.t2 = bf16[32,128]{1,0:T(8,128)(2,1)S(1)} collective-permute-done((bf16[32,128]{1,0:T(8,128)(2,1)S(1)}, bf16[32,128]{1,0:T(8,128)(2,1)S(1)}, u32[]{:S(2)}, u32[]{:S(2)}) %collective-permute-start.26) | collective-permute-done | bytes 8224 | tf_op jit(solution)/shard_map/ppermute | solution.py:426
  95.2 4.2 %pair_backward.1 = bf16[128,32,128]{2,1,0:T(8,128)(2,1)} custom-call(f32[4096,128]{1,0:T(8,128)S(1)} %get-tuple-element.116.xhat, f32[4096,128]{1,0:T(8,128)S(1)} %get-tuple-element.117.recip, f32[1,128]{1,0:T(1,128)S(1)} %bitcast.25, bf16[4,128]{1,0:T(4,128)(2,1)S(1)} %bitcast.27, bf16[32,128]{1,0:T(8,128)(2,1)S(1)} %get-tuple-element.122.t0, ...), custom_call_target="tpu_custom_call" | custom-call | flops 60000000 | bytes 5200000 | tf_op jit(solution)/shard_map/pair_backward/pallas_call | solution.py:412
  (80 shorter events, 26.6 us)
Async XLA Ops:
  8.1 19.2 %collective-permute-start.3 = (bf16[20,32,128]{2,1,0:T(8,128)(2,1)S(1)}, bf16[20,32,128]{2,1,0:T(8,128)(2,1)S(1)}, u32[]{:S(2)}, u32[]{:S(2)}) collective-permute-start(bf16[20,32,128]{2,1,0:T(8,128)(2,1)S(1)} %get-tuple-element.73), channel_id=1, source_target_pairs={{0,1},{1,2},{2,3},{3,0},{4,5},{5,6},{6,7},{7,4},{8,9},{9,10},{10,1... | collective-permute-start | bytes 491528 | tf_op jit(solution)/shard_map/ppermute | solution.py:426
  9.7 17.6 %collective-permute-start.4 = (bf16[20,32,128]{2,1,0:T(8,128)(2,1)S(1)}, bf16[20,32,128]{2,1,0:T(8,128)(2,1)S(1)}, u32[]{:S(2)}, u32[]{:S(2)}) collective-permute-start(bf16[20,32,128]{2,1,0:T(8,128)(2,1)S(1)} %get-tuple-element.74), channel_id=1, source_target_pairs={{0,2},{1,3},{2,0},{3,1},{4,6},{5,7},{6,4},{7,5},{8,10},{9,11},{10,... | collective-permute-start | bytes 491528 | tf_op jit(solution)/shard_map/ppermute | solution.py:426
  12.6 14.7 %collective-permute-start.5 = (bf16[20,32,128]{2,1,0:T(8,128)(2,1)S(1)}, bf16[20,32,128]{2,1,0:T(8,128)(2,1)S(1)}, u32[]{:S(2)}, u32[]{:S(2)}) collective-permute-start(bf16[20,32,128]{2,1,0:T(8,128)(2,1)S(1)} %get-tuple-element.75), channel_id=1, source_target_pairs={{0,3},{1,0},{2,1},{3,2},{4,7},{5,4},{6,5},{7,6},{8,11},{9,8},{10,9... | collective-permute-start | bytes 491528 | tf_op jit(solution)/shard_map/ppermute | solution.py:426
  14.0 7.0 %collective-permute-start.2 = (bf16[4,32,128]{2,1,0:T(8,128)(2,1)S(1)}, bf16[4,32,128]{2,1,0:T(8,128)(2,1)S(1)}, u32[]{:S(2)}, u32[]{:S(2)}) collective-permute-start(bf16[4,32,128]{2,1,0:T(8,128)(2,1)S(1)} %pair_bias.1.g0), channel_id=1, source_target_pairs={{0,48},{16,0},{32,16},{48,32},{1,49},{17,1},{33,17},{49,33},{2,50}... | collective-permute-start | bytes 98312 | tf_op jit(solution)/shard_map/ppermute | solution.py:426
  19.4 7.8 %collective-permute-start.1 = (bf16[4,32,128]{2,1,0:T(8,128)(2,1)S(1)}, bf16[4,32,128]{2,1,0:T(8,128)(2,1)S(1)}, u32[]{:S(2)}, u32[]{:S(2)}) collective-permute-start(bf16[4,32,128]{2,1,0:T(8,128)(2,1)S(1)} %pair_bias.1.g0), channel_id=1, source_target_pairs={{0,32},{16,48},{32,0},{48,16},{1,33},{17,49},{33,1},{49,17},{2,34}... | collective-permute-start | bytes 98312 | tf_op jit(solution)/shard_map/ppermute | solution.py:426
  21.0 6.3 %collective-permute-start = (bf16[4,32,128]{2,1,0:T(8,128)(2,1)S(1)}, bf16[4,32,128]{2,1,0:T(8,128)(2,1)S(1)}, u32[]{:S(2)}, u32[]{:S(2)}) collective-permute-start(bf16[4,32,128]{2,1,0:T(8,128)(2,1)S(1)} %pair_bias.1.g0), channel_id=1, source_target_pairs={{0,16},{16,32},{32,48},{48,0},{1,17},{17,33},{33,49},{49,1},{2,18}... | collective-permute-start | bytes 98312 | tf_op jit(solution)/shard_map/ppermute | solution.py:426
  27.4 18.4 %collective-permute-start.12 = (bf16[4,10,32,128]{3,2,1,0:T(8,128)(2,1)S(1)}, bf16[4,10,32,128]{3,2,1,0:T(8,128)(2,1)S(1)}, u32[]{:S(2)}, u32[]{:S(2)}) collective-permute-start(bf16[4,10,32,128]{3,2,1,0:T(8,128)(2,1)S(1)} %pad_maximum_fusion.1), channel_id=1, source_target_pairs={{0,4},{4,0},{1,5},{5,1},{2,6},{6,2},{3,7},{7,3},{8,12},{12,8},{9,1... | collective-permute-start | bytes 983048 | tf_op jit(solution)/shard_map/ppermute | solution.py:426
  28.8 5.1 %collective-permute-start.6 = (bf16[4,32,128]{2,1,0:T(8,128)(2,1)S(1)}, bf16[4,32,128]{2,1,0:T(8,128)(2,1)S(1)}, u32[]{:S(2)}, u32[]{:S(2)}) collective-permute-start(bf16[4,32,128]{2,1,0:T(8,128)(2,1)S(1)} %get-tuple-element.77), channel_id=1, source_target_pairs={{0,1},{1,2},{2,3},{3,0},{4,5},{5,6},{6,7},{7,4},{8,9},{9,10},{10,1... | collective-permute-start | bytes 98312 | tf_op jit(solution)/shard_map/ppermute | solution.py:426
  29.4 5.4 %collective-permute-start.7 = (bf16[4,32,128]{2,1,0:T(8,128)(2,1)S(1)}, bf16[4,32,128]{2,1,0:T(8,128)(2,1)S(1)}, u32[]{:S(2)}, u32[]{:S(2)}) collective-permute-start(bf16[4,32,128]{2,1,0:T(8,128)(2,1)S(1)} %get-tuple-element.78), channel_id=1, source_target_pairs={{0,2},{1,3},{2,0},{3,1},{4,6},{5,7},{6,4},{7,5},{8,10},{9,11},{10,... | collective-permute-start | bytes 98312 | tf_op jit(solution)/shard_map/ppermute | solution.py:426
  35.1 6.8 %collective-permute-start.11 = (bf16[4,4,32,128]{3,2,1,0:T(8,128)(2,1)S(1)}, bf16[4,4,32,128]{3,2,1,0:T(8,128)(2,1)S(1)}, u32[]{:S(2)}, u32[]{:S(2)}) collective-permute-start(bf16[4,4,32,128]{3,2,1,0:T(8,128)(2,1)S(1)} %pad_maximum_fusion.2), channel_id=1, source_target_pairs={{0,192},{64,0},{128,64},{192,128},{1,193},{65,1},{129,65},{193,129... | collective-permute-start | bytes 393224 | tf_op jit(solution)/shard_map/ppermute | solution.py:426
  38.0 6.6 %collective-permute-start.10 = (bf16[4,4,32,128]{3,2,1,0:T(8,128)(2,1)S(1)}, bf16[4,4,32,128]{3,2,1,0:T(8,128)(2,1)S(1)}, u32[]{:S(2)}, u32[]{:S(2)}) collective-permute-start(bf16[4,4,32,128]{3,2,1,0:T(8,128)(2,1)S(1)} %pad_maximum_fusion.2), channel_id=1, source_target_pairs={{0,128},{64,192},{128,0},{192,64},{1,129},{65,193},{129,1},{193,65... | collective-permute-start | bytes 393224 | tf_op jit(solution)/shard_map/ppermute | solution.py:426
  38.8 7.1 %collective-permute-start.9 = (bf16[4,4,32,128]{3,2,1,0:T(8,128)(2,1)S(1)}, bf16[4,4,32,128]{3,2,1,0:T(8,128)(2,1)S(1)}, u32[]{:S(2)}, u32[]{:S(2)}) collective-permute-start(bf16[4,4,32,128]{3,2,1,0:T(8,128)(2,1)S(1)} %pad_maximum_fusion.2), channel_id=1, source_target_pairs={{0,64},{64,128},{128,192},{192,0},{1,65},{65,129},{129,193},{193,1... | collective-permute-start | bytes 393224 | tf_op jit(solution)/shard_map/ppermute | solution.py:426
  58.5 10.0 %collective-permute-start.18 = (bf16[4,10,32,128]{3,2,1,0:T(8,128)(2,1)S(1)}, bf16[4,10,32,128]{3,2,1,0:T(8,128)(2,1)S(1)}, u32[]{:S(2)}, u32[]{:S(2)}) collective-permute-start(bf16[4,10,32,128]{3,2,1,0:T(8,128)(2,1)S(1)} %get-tuple-element.96), channel_id=1, source_target_pairs={{0,4},{4,0},{1,5},{5,1},{2,6},{6,2},{3,7},{7,3},{8,12},{12,8},{9,1... | collective-permute-start | bytes 983048 | tf_op jit(solution)/shard_map/ppermute | solution.py:426
  60.5 8.2 %collective-permute-start.15 = (bf16[4,4,32,128]{3,2,1,0:T(8,128)(2,1)S(1)}, bf16[4,4,32,128]{3,2,1,0:T(8,128)(2,1)S(1)}, u32[]{:S(2)}, u32[]{:S(2)}) collective-permute-start(bf16[4,4,32,128]{3,2,1,0:T(8,128)(2,1)S(1)} %get-tuple-element.92), channel_id=1, source_target_pairs={{0,192},{64,0},{128,64},{192,128},{1,193},{65,1},{129,65},{193,129... | collective-permute-start | bytes 393224 | tf_op jit(solution)/shard_map/ppermute | solution.py:426
  61.1 7.8 %collective-permute-start.16 = (bf16[4,4,32,128]{3,2,1,0:T(8,128)(2,1)S(1)}, bf16[4,4,32,128]{3,2,1,0:T(8,128)(2,1)S(1)}, u32[]{:S(2)}, u32[]{:S(2)}) collective-permute-start(bf16[4,4,32,128]{3,2,1,0:T(8,128)(2,1)S(1)} %get-tuple-element.93), channel_id=1, source_target_pairs={{0,128},{64,192},{128,0},{192,64},{1,129},{65,193},{129,1},{193,65... | collective-permute-start | bytes 393224 | tf_op jit(solution)/shard_map/ppermute | solution.py:426
  61.9 8.8 %collective-permute-start.17 = (bf16[4,4,32,128]{3,2,1,0:T(8,128)(2,1)S(1)}, bf16[4,4,32,128]{3,2,1,0:T(8,128)(2,1)S(1)}, u32[]{:S(2)}, u32[]{:S(2)}) collective-permute-start(bf16[4,4,32,128]{3,2,1,0:T(8,128)(2,1)S(1)} %get-tuple-element.94), channel_id=1, source_target_pairs={{0,64},{64,128},{128,192},{192,0},{1,65},{65,129},{129,193},{193,1... | collective-permute-start | bytes 393224 | tf_op jit(solution)/shard_map/ppermute | solution.py:426
  70.7 15.6 %collective-permute-start.22 = (bf16[20,32,128]{2,1,0:T(8,128)(2,1)S(1)}, bf16[20,32,128]{2,1,0:T(8,128)(2,1)S(1)}, u32[]{:S(2)}, u32[]{:S(2)}) collective-permute-start(bf16[20,32,128]{2,1,0:T(8,128)(2,1)S(1)} %get-tuple-element.109), channel_id=1, source_target_pairs={{0,3},{1,0},{2,1},{3,2},{4,7},{5,4},{6,5},{7,6},{8,11},{9,8},{10,9... | collective-permute-start | bytes 491528 | tf_op jit(solution)/shard_map/ppermute | solution.py:426
  73.2 13.1 %collective-permute-start.23 = (bf16[20,32,128]{2,1,0:T(8,128)(2,1)S(1)}, bf16[20,32,128]{2,1,0:T(8,128)(2,1)S(1)}, u32[]{:S(2)}, u32[]{:S(2)}) collective-permute-start(bf16[20,32,128]{2,1,0:T(8,128)(2,1)S(1)} %get-tuple-element.110), channel_id=1, source_target_pairs={{0,2},{1,3},{2,0},{3,1},{4,6},{5,7},{6,4},{7,5},{8,10},{9,11},{10,... | collective-permute-start | bytes 491528 | tf_op jit(solution)/shard_map/ppermute | solution.py:426
  74.4 11.9 %collective-permute-start.24 = (bf16[20,32,128]{2,1,0:T(8,128)(2,1)S(1)}, bf16[20,32,128]{2,1,0:T(8,128)(2,1)S(1)}, u32[]{:S(2)}, u32[]{:S(2)}) collective-permute-start(bf16[20,32,128]{2,1,0:T(8,128)(2,1)S(1)} %get-tuple-element.111), channel_id=1, source_target_pairs={{0,1},{1,2},{2,3},{3,0},{4,5},{5,6},{6,7},{7,4},{8,9},{9,10},{10,1... | collective-permute-start | bytes 491528 | tf_op jit(solution)/shard_map/ppermute | solution.py:426
  74.5 5.2 %collective-permute-start.19 = (bf16[4,32,128]{2,1,0:T(8,128)(2,1)S(1)}, bf16[4,32,128]{2,1,0:T(8,128)(2,1)S(1)}, u32[]{:S(2)}, u32[]{:S(2)}) collective-permute-start(bf16[4,32,128]{2,1,0:T(8,128)(2,1)S(1)} %get-tuple-element.105), channel_id=1, source_target_pairs={{0,48},{16,0},{32,16},{48,32},{1,49},{17,1},{33,17},{49,33},{2,50}... | collective-permute-start | bytes 98312 | tf_op jit(solution)/shard_map/ppermute | solution.py:426
  77.2 8.0 %collective-permute-start.20 = (bf16[4,32,128]{2,1,0:T(8,128)(2,1)S(1)}, bf16[4,32,128]{2,1,0:T(8,128)(2,1)S(1)}, u32[]{:S(2)}, u32[]{:S(2)}) collective-permute-start(bf16[4,32,128]{2,1,0:T(8,128)(2,1)S(1)} %get-tuple-element.106), channel_id=1, source_target_pairs={{0,32},{16,48},{32,0},{48,16},{1,33},{17,49},{33,1},{49,17},{2,34}... | collective-permute-start | bytes 98312 | tf_op jit(solution)/shard_map/ppermute | solution.py:426
  79.7 6.6 %collective-permute-start.21 = (bf16[4,32,128]{2,1,0:T(8,128)(2,1)S(1)}, bf16[4,32,128]{2,1,0:T(8,128)(2,1)S(1)}, u32[]{:S(2)}, u32[]{:S(2)}) collective-permute-start(bf16[4,32,128]{2,1,0:T(8,128)(2,1)S(1)} %get-tuple-element.107), channel_id=1, source_target_pairs={{0,16},{16,32},{32,48},{48,0},{1,17},{17,33},{33,49},{49,1},{2,18}... | collective-permute-start | bytes 98312 | tf_op jit(solution)/shard_map/ppermute | solution.py:426
  86.3 5.8 %collective-permute-start.25 = (bf16[32,128]{1,0:T(8,128)(2,1)S(1)}, bf16[32,128]{1,0:T(8,128)(2,1)S(1)}, u32[]{:S(2)}, u32[]{:S(2)}) collective-permute-start(bf16[32,128]{1,0:T(8,128)(2,1)S(1)} %get-tuple-element.123), channel_id=1, source_target_pairs={{0,3},{1,0},{2,1},{3,2},{4,7},{5,4},{6,5},{7,6},{8,11},{9,8},{10,9... | collective-permute-start | bytes 24584 | tf_op jit(solution)/shard_map/ppermute | solution.py:426
  89.3 5.2 %collective-permute-start.26 = (bf16[32,128]{1,0:T(8,128)(2,1)S(1)}, bf16[32,128]{1,0:T(8,128)(2,1)S(1)}, u32[]{:S(2)}, u32[]{:S(2)}) collective-permute-start(bf16[32,128]{1,0:T(8,128)(2,1)S(1)} %get-tuple-element.124), channel_id=1, source_target_pairs={{0,2},{1,3},{2,0},{3,1},{4,6},{5,7},{6,4},{7,5},{8,10},{9,11},{10,... | collective-permute-start | bytes 24584 | tf_op jit(solution)/shard_map/ppermute | solution.py:426
  (20 other events, 163.5 us)
